TPU v7x, 512 devices: a whole 4x4x16 slice. The times are simulated.
512 devices in a mesh: grp: 2 (over y_lo), space: 64 (over z, x), mem: 4 (over y_hi, core).
Axes of the slice: x: 4, y: 4 (y_hi: 2, y_lo: 2; y = y_hi * 2 + y_lo), z: 16, core: 2. Of those that a mesh axis runs over, the one named last changes fastest.
Arguments:
- start_field: float32 [4, 1024, 32, 256], P('mem', 'space', 'grp'), may hold values from -6 to 6
- material: int32 [1024, 32, 256], P('space', 'grp'), may hold values from 0 to 7
- conductivity: float32 [4, 8], P('mem'), may hold values from 0.02 to 0.16
- owners: int32 [4, 2, 64, 128, 1], P('mem', 'grp'), may hold values from 0 to 63; in each aligned block of 128 rows (0 to 127, 128 to 255, ..., all dimensions but the last counted through in order) at most 4 rows name the same one
- tile_ids: int32 [4, 2, 64, 128], P('mem', 'grp'), may hold values from 0 to 15
- embed_weight: bfloat16 [512, 1536], P(None, ('grp', 'mem')), may hold values from -0.25 to 0.25
- layer_norm_gain: float32 [1536], replicated, may hold values from 0.5 to 1.5
- w_qkv: bfloat16 [3, 1536, 1024], P(None, None, ('grp', 'mem')), may hold values from -1.5 to 1.5
- w_out: bfloat16 [1024, 1536], P(('grp', 'mem')), may hold values from -0.1875 to 0.1875
- w_read: bfloat16 [1536, 128], replicated, may hold values from -0.15625 to 0.15625
Outputs:
- final_field: float32 [4, 1024, 32, 256], P('mem', 'space', 'grp')
- grad_qkv: bfloat16 [3, 1536, 1024], P(None, None, ('grp', 'mem'))
- grad_gain: float32 [1536], replicated
Inputs may be any that keep to these rules, and one draw needn't show every extreme that they name: `owners`: in each aligned block of 128 rows (the slots of one member, half and shard) no owner is named more than 4 times, and in some blocks one owner exactly 4 times.
All inputs are finite; a program needn't handle non-finite values.
Results may differ from a plain program's by a relative error of at most 0.015.
Values may be sent and summed in bfloat16 or wider, within the bound.
No kernel may reach another device: no remote copies, remote signals or barrier semaphores. Data moves between devices by JAX's collectives and lax.ppermute only.
A program may use at most 64 MiB of HBM per device.

v0:
```python
import math

import jax
import jax.numpy as jnp
from jax import lax
from jax.sharding import PartitionSpec as P

SPD = 128
STEPS = 3
TILE = 16
HD = 128


NORM_EPSILON = 1e-06


def with_halo(block, sides, width):
    for axis, dim in sides:
        count = lax.axis_size(axis)
        forward = [(i, i + 1) for i in range(count - 1)]
        backward = [(target, source) for source, target in forward]
        low = lax.ppermute(
            lax.slice_in_dim(block, block.shape[dim] - width, None, axis=dim), axis, forward
        )
        high = lax.ppermute(lax.slice_in_dim(block, 0, width, axis=dim), axis, backward)
        block = jnp.concatenate([low, block, high], axis=dim)
    return block


def relax_step(padded_field, padded_cond):
    field_ext = jnp.pad(padded_field, ((0, 0), (0, 0), (1, 1)))
    cond_ext = jnp.pad(padded_cond, ((0, 0), (0, 0), (1, 1)))
    center = field_ext[1:-1, 1:-1, 1:-1]
    center_cond = cond_ext[1:-1, 1:-1, 1:-1]
    change = jnp.zeros_like(center)
    for axis_id in range(3):
        for offset in (0, 2):
            window = [
                slice(1, 1 + center.shape[0]),
                slice(1, 1 + center.shape[1]),
                slice(1, 1 + center.shape[2]),
            ]
            window[axis_id] = slice(offset, offset + center.shape[axis_id])
            window = tuple(window)
            change = change + 0.5 * (center_cond + cond_ext[window]) * (field_ext[window] - center)
    return center + change


def material_cond(material, table_row):
    conductance = jnp.zeros(material.shape, jnp.float32)
    for level_id in range(table_row.shape[0]):
        conductance = conductance + jnp.where(
            material == level_id, table_row[level_id], jnp.float32(0.0)
        )
    return conductance


def solve_slab(field, conductance):
    stacked = jnp.stack([field, conductance])
    padded = with_halo(stacked, (("grp", 2), ("space", 1)), 1)
    cond_pad = padded[1]
    current = relax_step(padded[0], cond_pad)
    before_last = current
    for section_id in range(1, STEPS):
        before_last = current
        extended = with_halo(current[None], (("grp", 2), ("space", 1)), 1)
        current = relax_step(extended[0], cond_pad)
    return (before_last, current)


def cut_tiles(field, tile_size):
    span_x, span_y, span_z = field.shape
    shaped = field.reshape(
        span_x // tile_size,
        tile_size,
        span_y // tile_size,
        tile_size,
        span_z // tile_size,
        tile_size,
    )
    return shaped.transpose(0, 2, 4, 1, 3, 5).reshape(-1, tile_size, tile_size, tile_size)


def coarse_tokens(tiles, tile_size):
    count_tiles = tiles.shape[0]
    half_size = tile_size // 2
    shaped = tiles.reshape(count_tiles, half_size, 2, half_size, 2, half_size, 2)
    return jnp.mean(shaped, axis=(2, 4, 6)).reshape(count_tiles, -1)


def coarse_targets(tiles, tile_size):
    count_tiles = tiles.shape[0]
    shaped = tiles.reshape(count_tiles, tile_size // 4, 4, tile_size // 4, 4, tile_size // 2, 2)
    return jnp.mean(shaped, axis=(2, 4, 6)).reshape(count_tiles, -1)


def relay_samples(token_rows, target_rows, owner_list, tile_list):
    slot_count = owner_list.shape[1]
    capacity = 2 * slot_count // lax.axis_size("space")
    my_index = lax.axis_index("space")
    same_owner = owner_list[:, :, None] == owner_list[:, None, :]
    slot_order = jnp.arange(slot_count, dtype=jnp.int32)
    earlier = slot_order[None, :] < slot_order[:, None]
    slot_rank = jnp.sum((same_owner & earlier[None]).astype(jnp.int32), axis=2)
    owned_here = owner_list == my_index
    slot_ids = jnp.arange(capacity, dtype=jnp.int32)
    slot_match = owned_here[:, None, :] & (slot_rank[:, None, :] == slot_ids[None, :, None])
    chosen = jnp.sum(jnp.where(slot_match, tile_list[:, None, :] + 1, 0), axis=2) - 1
    present = (chosen >= 0)[:, :, None]
    picked = jnp.maximum(chosen, 0)
    send_tokens = jnp.where(present, token_rows[picked], jnp.zeros((), jnp.bfloat16))
    send_targets = jnp.where(present, target_rows[picked], jnp.zeros((), jnp.bfloat16))
    got_tokens, got_targets = (
        lax.all_to_all(send_tokens, "space", split_axis=0, concat_axis=0, tiled=True),
        lax.all_to_all(send_targets, "space", split_axis=0, concat_axis=0, tiled=True),
    )
    own_owner = jnp.take(owner_list, my_index, axis=0)
    own_rank = jnp.take(slot_rank, my_index, axis=0)
    flat_index = own_owner * capacity + own_rank
    sample_tokens = got_tokens.reshape(-1, got_tokens.shape[2])[flat_index]
    sample_targets = got_targets.reshape(-1, got_targets.shape[2])[flat_index]
    return (sample_tokens, sample_targets)


def train_shard(sample_tokens, sample_targets, embed_weight, layer_norm_gain, w_qkv, w_out, w_read):
    tokens, targets = (
        lax.all_gather(sample_tokens, ("grp", "mem"), axis=0, tiled=True),
        lax.all_gather(sample_targets, ("grp", "mem"), axis=0, tiled=True),
    )
    row_count = tokens.shape[0]
    width_own = embed_weight.shape[1]
    part_index = lax.axis_index(("grp", "mem"))
    own_cols = jnp.dot(tokens, embed_weight, preferred_element_type=jnp.float32).astype(
        jnp.bfloat16
    )
    embedded = lax.all_gather(own_cols, ("grp", "mem"), axis=1, tiled=True)
    embedded_wide = embedded.astype(jnp.float32)
    row_mean = jnp.mean(embedded_wide, axis=1, keepdims=True)
    mean_removed = embedded_wide - row_mean
    row_variance = jnp.mean(mean_removed * mean_removed, axis=1, keepdims=True)
    standardized_input = mean_removed * lax.rsqrt(row_variance + NORM_EPSILON)
    normalized_rows = (standardized_input * layer_norm_gain).astype(jnp.bfloat16)
    projected = jnp.einsum(
        "rd,tdc->trc", normalized_rows, w_qkv, preferred_element_type=jnp.float32
    ).astype(jnp.bfloat16)
    heads_own = w_qkv.shape[2] // HD
    seq_count = row_count // SPD
    split_heads = projected.reshape(3, seq_count, SPD, heads_own, HD)
    query_rows, key_rows, value_rows = (split_heads[0], split_heads[1], split_heads[2])
    score_scale = 1.0 / math.sqrt(HD)
    scores = (
        jnp.einsum("bqhd,bkhd->bhqk", query_rows, key_rows, preferred_element_type=jnp.float32)
        * score_scale
    )
    top_score = jnp.max(scores, axis=-1, keepdims=True)
    raised = jnp.exp(scores - top_score)
    prob_table = raised / jnp.sum(raised, axis=-1, keepdims=True)
    probs_low = prob_table.astype(jnp.bfloat16)
    attended = jnp.einsum(
        "bhqk,bkhd->bqhd", probs_low, value_rows, preferred_element_type=jnp.float32
    )
    attended = attended.astype(jnp.bfloat16).reshape(row_count, heads_own * HD)
    read_wide = w_read.astype(jnp.float32)
    read_rows = lax.dynamic_slice_in_dim(w_read, part_index * width_own, width_own, 0)
    mixing = jnp.dot(w_out, w_read, preferred_element_type=jnp.float32)
    partial_pred = jnp.dot(attended.astype(jnp.float32), mixing, precision=lax.Precision.HIGHEST)
    partial_pred = partial_pred + jnp.dot(own_cols, read_rows, preferred_element_type=jnp.float32)
    prediction = lax.psum(partial_pred.astype(jnp.bfloat16), ("grp", "mem")).astype(jnp.float32)
    loss_scale = math.sqrt(w_read.shape[0] / (lax.axis_size("space") * row_count * w_read.shape[1]))
    delta = (prediction - targets.astype(jnp.float32)) * loss_scale
    upstream = jnp.dot(delta, read_wide.T, precision=lax.Precision.HIGHEST).astype(jnp.bfloat16)
    grad_attended = jnp.dot(upstream, w_out.T, preferred_element_type=jnp.float32).astype(
        jnp.bfloat16
    )
    grad_attended = grad_attended.reshape(seq_count, SPD, heads_own, HD)
    grad_probs = jnp.einsum(
        "bqhd,bkhd->bhqk", grad_attended, value_rows, preferred_element_type=jnp.float32
    )
    grad_values = jnp.einsum(
        "bhqk,bqhd->bkhd", probs_low, grad_attended, preferred_element_type=jnp.float32
    ).astype(jnp.bfloat16)
    inner_sum = jnp.sum(prob_table * grad_probs, axis=-1, keepdims=True)
    grad_scores = (prob_table * (grad_probs - inner_sum) * score_scale).astype(jnp.bfloat16)
    grad_queries = jnp.einsum(
        "bhqk,bkhd->bqhd", grad_scores, key_rows, preferred_element_type=jnp.float32
    ).astype(jnp.bfloat16)
    grad_keys = jnp.einsum(
        "bhqk,bqhd->bkhd", grad_scores, query_rows, preferred_element_type=jnp.float32
    ).astype(jnp.bfloat16)
    grad_proj = jnp.stack([grad_queries, grad_keys, grad_values]).reshape(
        3, row_count, heads_own * HD
    )
    grad_weights = jnp.einsum(
        "rd,trc->tdc", normalized_rows, grad_proj, preferred_element_type=jnp.float32
    )
    gradient_normalized = jnp.einsum(
        "trc,tdc->rd", grad_proj, w_qkv, preferred_element_type=jnp.float32
    )
    gain_contribution = jnp.sum(gradient_normalized * standardized_input, axis=0)
    weight_sum, gain_vector = lax.psum((grad_weights, gain_contribution), "space")
    weight_total = weight_sum.astype(jnp.bfloat16)
    gain_total = lax.psum(gain_vector, ("grp", "mem"))
    return (weight_total, gain_total)


def shards(
    start_field,
    material,
    conductivity,
    owners,
    tile_ids,
    embed_weight,
    layer_norm_gain,
    w_qkv,
    w_out,
    w_read,
):
    conductance = material_cond(material, conductivity[0])
    before_last, final_local = solve_slab(start_field[0], conductance)
    token_rows = coarse_tokens(cut_tiles(before_last, TILE), TILE).astype(jnp.bfloat16)
    target_rows = coarse_targets(cut_tiles(final_local, TILE), TILE).astype(jnp.bfloat16)
    sample_tokens, sample_targets = relay_samples(
        token_rows, target_rows, owners[0, 0, :, :, 0], tile_ids[0, 0]
    )
    grad_weights, grad_gain = train_shard(
        sample_tokens, sample_targets, embed_weight, layer_norm_gain, w_qkv, w_out, w_read
    )
    return (final_local[None], grad_weights, grad_gain)


def solution(mesh):
    placed = (
        P("mem", "space", "grp", None),
        P("space", "grp", None),
        P("mem", None),
        P("mem", "grp", None, None, None),
        P("mem", "grp", None, None),
        P(None, ("grp", "mem")),
        P(),
        P(None, None, ("grp", "mem")),
        P(("grp", "mem"), None),
        P(),
    )
    return jax.shard_map(
        shards,
        mesh=mesh,
        in_specs=placed,
        out_specs=(P("mem", "space", "grp", None), P(None, None, ("grp", "mem")), P()),
        check_vma=False,
    )
```

profile of v0, /device:TPU:1, one launch (start us, length us, event | category | flops | bytes accessed | tf_op | source)
XLA Modules:
  0.0 629.3 jit_solution(1853725206715971725)
XLA Ops:
  7.2 1.6 fusion.103
  8.8 6.2 add_bitcast_fusion
  16.0 4.0 collective-permute-start
  20.1 1.3 collective-permute-start.1
  22.2 3.5 convert_reduce_fusion.1
  27.3 3.1 collective-permute-start.2
  30.5 1.3 collective-permute-start.3
  31.8 3.5 collective-permute-done.3
  36.9 4.0 collective-permute-start.4
  40.9 1.3 collective-permute-start.5
  42.5 3.0 collective-permute-done.5
  45.4 3.1 collective-permute-start.6
  48.6 1.3 collective-permute-start.7
  50.0 3.1 collective-permute-done.7
  53.7 2.0 reshape.189
  55.7 2.9 copy.50
  58.5 3.0 reduce_sum.83
  61.7 1.2 gather_fusion
  63.8 22.4 %all-to-all-start = ((bf16[64,4,512]{2,1,0:T(4,128)(2,1)}), bf16[64,4,512]{2,1,0:T(4,128)(2,1)S(1)}, u32[]{:S(2)}, u32[]{:S(2)}) async-start(bf16[64,4,512]{2,1,0:T(4,128)(2,1)} %broadcast_select_fusion), calls=%async_computation | async-start | bytes 524288 | tf_op jit(solution)/shard_map/all_to_all | solution.py:114
  87.0 16.7 %all-to-all-done = bf16[64,4,512]{2,1,0:T(4,128)(2,1)S(1)} async-done(((bf16[64,4,512]{2,1,0:T(4,128)(2,1)}), bf16[64,4,512]{2,1,0:T(4,128)(2,1)S(1)}, u32[]{:S(2)}, u32[]{:S(2)}) %all-to-all-start) | async-done | bytes 262176 | tf_op jit(solution)/shard_map/all_to_all | solution.py:114
  103.8 1.5 gather_fusion.1
  105.4 37.6 %all-gather.7.cloned.1.call-done = bf16[1024,512]{1,0:T(8,128)(2,1)} async-done(((bf16[128,512]{1,0:T(8,128)(2,1)}), bf16[1024,512]{1,0:T(8,128)(2,1)}) %all-gather.7.cloned.1.call-update) | async-done | bytes 1048592 | tf_op jit(solution)/shard_map/all_gather | solution.py:127
  143.0 2.5 convolution_convert_fusion.2
  145.5 2.1 collective-permute-start.8
  147.6 1.3 collective-permute-start.9
  148.9 3.4 collective-permute-done.9
  152.4 3.1 collective-permute-start.10
  155.5 1.3 collective-permute-start.11
  157.1 3.0 collective-permute-done.11
  160.6 2.0 reshape.195
  162.6 1.9 copy.56
  164.6 1.1 reduce_sum.87
  167.4 17.5 %all-to-all-start.1 = ((bf16[64,4,128]{2,1,0:T(4,128)(2,1)}), bf16[64,4,128]{2,1,0:T(4,128)(2,1)S(1)}, u32[]{:S(2)}, u32[]{:S(2)}) async-start(bf16[64,4,128]{2,1,0:T(4,128)(2,1)} %broadcast_select_fusion.1), calls=%async_computation.1 | async-start | bytes 131072 | tf_op jit(solution)/shard_map/all_to_all | solution.py:115
  184.9 9.3 %all-gather.5.cloned.1.call-done = bf16[1024,1536]{0,1:T(8,128)(2,1)} async-done(((bf16[1024,192]{0,1:T(8,128)(2,1)}), bf16[1024,1536]{0,1:T(8,128)(2,1)}) %all-gather.5.cloned.1.call-update) | async-done | bytes 3145744 | tf_op jit(solution)/shard_map/all_gather | solution.py:136
  194.2 2.6 convert_reduce_fusion
  197.9 2.0 fusion.10
  200.0 1.1 fusion.104
  202.1 1.1 fusion.19
  203.9 15.2 %all-gather.1 = bf16[1024,128]{1,0:T(8,128)(2,1)S(1)} all-gather(bf16[128,128]{1,0:T(8,128)(2,1)S(1)} %gather_fusion.3), channel_id=3, replica_groups=mesh['grp'=2,'space'=64,'mem'=4] {'grp','mem'}, dimensions={0}, use_global_device_ids=true | all-gather | bytes 294912 | tf_op jit(solution)/shard_map/all_gather | solution.py:128
  219.2 59.5 %all-reduce.8.cloned.1.call-done = bf16[1024,128]{1,0:T(8,128)(2,1)} async-done(((bf16[1024,128]{1,0:T(8,128)(2,1)}), bf16[1024,128]{1,0:T(8,128)(2,1)}) %all-reduce.8.cloned.1.call-update) | async-done | bytes 262160 | tf_op jit(solution)/shard_map/psum | solution.py:168
  278.7 3.8 convolution_convert_fusion
  284.2 1.7 convolution_convert_fusion.5
  285.9 1.6 convolution_convert_fusion.4
  290.1 3.8 convolution_bitcast_fusion
  293.9 2.3 fusion.7
  296.2 256.0 %all-reduce.9 = (bf16[3,1536,128]{1,2,0:T(8,128)(2,1)}, f32[1536]{0:T(1024)}) all-reduce(f32[3,1536,128]{1,2,0:T(8,128)S(1)} %convolution_bitcast_fusion, f32[1536]{0:T(1024)S(1)} %fusion.7), channel_id=1, replica_groups=mesh['grp'=2,'space'=64,'mem'=4] {'space'}, use_global_device_ids=true, to_apply=%region_10.12 | all-reduce | flops 591360 | bytes 3551232 | tf_op jit(solution)/shard_map/psum | solution.py:200
  552.2 2.4 copy.65
  554.5 68.2 %psum.31 = f32[1536]{0:T(1024)} all-reduce(f32[1536]{0:T(1024)} %get-tuple-element.28), channel_id=1, replica_groups=mesh['grp'=2,'space'=64,'mem'=4] {'grp','mem'}, use_global_device_ids=true, to_apply=%region_13.15 | all-reduce | flops 1536 | bytes 12288 | tf_op jit(solution)/shard_map/psum | solution.py:202
  (90 shorter events, 17.7 us)
Async XLA Ops:
  7.2 190.7 %copy-start = (bf16[3,1536,128]{2,1,0:T(8,128)(2,1)S(1)}, bf16[3,1536,128]{2,1,0:T(8,128)(2,1)}, u32[]{:S(2)}) copy-start(bf16[3,1536,128]{2,1,0:T(8,128)(2,1)} %param.19) | copy-start | bytes 3538948
  16.0 10.5 %collective-permute-start = (f32[2,16,1,256]{3,2,1,0:T(1,128)S(1)}, f32[2,16,1,256]{3,2,1,0:T(1,128)S(1)}, u32[]{:S(2)}, u32[]{:S(2)}) collective-permute-start(f32[2,16,1,256]{3,2,1,0:T(1,128)S(1)} %get-tuple-element.36), channel_id=1, source_target_pairs={{0,256},{1,257},{2,258},{3,259},{4,260},{5,261},{6,262},{7,263},{8... | collective-permute-start | bytes 98312 | tf_op jit(solution)/shard_map/ppermute | solution.py:22
  20.1 6.5 %collective-permute-start.1 = (f32[2,16,1,256]{3,2,1,0:T(1,128)S(1)}, f32[2,16,1,256]{3,2,1,0:T(1,128)S(1)}, u32[]{:S(2)}, u32[]{:S(2)}) collective-permute-start(f32[2,16,1,256]{3,2,1,0:T(1,128)S(1)} %get-tuple-element.37), channel_id=1, source_target_pairs={{256,0},{257,1},{258,2},{259,3},{260,4},{261,5},{262,6},{263,7},{2... | collective-permute-start | bytes 98312 | tf_op jit(solution)/shard_map/ppermute | solution.py:25
  27.3 4.4 collective-permute-start.2
  30.5 4.8 collective-permute-start.3
  36.9 5.5 collective-permute-start.4
  40.9 4.5 collective-permute-start.5
  45.4 4.6 collective-permute-start.6
  48.6 4.6 collective-permute-start.7
  61.5 81.4 %copy-start.12 = (bf16[512,192]{0,1:T(8,128)(2,1)S(1)}, bf16[512,192]{0,1:T(8,128)(2,1)}, u32[]{:S(2)}) copy-start(bf16[512,192]{0,1:T(8,128)(2,1)} %param.17) | copy-start | bytes 589828
  62.8 94.0 %copy-start.4 = (bf16[1536,128]{1,0:T(8,128)(2,1)S(1)}, bf16[1536,128]{1,0:T(8,128)(2,1)}, u32[]{:S(2)}) copy-start(bf16[1536,128]{1,0:T(8,128)(2,1)} %param.21) | copy-start | bytes 1179652
  62.8 94.0 %copy-start.7 = (bf16[128,1536]{1,0:T(8,128)(2,1)S(1)}, bf16[128,1536]{1,0:T(8,128)(2,1)}, u32[]{:S(2)}) copy-start(bf16[128,1536]{1,0:T(8,128)(2,1)} %param.20) | copy-start | bytes 1179652
  63.8 39.9 %all-to-all-start = ((bf16[64,4,512]{2,1,0:T(4,128)(2,1)}), bf16[64,4,512]{2,1,0:T(4,128)(2,1)S(1)}, u32[]{:S(2)}, u32[]{:S(2)}) async-start(bf16[64,4,512]{2,1,0:T(4,128)(2,1)} %broadcast_select_fusion), calls=%async_computation | async-start | bytes 524288 | tf_op jit(solution)/shard_map/all_to_all | solution.py:114
  86.3 56.7 %all-gather.7.cloned.1.call-start = ((), (), s32[]{:S(2)}) async-start(), calls=%async_computation.4 | async-start | bytes 1179648 | tf_op jit(solution)/shard_map/all_gather | solution.py:127
  105.3 88.8 %all-gather.5.cloned.1.call-start = ((), (), s32[]{:S(2)}) async-start(), calls=%async_computation.2 | async-start | bytes 3538944 | tf_op jit(solution)/shard_map/all_gather | solution.py:136
  145.5 3.4 collective-permute-start.8
  147.6 4.8 collective-permute-start.9
  152.4 4.7 collective-permute-start.10
  155.5 4.6 collective-permute-start.11
  160.6 2.0 copy-start.6
  167.4 35.9 %all-to-all-start.1 = ((bf16[64,4,128]{2,1,0:T(4,128)(2,1)}), bf16[64,4,128]{2,1,0:T(4,128)(2,1)S(1)}, u32[]{:S(2)}, u32[]{:S(2)}) async-start(bf16[64,4,128]{2,1,0:T(4,128)(2,1)} %broadcast_select_fusion.1), calls=%async_computation.1 | async-start | bytes 131072 | tf_op jit(solution)/shard_map/all_to_all | solution.py:115
  184.8 13.1 %copy-start.13 = (f32[1536]{0:T(1024)S(1)}, f32[1536]{0:T(1024)}, u32[]{:S(2)}) copy-start(f32[1536]{0:T(1024)} %param.18) | copy-start | bytes 18436
  184.8 93.8 %all-reduce.8.cloned.1.call-start = ((), (), s32[]{:S(2)}) async-start(), calls=%async_computation.3 | async-start | bytes 524288 | tf_op jit(solution)/shard_map/psum | solution.py:168
  194.2 2.8 copy-start.1
  199.9 2.2 copy-start.3
  199.9 2.2 copy-start.5
  202.1 80.3 %copy-start.8 = (bf16[128,1536]{1,0:T(8,128)(2,1)S(1)}, bf16[128,1536]{1,0:T(8,128)(2,1)}, u32[]{:S(2)}) copy-start(bf16[128,1536]{1,0:T(8,128)(2,1)} %param.20) | copy-start | bytes 1179652
  290.1 3.8 copy-start.2
  290.1 3.8 copy-start.9
  290.1 3.8 copy-start.10
  290.1 3.8 copy-start.11
Sparse Core Ops, SparseCore 0:
  105.5 37.4 all-gather.6
  145.6 48.5 all-gather.4
  203.3 75.2 all-reduce.7
where the time goes:
time: 631 us; the launch traced here: 629 us
  blocking collectives  339 us (54%)
  waiting for transfers between devices  139 us (22%)
  starting transfers between devices  67.2 us (11%)
  other arithmetic  25.8 us (4%)
  matrix products  22.7 us (4%)
  local copies, waits for them, and re-layouts  20.6 us (3%)
  between operations  14.3 us (2%)
    psum x1, blocking collectives, train_shard(): lax.psum((grad_weights, gain_contribution), 'space')  256 us
    psum x1, blocking collectives, train_shard(): gain_total = lax.psum(gain_vector, ('grp', 'mem'))  68.2 us
    psum x1, waiting for transfers between devices, train_shard(): lax.psum(partial_pred.astype(jnp.bfloat16), ('grp', 'mem'))  59.5 us
    all_gather x1, waiting for transfers between devices, train_shard(): lax.all_gather(sample_tokens, ('grp', 'mem'), axis=0, tiled=True)  37.6 us
    all_to_all x1, starting transfers between devices, relay_samples(): lax.all_to_all(send_tokens, 'space', split_axis=0, concat_axis=0, tiled=T...  22.4 us
    ppermute x6, starting transfers between devices, with_halo(): lax.ppermute(lax.slice_in_dim(block, block.shape[dim] - width, None, axis...  19.4 us
    all_to_all x1, starting transfers between devices, relay_samples(): lax.all_to_all(send_targets, 'space', split_axis=0, concat_axis=0, tiled=...  17.5 us
    all_to_all x1, waiting for transfers between devices, relay_samples(): lax.all_to_all(send_tokens, 'space', split_axis=0, concat_axis=0, tiled=T...  16.7 us
  transfers between devices with their start and end apart: 17, of which 9 were waited for; matrix products, arithmetic and copies ran while one was open for 4% of the time, Pallas kernels for 0%

commit v1 on v0

v1 whole, which is shorter than its diff:
```python
import math

import jax
import jax.numpy as jnp
from jax import lax
from jax.sharding import Mesh
from jax.sharding import PartitionSpec as P

SPD = 128
STEPS = 3
TILE = 16
HD = 128
NORM_EPSILON = 1e-06

SPACE = ("z", "x")
MEM = ("yhi", "core")
GROUP = ("grp", "yhi", "core")


def material_cond(material, table_row):
    conductance = jnp.zeros(material.shape, jnp.float32)
    for level_id in range(table_row.shape[0]):
        conductance = conductance + jnp.where(
            material == level_id, table_row[level_id], jnp.float32(0.0)
        )
    return conductance


def with_halo(block, width):
    half = lax.axis_index("grp")
    face = jnp.where(half == 0, block[:, :, -width:], block[:, :, :width])
    got = lax.ppermute(face, "grp", [(0, 1), (1, 0)])
    low = jnp.where(half == 0, 0.0, got)
    high = jnp.where(half == 0, got, 0.0)
    block = jnp.concatenate([low, block, high], axis=2)
    count = lax.axis_size(SPACE)
    forward = [(i, i + 1) for i in range(count - 1)]
    backward = [(i + 1, i) for i in range(count - 1)]
    low = lax.ppermute(block[:, -width:], SPACE, forward)
    high = lax.ppermute(block[:, :width], SPACE, backward)
    return jnp.concatenate([low, block, high], axis=1)


def relax_step(field, cond, inside):
    field_ext = jnp.pad(field, ((0, 0), (0, 0), (1, 1)))
    cond_ext = jnp.pad(cond, ((0, 0), (0, 0), (1, 1)))
    center = field_ext[1:-1, 1:-1, 1:-1]
    center_cond = cond_ext[1:-1, 1:-1, 1:-1]
    change = jnp.zeros_like(center)
    for axis_id in range(3):
        for offset in (0, 2):
            window = [slice(1, 1 + size) for size in center.shape]
            window[axis_id] = slice(offset, offset + center.shape[axis_id])
            window = tuple(window)
            change = change + 0.5 * (center_cond + cond_ext[window]) * (field_ext[window] - center)
    return jnp.where(inside, center + change, 0.0)


def solve_slab(field, conductance):
    span_x, span_y = field.shape[:2]
    padded = with_halo(jnp.stack([field, conductance]), STEPS)
    place_x = lax.axis_index(SPACE) * span_x
    place_y = lax.axis_index("grp") * span_y
    total_x = lax.axis_size(SPACE) * span_x
    total_y = lax.axis_size("grp") * span_y
    current, cond = padded[0], padded[1]
    for step in range(STEPS):
        before_last = current
        edge = STEPS - 1 - step
        row = place_x - edge + jnp.arange(span_x + 2 * edge)
        col = place_y - edge + jnp.arange(span_y + 2 * edge)
        inside = ((row >= 0) & (row < total_x))[:, None, None] & (
            (col >= 0) & (col < total_y)
        )[None, :, None]
        current = relax_step(current, cond, inside)
        cond = cond[1:-1, 1:-1]
    return before_last[1:-1, 1:-1], current


def cut_tiles(field, tile_size):
    span_x, span_y, span_z = field.shape
    shaped = field.reshape(
        span_x // tile_size,
        tile_size,
        span_y // tile_size,
        tile_size,
        span_z // tile_size,
        tile_size,
    )
    return shaped.transpose(0, 2, 4, 1, 3, 5).reshape(-1, tile_size, tile_size, tile_size)


def coarse_tokens(tiles, tile_size):
    count_tiles = tiles.shape[0]
    half_size = tile_size // 2
    shaped = tiles.reshape(count_tiles, half_size, 2, half_size, 2, half_size, 2)
    return jnp.mean(shaped, axis=(2, 4, 6)).reshape(count_tiles, -1)


def coarse_targets(tiles, tile_size):
    count_tiles = tiles.shape[0]
    shaped = tiles.reshape(count_tiles, tile_size // 4, 4, tile_size // 4, 4, tile_size // 2, 2)
    return jnp.mean(shaped, axis=(2, 4, 6)).reshape(count_tiles, -1)


def swap(parts, axis):
    return lax.all_to_all(parts, axis, split_axis=0, concat_axis=0, tiled=True)


def spread(own, axis):
    count = lax.axis_size(axis)
    return swap(jnp.broadcast_to(own[None], (count,) + own.shape), axis)


def relay_samples(rows, owner_list, tile_list):
    slot_count = owner_list.shape[1]
    capacity = 2 * slot_count // lax.axis_size(SPACE)
    my_index = lax.axis_index(SPACE)
    same_owner = owner_list[:, :, None] == owner_list[:, None, :]
    slot_order = jnp.arange(slot_count, dtype=jnp.int32)
    earlier = slot_order[None, :] < slot_order[:, None]
    slot_rank = jnp.sum((same_owner & earlier[None]).astype(jnp.int32), axis=2)
    owned_here = owner_list == my_index
    slot_ids = jnp.arange(capacity, dtype=jnp.int32)
    slot_match = owned_here[:, None, :] & (slot_rank[:, None, :] == slot_ids[None, :, None])
    chosen = jnp.sum(jnp.where(slot_match, tile_list[:, None, :] + 1, 0), axis=2) - 1
    present = (chosen >= 0)[:, :, None]
    picked = jnp.maximum(chosen, 0)
    send = jnp.where(present, rows[picked], jnp.zeros((), jnp.bfloat16))
    got = swap(send, SPACE)
    own_owner = jnp.take(owner_list, my_index, axis=0)
    own_rank = jnp.take(slot_rank, my_index, axis=0)
    flat_index = own_owner * capacity + own_rank
    return got.reshape(-1, got.shape[2])[flat_index]


def sum_over_space(grads):
    count_x, count_z = lax.axis_size("x"), lax.axis_size("z")
    columns = grads.shape[-1]
    parts = grads.astype(jnp.bfloat16).reshape(count_x, -1, columns)
    part = jnp.sum(swap(parts, "x").astype(jnp.float32), axis=0)
    parts = part.astype(jnp.bfloat16).reshape(count_z, -1, columns)
    total = jnp.sum(swap(parts, "z").astype(jnp.float32), axis=0).astype(jnp.bfloat16)
    whole = spread(total, "z").reshape(-1, columns)
    return spread(whole, "x").reshape(grads.shape)


def train_shard(samples, targets, embed_weight, layer_norm_gain, w_qkv, w_out, w_read):
    part_index = lax.axis_index(GROUP)
    embed_full = lax.all_gather(embed_weight, GROUP, axis=1, tiled=True)
    mixing = jnp.dot(w_out, w_read, preferred_element_type=jnp.float32)
    mixing_high = mixing.astype(jnp.bfloat16)
    mixing_low = (mixing - mixing_high.astype(jnp.float32)).astype(jnp.bfloat16)
    mixing_pair = jnp.concatenate([mixing_high, mixing_low], axis=0)

    tokens = spread(samples, GROUP).reshape(-1, samples.shape[1])
    row_count = tokens.shape[0]
    embedded = jnp.dot(tokens, embed_full, preferred_element_type=jnp.float32).astype(jnp.bfloat16)
    embedded_wide = embedded.astype(jnp.float32)
    row_mean = jnp.mean(embedded_wide, axis=1, keepdims=True)
    mean_removed = embedded_wide - row_mean
    row_variance = jnp.mean(mean_removed * mean_removed, axis=1, keepdims=True)
    standardized_input = mean_removed * lax.rsqrt(row_variance + NORM_EPSILON)
    normalized_rows = (standardized_input * layer_norm_gain).astype(jnp.bfloat16)
    projected = jnp.einsum(
        "rd,tdc->trc", normalized_rows, w_qkv, preferred_element_type=jnp.float32
    ).astype(jnp.bfloat16)
    seq_count = row_count // SPD
    query_rows, key_rows, value_rows = projected.reshape(3, seq_count, SPD, HD)
    score_scale = 1.0 / math.sqrt(HD)
    scores = (
        jnp.einsum("bqd,bkd->bqk", query_rows, key_rows, preferred_element_type=jnp.float32)
        * score_scale
    )
    top_score = jnp.max(scores, axis=-1, keepdims=True)
    raised = jnp.exp(scores - top_score)
    prob_table = raised / jnp.sum(raised, axis=-1, keepdims=True)
    probs_low = prob_table.astype(jnp.bfloat16)
    attended = jnp.einsum("bqk,bkd->bqd", probs_low, value_rows, preferred_element_type=jnp.float32)
    attended = attended.astype(jnp.bfloat16).reshape(row_count, HD)
    partial_pred = jnp.dot(
        jnp.concatenate([attended, attended], axis=1),
        mixing_pair,
        preferred_element_type=jnp.float32,
    )
    shares = swap(partial_pred.astype(jnp.bfloat16).reshape(seq_count, SPD, -1), GROUP)
    own_rows = lax.dynamic_slice_in_dim(embedded, part_index * SPD, SPD, 0)
    prediction = jnp.sum(shares.astype(jnp.float32), axis=0) + jnp.dot(
        own_rows, w_read, preferred_element_type=jnp.float32
    )
    loss_scale = math.sqrt(
        w_read.shape[0] / (lax.axis_size(SPACE) * row_count * w_read.shape[1])
    )
    own_delta = ((prediction - targets.astype(jnp.float32)) * loss_scale).astype(jnp.bfloat16)
    delta = spread(own_delta, GROUP).reshape(row_count, -1)
    mixing_t = jnp.concatenate([mixing_high, mixing_low], axis=1).T
    grad_attended = jnp.dot(
        jnp.concatenate([delta, delta], axis=1), mixing_t, preferred_element_type=jnp.float32
    ).astype(jnp.bfloat16)
    grad_attended = grad_attended.reshape(seq_count, SPD, HD)
    grad_probs = jnp.einsum(
        "bqd,bkd->bqk", grad_attended, value_rows, preferred_element_type=jnp.float32
    )
    grad_values = jnp.einsum(
        "bqk,bqd->bkd", probs_low, grad_attended, preferred_element_type=jnp.float32
    ).astype(jnp.bfloat16)
    inner_sum = jnp.sum(prob_table * grad_probs, axis=-1, keepdims=True)
    grad_scores = (prob_table * (grad_probs - inner_sum) * score_scale).astype(jnp.bfloat16)
    grad_queries = jnp.einsum(
        "bqk,bkd->bqd", grad_scores, key_rows, preferred_element_type=jnp.float32
    ).astype(jnp.bfloat16)
    grad_keys = jnp.einsum(
        "bqk,bqd->bkd", grad_scores, query_rows, preferred_element_type=jnp.float32
    ).astype(jnp.bfloat16)
    grad_proj = jnp.stack([grad_queries, grad_keys, grad_values]).reshape(3, row_count, HD)
    grad_weights = jnp.einsum(
        "rd,trc->tdc", normalized_rows, grad_proj, preferred_element_type=jnp.float32
    )
    weight_total = sum_over_space(grad_weights)
    gain_share = (
        jnp.sum(w_qkv.astype(jnp.float32) * weight_total.astype(jnp.float32), axis=(0, 2))
        / layer_norm_gain
    )
    gain_total = jnp.sum(spread(gain_share, GROUP), axis=0)
    return (weight_total, gain_total)


def shards(
    start_field,
    material,
    conductivity,
    owners,
    tile_ids,
    embed_weight,
    layer_norm_gain,
    w_qkv,
    w_out,
    w_read,
):
    conductance = material_cond(material, conductivity[0])
    before_last, final_local = solve_slab(start_field[0], conductance)
    token_rows = coarse_tokens(cut_tiles(before_last, TILE), TILE).astype(jnp.bfloat16)
    target_rows = coarse_targets(cut_tiles(final_local, TILE), TILE).astype(jnp.bfloat16)
    rows = jnp.concatenate([token_rows, target_rows], axis=1)
    samples = relay_samples(rows, owners[0, 0, :, :, 0], tile_ids[0, 0])
    width = token_rows.shape[1]
    grad_weights, grad_gain = train_shard(
        samples[:, :width],
        samples[:, width:],
        embed_weight,
        layer_norm_gain,
        w_qkv,
        w_out,
        w_read,
    )
    return (final_local[None], grad_weights, grad_gain)


def solution(mesh):
    halves, space, members = (mesh.shape[name] for name in ("grp", "space", "mem"))
    fine = Mesh(
        mesh.devices.reshape(halves, space // 4, 4, members // 2, 2),
        ("grp", "z", "x", "yhi", "core"),
    )
    placed = (
        P(MEM, SPACE, "grp", None),
        P(SPACE, "grp", None),
        P(MEM, None),
        P(MEM, "grp", None, None, None),
        P(MEM, "grp", None, None),
        P(None, GROUP),
        P(),
        P(None, None, GROUP),
        P(GROUP, None),
        P(),
    )
    return jax.shard_map(
        shards,
        mesh=fine,
        in_specs=placed,
        out_specs=(P(MEM, SPACE, "grp", None), P(None, None, GROUP), P()),
        check_vma=False,
    )
```

time: 631 us -> 278 us (0.44)
  the two profiles are of different devices: /device:TPU:1 before, /device:TPU:32 now
where the time goes in v1:
time: 278 us; the launch traced here: 277 us
  blocking collectives  101 us (36%)
  waiting for transfers between devices  46.5 us (17%)
  starting transfers between devices  39.8 us (14%)
  matrix products  28.1 us (10%)
  local copies, waits for them, and re-layouts  23.9 us (9%)
  other arithmetic  22.6 us (8%)
  between operations  14.5 us (5%)
    all_to_all x6, blocking collectives, swap(): return lax.all_to_all(parts, axis, split_axis=0, concat_axis=0, tiled=True)  101 us
    all_to_all x3, waiting for transfers between devices, swap(): return lax.all_to_all(parts, axis, split_axis=0, concat_axis=0, tiled=True)  44.2 us
    all_to_all x3, starting transfers between devices, swap(): return lax.all_to_all(parts, axis, split_axis=0, concat_axis=0, tiled=True)  28.3 us
    another operation x1, other arithmetic, solve_slab(): padded = with_halo(jnp.stack([field, conductance]), STEPS)  6.21 us
  transfers between devices with their start and end apart: 7, of which 5 were waited for; matrix products, arithmetic and copies ran while one was open for 9% of the time, Pallas kernels for 0%

profile of v1, /device:TPU:32, one launch (start us, length us, event | category | flops | bytes accessed | tf_op | source)
XLA Modules:
  0.0 276.7 jit_solution(928659134558662689)
XLA Ops:
  7.2 1.6 fusion.134
  8.9 6.2 %add_bitcast_fusion = f32[1,16,16,256]{3,2,1,0:T(8,128)S(1)} fusion(s32[16,16,256]{2,1,0:T(8,128)} %param.13, f32[]{:T(128)} %bitcast.7, f32[]{:T(128)} %bitcast.6, f32[]{:T(128)} %bitcast.5, f32[]{:T(128)} %bitcast.4, f32[]{:T(128)} %bitcast.3, f32[]{:T(128)} %bitcast.2, f32[]{:T(128)} %bitcast.1, f32[]{:T(128)} %bitcast), kind=kLoop, calls=%fused_computation.165 | loop fusion | flops 1507328 | bytes 524320 | tf_op jit(solution)/shard_map/stack | solution.py:61
  15.1 1.0 fusion.108
  16.1 3.5 %collective-permute-start = (f32[2,16,3,256]{3,2,1,0:T(4,128)S(1)}, f32[2,16,3,256]{3,2,1,0:T(4,128)S(1)}, u32[]{:S(2)}, u32[]{:S(2)}) collective-permute-start(f32[2,16,3,256]{3,2,1,0:T(4,128)S(1)} %fusion.108), channel_id=1, source_target_pairs={{0,256},{256,0},{1,257},{257,1},{2,258},{258,2},{3,259},{259,3},{4... | collective-permute-start | bytes 294920 | tf_op jit(solution)/shard_map/ppermute | solution.py:32
  20.4 3.5 %convert_reduce_fusion.1 = s32[64,128]{1,0:T(8,128)S(1)} fusion(s32[64,128]{1,0:T(8,128)} %bitcast.94, pred[128,128]{1,0:T(8,128)(4,1)S(1)} %iota_compare_fusion.1), kind=kLoop, calls=%fused_computation.11 | loop fusion | flops 4186112 | bytes 81920 | tf_op jit(solution)/shard_map/reduce_sum | solution.py:122
  25.2 3.4 %collective-permute-start.1 = (f32[2,3,22,256]{3,2,1,0:T(8,128)S(1)}, f32[2,3,22,256]{3,2,1,0:T(8,128)S(1)}, u32[]{:S(2)}, u32[]{:S(2)}) collective-permute-start(f32[2,3,22,256]{3,2,1,0:T(8,128)S(1)} %get-tuple-element.22), channel_id=1, source_target_pairs={{0,4},{4,8},{8,12},{12,16},{16,20},{20,24},{24,28},{28,32},{32,36}... | collective-permute-start | bytes 405512 | tf_op jit(solution)/shard_map/ppermute | solution.py:39
  28.6 4.6 %collective-permute-start.2 = (f32[2,3,22,256]{3,2,1,0:T(8,128)S(1)}, f32[2,3,22,256]{3,2,1,0:T(8,128)S(1)}, u32[]{:S(2)}, u32[]{:S(2)}) collective-permute-start(f32[2,3,22,256]{3,2,1,0:T(8,128)S(1)} %get-tuple-element.23), channel_id=1, source_target_pairs={{4,0},{8,4},{12,8},{16,12},{20,16},{24,20},{28,24},{32,28},{36,32}... | collective-permute-start | bytes 405512 | tf_op jit(solution)/shard_map/ppermute | solution.py:40
  33.5 1.0 collective-permute-done.1
  34.5 1.3 collective-permute-done.2
  38.2 2.0 reshape.290
  40.3 1.9 copy.49
  42.2 1.4 reduce_sum.125
  43.7 2.0 reshape.291
  45.7 1.9 copy.50
  47.6 1.1 reduce_sum.126
  48.8 1.2 gather_fusion
  50.1 1.0 broadcast_select_fusion
  51.1 20.1 %all-to-all-start = ((bf16[64,4,640]{2,1,0:T(4,128)(2,1)}), bf16[64,4,640]{2,1,0:T(4,128)(2,1)S(1)}, u32[]{:S(2)}, u32[]{:S(2)}) async-start(bf16[64,4,640]{2,1,0:T(4,128)(2,1)} %broadcast_select_fusion), calls=%async_computation | async-start | bytes 655360 | tf_op jit(solution)/shard_map/all_to_all | solution.py:107
  71.9 22.1 %all-to-all-done = bf16[64,4,640]{2,1,0:T(4,128)(2,1)S(1)} async-done(((bf16[64,4,640]{2,1,0:T(4,128)(2,1)}), bf16[64,4,640]{2,1,0:T(4,128)(2,1)S(1)}, u32[]{:S(2)}, u32[]{:S(2)}) %all-to-all-start) | async-done | bytes 327712 | tf_op jit(solution)/shard_map/all_to_all | solution.py:107
  95.0 1.1 broadcast_in_dim.187
  96.1 4.2 %all-to-all-start.1 = ((bf16[8,128,512]{2,1,0:T(8,128)(2,1)}), bf16[8,128,512]{2,1,0:T(8,128)(2,1)S(1)}, u32[]{:S(2)}, u32[]{:S(2)}) async-start(bf16[8,128,512]{2,1,0:T(8,128)(2,1)} %broadcast_in_dim.187), calls=%async_computation.1 | async-start | bytes 2097152 | tf_op jit(solution)/shard_map/all_to_all | solution.py:107
  101.2 14.8 %all-to-all-done.1 = bf16[8,128,512]{2,1,0:T(8,128)(2,1)S(1)} async-done(((bf16[8,128,512]{2,1,0:T(8,128)(2,1)}), bf16[8,128,512]{2,1,0:T(8,128)(2,1)S(1)}, u32[]{:S(2)}, u32[]{:S(2)}) %all-to-all-start.1) | async-done | bytes 1048608 | tf_op jit(solution)/shard_map/all_to_all | solution.py:107
  117.0 3.6 %convert_reduce_fusion = (f32[1024]{0:T(1024)S(1)}, bf16[1024,1536]{1,0:T(8,128)(2,1)S(1)}) fusion(bf16[1024,512]{1,0:T(8,128)(2,1)} %bitcast.89, bf16[512,1536]{0,1:T(8,128)(2,1)} %all-gather.2.cloned.1.call-done), kind=kOutput, calls=%fused_computation.5 | convolution fusion | flops 1615330304 | bytes 5771264 | tf_op jit(solution)/shard_map/dot_general | solution.py:158
  121.9 1.9 fusion.9
  124.7 2.8 fusion.135
  127.5 2.4 convolution_convert_fusion.8
  129.9 2.0 convolution_convert_fusion.7
  131.9 4.0 %all-to-all-start.2 = ((bf16[8,128,128]{2,1,0:T(8,128)(2,1)}), bf16[8,128,128]{2,1,0:T(8,128)(2,1)}, u32[]{:S(2)}, u32[]{:S(2)}) async-start(bf16[8,128,128]{2,1,0:T(8,128)(2,1)} %bitcast.96), calls=%async_computation.2 | async-start | bytes 524288 | tf_op jit(solution)/shard_map/all_to_all | solution.py:107
  136.0 7.2 %all-to-all-done.2 = bf16[8,128,128]{2,1,0:T(8,128)(2,1)} async-done(((bf16[8,128,128]{2,1,0:T(8,128)(2,1)}), bf16[8,128,128]{2,1,0:T(8,128)(2,1)}, u32[]{:S(2)}, u32[]{:S(2)}) %all-to-all-start.2) | async-done | bytes 262176 | tf_op jit(solution)/shard_map/all_to_all | solution.py:107
  143.2 1.0 convert_reduce_fusion.2
  144.2 1.0 fusion.20
  145.3 9.8 %all_to_all.46 = bf16[8,128,128]{2,1,0:T(8,128)(2,1)S(1)} all-to-all(bf16[8,128,128]{2,1,0:T(8,128)(2,1)S(1)} %broadcast_in_dim.188), channel_id=1, replica_groups=mesh['grp'=2,'z'=16,'x'=4,'yhi'=2,'core'=2] {'grp','yhi','core'}, dimensions={0} | all-to-all | bytes 524288 | tf_op jit(solution)/shard_map/all_to_all | solution.py:107
  155.1 1.1 convolution_convert_fusion.6
  156.2 1.1 fusion.136
  157.3 2.7 convolution_convert_fusion.5
  160.0 2.7 convolution_convert_fusion.4
  162.7 2.3 convolution_convert_fusion.3
  165.0 1.8 copy.56
  166.7 1.8 copy.57
  168.5 1.8 copy.58
  170.3 3.7 %fusion.8 = bf16[3,1536,128]{1,2,0:T(8,128)(2,1)} fusion(bf16[1024,1536]{1,0:T(8,128)(2,1)S(1)} %get-tuple-element.41, f32[1536]{0:T(1024)S(1)} %copy-done.10, f32[1024]{0:T(1024)S(1)} %add_rsqrt_fusion, f32[1024]{0:T(1024)S(1)} %broadcast_multiply_fusion, bf16[1,1024,128]{1,2,0:T(8,128)(2,1)} %copy.58, bf16[1,1024,128]{1,2,0:T(8,128)(2,1)} %copy.57, ...), kind=kOutput, calls=%fused_computation.15 | convolution fusion | flops 1217200128 | bytes 5126144 | tf_op jit(solution)/shard_map/rd,trc->tdc/dot_general | solution.py:216
  174.1 1.7 copy.59
  175.8 19.2 %all_to_all.47 = bf16[4,1152,128]{2,1,0:T(8,128)(2,1)S(1)} all-to-all(bf16[4,1152,128]{2,1,0:T(8,128)(2,1)S(1)} %bitcast.85), channel_id=1, replica_groups=mesh['grp'=2,'z'=16,'x'=4,'yhi'=2,'core'=2] {'x'}, dimensions={0} | all-to-all | bytes 2359296 | tf_op jit(solution)/shard_map/all_to_all | solution.py:107
  195.3 22.5 %all_to_all.48 = bf16[16,72,128]{2,1,0:T(8,128)(2,1)S(1)} all-to-all(bf16[16,72,128]{2,1,0:T(8,128)(2,1)S(1)} %bitcast.86), channel_id=1, replica_groups=mesh['grp'=2,'z'=16,'x'=4,'yhi'=2,'core'=2] {'z'}, dimensions={0} | all-to-all | bytes 589824 | tf_op jit(solution)/shard_map/all_to_all | solution.py:107
  217.9 24.2 %all_to_all.49 = bf16[16,72,128]{2,1,0:T(8,128)(2,1)S(1)} all-to-all(bf16[16,72,128]{2,1,0:T(8,128)(2,1)S(1)} %broadcast_in_dim.189), channel_id=1, replica_groups=mesh['grp'=2,'z'=16,'x'=4,'yhi'=2,'core'=2] {'z'}, dimensions={0} | all-to-all | bytes 589824 | tf_op jit(solution)/shard_map/all_to_all | solution.py:107
  242.3 16.6 %all_to_all.50 = bf16[4,1152,128]{2,1,0:T(8,128)(2,1)S(1)} all-to-all(bf16[4,1152,128]{2,1,0:T(8,128)(2,1)S(1)} %broadcast_in_dim.191), channel_id=1, replica_groups=mesh['grp'=2,'z'=16,'x'=4,'yhi'=2,'core'=2] {'x'}, dimensions={0} | all-to-all | bytes 2359296 | tf_op jit(solution)/shard_map/all_to_all | solution.py:107
  259.4 8.8 %all_to_all.51 = f32[8,1,1536]{2,1,0:T(1,128)S(1)} all-to-all(f32[8,1,1536]{2,1,0:T(1,128)S(1)} %broadcast_in_dim.192), channel_id=1, replica_groups=mesh['grp'=2,'z'=16,'x'=4,'yhi'=2,'core'=2] {'grp','yhi','core'}, dimensions={0} | all-to-all | bytes 98304 | tf_op jit(solution)/shard_map/all_to_all | solution.py:107
  268.8 1.0 copy.65
  (75 shorter events, 12.5 us)
Async XLA Ops:
  7.2 93.2 %copy-start = (bf16[1536,128]{1,0:T(8,128)(2,1)S(1)}, bf16[1536,128]{1,0:T(8,128)(2,1)}, u32[]{:S(2)}) copy-start(bf16[1536,128]{1,0:T(8,128)(2,1)} %param.21) | copy-start | bytes 1179652
  7.2 18.0 %copy-start.1 = (f32[1,16,16,256]{3,2,1,0:T(8,128)S(1)}, f32[1,16,16,256]{3,2,1,0:T(8,128)}, u32[]{:S(2)}) copy-start(f32[1,16,16,256]{3,2,1,0:T(8,128)} %param.12) | copy-start | bytes 786436
  7.2 108.8 %all-gather.2.cloned.1.call-start = ((), (), s32[]{:S(2)}) async-start(), calls=%async_computation.9 | async-start | bytes 1769472 | tf_op jit(solution)/shard_map/all_gather | solution.py:150
  16.1 9.0 %collective-permute-start = (f32[2,16,3,256]{3,2,1,0:T(4,128)S(1)}, f32[2,16,3,256]{3,2,1,0:T(4,128)S(1)}, u32[]{:S(2)}, u32[]{:S(2)}) collective-permute-start(f32[2,16,3,256]{3,2,1,0:T(4,128)S(1)} %fusion.108), channel_id=1, source_target_pairs={{0,256},{256,0},{1,257},{257,1},{2,258},{258,2},{3,259},{259,3},{4... | collective-permute-start | bytes 294920 | tf_op jit(solution)/shard_map/ppermute | solution.py:32
  25.2 9.3 %collective-permute-start.1 = (f32[2,3,22,256]{3,2,1,0:T(8,128)S(1)}, f32[2,3,22,256]{3,2,1,0:T(8,128)S(1)}, u32[]{:S(2)}, u32[]{:S(2)}) collective-permute-start(f32[2,3,22,256]{3,2,1,0:T(8,128)S(1)} %get-tuple-element.22), channel_id=1, source_target_pairs={{0,4},{4,8},{8,12},{12,16},{16,20},{20,24},{24,28},{28,32},{32,36}... | collective-permute-start | bytes 405512 | tf_op jit(solution)/shard_map/ppermute | solution.py:39
  28.6 7.2 %collective-permute-start.2 = (f32[2,3,22,256]{3,2,1,0:T(8,128)S(1)}, f32[2,3,22,256]{3,2,1,0:T(8,128)S(1)}, u32[]{:S(2)}, u32[]{:S(2)}) collective-permute-start(f32[2,3,22,256]{3,2,1,0:T(8,128)S(1)} %get-tuple-element.23), channel_id=1, source_target_pairs={{4,0},{8,4},{12,8},{16,12},{20,16},{24,20},{28,24},{32,28},{36,32}... | collective-permute-start | bytes 405512 | tf_op jit(solution)/shard_map/ppermute | solution.py:40
  38.2 5.4 %copy-start.4 = (f32[16,16,256]{2,1,0:T(8,128)}, f32[16,16,256]{2,1,0:T(8,128)S(1)}, u32[]{:S(2)}) copy-start(f32[16,16,256]{2,1,0:T(8,128)S(1)} %get-tuple-element.29) | copy-start | bytes 786436
  51.1 42.9 %all-to-all-start = ((bf16[64,4,640]{2,1,0:T(4,128)(2,1)}), bf16[64,4,640]{2,1,0:T(4,128)(2,1)S(1)}, u32[]{:S(2)}, u32[]{:S(2)}) async-start(bf16[64,4,640]{2,1,0:T(4,128)(2,1)} %broadcast_select_fusion), calls=%async_computation | async-start | bytes 655360 | tf_op jit(solution)/shard_map/all_to_all | solution.py:107
  94.1 6.2 %copy-start.8 = (bf16[128,1536]{1,0:T(8,128)(2,1)S(1)}, bf16[128,1536]{1,0:T(8,128)(2,1)}, u32[]{:S(2)}) copy-start(bf16[128,1536]{1,0:T(8,128)(2,1)} %param.20) | copy-start | bytes 1179652
  95.0 1.1 copy-start.7
  96.1 19.9 %all-to-all-start.1 = ((bf16[8,128,512]{2,1,0:T(8,128)(2,1)}), bf16[8,128,512]{2,1,0:T(8,128)(2,1)S(1)}, u32[]{:S(2)}, u32[]{:S(2)}) async-start(bf16[8,128,512]{2,1,0:T(8,128)(2,1)} %broadcast_in_dim.187), calls=%async_computation.1 | async-start | bytes 2097152 | tf_op jit(solution)/shard_map/all_to_all | solution.py:107
  116.0 1.0 copy-start.5
  120.6 1.3 copy-start.2
  120.6 1.3 copy-start.10
  131.9 11.3 %all-to-all-start.2 = ((bf16[8,128,128]{2,1,0:T(8,128)(2,1)}), bf16[8,128,128]{2,1,0:T(8,128)(2,1)}, u32[]{:S(2)}, u32[]{:S(2)}) async-start(bf16[8,128,128]{2,1,0:T(8,128)(2,1)} %bitcast.96), calls=%async_computation.2 | async-start | bytes 524288 | tf_op jit(solution)/shard_map/all_to_all | solution.py:107
  143.2 13.0 %copy-start.6 = (bf16[1,1024,128]{2,1,0:T(8,128)(2,1)S(1)}, bf16[1,1024,128]{2,1,0:T(8,128)(2,1)}, u32[]{:S(2)}) copy-start(bf16[1,1024,128]{2,1,0:T(8,128)(2,1)} %get-tuple-element.20) | copy-start | bytes 786436
  156.2 1.1 copy-start.9
  217.8 41.1 %copy-start.3 = (bf16[3,1536,128]{2,1,0:T(8,128)(2,1)S(1)}, bf16[3,1536,128]{2,1,0:T(8,128)(2,1)}, u32[]{:S(2)}) copy-start(bf16[3,1536,128]{2,1,0:T(8,128)(2,1)} %param.19) | copy-start | bytes 3538948
Sparse Core Ops, SparseCore 0:
  19.7 46.6 all-gather.1

commit v2 on v1

v2 whole, which is shorter than its diff:
```python
import functools
import math

import jax
import jax.numpy as jnp
from jax import lax
from jax.experimental import pallas as pl
from jax.experimental.pallas import tpu as pltpu
from jax.sharding import Mesh
from jax.sharding import PartitionSpec as P

SPD = 128
STEPS = 3
TILE = 16
HD = 128
NORM_EPSILON = 1e-06

SPACE = ("z", "x")
MEM = ("yhi", "core")
GROUP = ("grp", "yhi", "core")
CHIPS = ("grp", "yhi")

PAD = 8
BLOCK_ROWS = 256
VMEM = pl.BlockSpec(memory_space=pltpu.VMEM)
SMEM = pl.BlockSpec(memory_space=pltpu.SMEM)
LIMIT = 48 * 1024 * 1024
EXACT = lax.Precision.HIGHEST


def swap(parts, axis):
    return lax.all_to_all(parts, axis, split_axis=0, concat_axis=0, tiled=True)


def spread(own, axis):
    count = lax.axis_size(axis)
    return swap(jnp.broadcast_to(own[None], (count,) + own.shape), axis)


def swap_cores(own):
    return lax.ppermute(own, "core", [(0, 1), (1, 0)])


def halos(block, width):
    half = lax.axis_index("grp")
    face = jnp.where(half == 0, block[:, :, -width:], block[:, :, :width])
    side = lax.ppermute(face, "grp", [(0, 1), (1, 0)])
    count = lax.axis_size(SPACE)
    forward = [(i, i + 1) for i in range(count - 1)]
    backward = [(i + 1, i) for i in range(count - 1)]
    top = jnp.concatenate([side[:, -width:], block[:, -width:], side[:, -width:]], axis=2)
    bottom = jnp.concatenate([side[:, :width], block[:, :width], side[:, :width]], axis=2)
    low = lax.ppermute(top, SPACE, forward)
    high = lax.ppermute(bottom, SPACE, backward)
    return side, low, high


def slab_kernel(
    place_ref,
    table_ref,
    field_ref,
    material_ref,
    side_ref,
    low_ref,
    high_ref,
    pick_ref,
    final_ref,
    send_ref,
    field_a,
    field_b,
    cond,
    coef,
    pairs,
    quads,
    rows_t,
    *,
    total_x,
    total_y,
):
    span_x, span_y, span_z = field_ref.shape
    width = low_ref.shape[1]
    rows = span_y + 2 * PAD
    planes = span_x + 2 * width
    own_x = slice(width, width + span_x)
    own_y = slice(PAD, PAD + span_y)
    ext_y = slice(PAD - width, PAD + span_y + width)

    field_a[...] = jnp.zeros_like(field_a)
    cond[...] = jnp.zeros_like(cond)
    for part, target in ((0, field_a), (1, cond)):
        target[own_x, slice(PAD - width, PAD), :] = side_ref[part]
        target[own_x, slice(PAD + span_y, PAD + span_y + width), :] = side_ref[part]
        target[slice(0, width), ext_y, :] = low_ref[part]
        target[slice(width + span_x, planes), ext_y, :] = high_ref[part]
    field_a[own_x, own_y, :] = field_ref[...]
    cond[own_x, own_y, :] = material_ref[...].astype(jnp.float32)

    place_x = place_ref[0] * span_x - width
    place_y = place_ref[1] * span_y - PAD
    row_id = place_y + lax.broadcasted_iota(jnp.int32, (rows, span_z), 0)
    col_id = lax.broadcasted_iota(jnp.int32, (rows, span_z), 1)
    inside_y = (row_id >= 0) & (row_id < total_y)
    first_z = col_id == 0
    last_z = col_id == span_z - 1

    def inside(plane):
        at = place_x + plane
        in_x = ((at >= 0) & (at < total_x)).astype(jnp.int32)
        return inside_y & (jnp.full((rows, span_z), in_x) > 0)

    def set_cond(plane, _):
        kind = cond[plane]
        value = jnp.zeros_like(kind)
        for level in range(table_ref.shape[0]):
            value = jnp.where(kind == float(level), table_ref[level], value)
        keep = inside(plane)
        cond[plane] = jnp.where(keep, value, 0.0)
        field_a[plane] = jnp.where(keep, field_a[plane], 0.0)
        return 0

    lax.fori_loop(0, planes, set_cond, 0)

    def set_coef(plane, _):
        mine = 0.5 * cond[plane]
        keep = inside(plane)
        ups = mine + pltpu.roll(mine, 1, 0)
        downs = mine + pltpu.roll(mine, rows - 1, 0)
        before = mine + jnp.where(first_z, 0.0, pltpu.roll(mine, 1, 1))
        after = mine + jnp.where(last_z, 0.0, pltpu.roll(mine, span_z - 1, 1))
        left = mine + 0.5 * cond[plane - 1]
        right = mine + 0.5 * cond[plane + 1]
        rest = 1.0 - (ups + downs + before + after + left + right)
        coef[0, plane] = jnp.where(keep, rest, 0.0)
        coef[1, plane] = jnp.where(keep, left, 0.0)
        coef[2, plane] = jnp.where(keep, right, 0.0)
        coef[3, plane] = jnp.where(keep, ups, 0.0)
        coef[4, plane] = jnp.where(keep, downs, 0.0)
        coef[5, plane] = jnp.where(keep & ~first_z, before, 0.0)
        coef[6, plane] = jnp.where(keep & ~last_z, after, 0.0)
        return 0

    lax.fori_loop(1, planes - 1, set_coef, 0)

    def step(source, target):
        def one(plane, _):
            mid = source[plane]
            value = coef[0, plane] * mid
            value = value + coef[1, plane] * source[plane - 1]
            value = value + coef[2, plane] * source[plane + 1]
            value = value + coef[3, plane] * pltpu.roll(mid, 1, 0)
            value = value + coef[4, plane] * pltpu.roll(mid, rows - 1, 0)
            value = value + coef[5, plane] * pltpu.roll(mid, 1, 1)
            value = value + coef[6, plane] * pltpu.roll(mid, span_z - 1, 1)
            target[plane] = value
            return 0

        return one

    for number in range(STEPS):
        source, target = (field_a, field_b) if number % 2 == 0 else (field_b, field_a)
        lax.fori_loop(1 + number, planes - 1 - number, step(source, target), 0)

    before_last, last = (field_a, field_b) if STEPS % 2 == 1 else (field_b, field_a)
    final_ref[...] = last[own_x, own_y, :]

    for i in range(span_x // 2):
        plane = width + 2 * i
        pairs[span_y * i : span_y * (i + 1), :] = (
            before_last[plane, own_y, :] + before_last[plane + 1, own_y, :]
        )
    for i in range(span_x // 4):
        plane = width + 4 * i
        quads[span_y * i : span_y * (i + 1), :] = (
            last[plane, own_y, :] + last[plane + 1, own_y, :]
        ) + (last[plane + 2, own_y, :] + last[plane + 3, own_y, :])
    depth = TILE // 2
    tiles = span_z // TILE
    z_id = lax.broadcasted_iota(jnp.int32, (span_z, depth * tiles), 0) // 2
    c_id = lax.broadcasted_iota(jnp.int32, (span_z, depth * tiles), 1)
    fold_z = (z_id == (c_id % tiles) * depth + c_id // tiles).astype(jnp.float32)

    def fold_y(stacked, group):
        size = stacked.shape[0]
        out_id = lax.broadcasted_iota(jnp.int32, (size // group, size), 0)
        in_id = lax.broadcasted_iota(jnp.int32, (size // group, size), 1)
        matrix = (out_id == in_id // group).astype(jnp.float32)
        part = jnp.dot(stacked, fold_z, precision=EXACT, preferred_element_type=jnp.float32)
        return jnp.dot(matrix, part, precision=EXACT, preferred_element_type=jnp.float32)

    fine = fold_y(pairs[...], 2) * 0.125
    rough = fold_y(quads[...], 4) * 0.03125
    fine_rows, rough_rows = fine.shape[0], rough.shape[0]
    for k in range(depth):
        cut = slice(tiles * k, tiles * (k + 1))
        rows_t[fine_rows * k : fine_rows * (k + 1), :] = fine[:, cut]
        start = fine_rows * depth + rough_rows * k
        rows_t[start : start + rough_rows, :] = rough[:, cut]
    send_ref[...] = lax.dot_general(
        pick_ref[...],
        rows_t[...].astype(jnp.bfloat16),
        (((1,), (1,)), ((), ())),
        preferred_element_type=jnp.float32,
    ).astype(jnp.bfloat16)


def run_slab(field, material, table, pick):
    span_x, span_y, span_z = field.shape
    width = STEPS
    block = jnp.stack([field, material.astype(jnp.float32)])
    side, low, high = halos(block, width)
    place = jnp.stack([lax.axis_index(SPACE), lax.axis_index("grp")]).astype(jnp.int32)
    planes, rows = span_x + 2 * width, span_y + 2 * PAD
    tiles = span_z // TILE
    values = (span_x * span_y // 4 + span_x * span_y // 16) * TILE // 2
    extended = pltpu.VMEM((planes, rows, span_z), jnp.float32)
    return pl.pallas_call(
        functools.partial(
            slab_kernel,
            total_x=lax.axis_size(SPACE) * span_x,
            total_y=lax.axis_size("grp") * span_y,
        ),
        out_shape=(
            jax.ShapeDtypeStruct(field.shape, jnp.float32),
            jax.ShapeDtypeStruct((pick.shape[0], values), jnp.bfloat16),
        ),
        in_specs=[SMEM, SMEM] + [VMEM] * 6,
        out_specs=(VMEM, VMEM),
        scratch_shapes=[
            extended,
            extended,
            extended,
            pltpu.VMEM((7, planes, rows, span_z), jnp.float32),
            pltpu.VMEM((span_x * span_y // 2, span_z), jnp.float32),
            pltpu.VMEM((span_x * span_y // 4, span_z), jnp.float32),
            pltpu.VMEM((values, tiles), jnp.float32),
        ],
        compiler_params=pltpu.CompilerParams(vmem_limit_bytes=LIMIT),
        name="slab",
    )(place, table, field, material, side, low, high, pick)


def slots(owner_list, tile_list, tile_count):
    shard_count, slot_count = owner_list.shape
    capacity = 2 * slot_count // shard_count
    my_index = lax.axis_index(SPACE)
    same_owner = owner_list[:, :, None] == owner_list[:, None, :]
    slot_order = jnp.arange(slot_count, dtype=jnp.int32)
    earlier = slot_order[None, :] < slot_order[:, None]
    slot_rank = jnp.sum((same_owner & earlier[None]).astype(jnp.int32), axis=2)
    owned_here = owner_list == my_index
    slot_ids = jnp.arange(capacity, dtype=jnp.int32)
    slot_match = owned_here[:, None, :] & (slot_rank[:, None, :] == slot_ids[None, :, None])
    chosen = jnp.sum(jnp.where(slot_match, tile_list[:, None, :] + 1, 0), axis=2) - 1
    tile_ids = jnp.arange(tile_count, dtype=jnp.int32)
    pick = (chosen.reshape(-1, 1) == tile_ids[None, :]).astype(jnp.bfloat16)
    own_owner = jnp.take(owner_list, my_index, axis=0)
    own_rank = jnp.take(slot_rank, my_index, axis=0)
    flat_index = own_owner * capacity + own_rank
    flat_ids = jnp.arange(shard_count * capacity, dtype=jnp.int32)
    place = (flat_index[:, None] == flat_ids[None, :]).astype(jnp.bfloat16)
    return pick, place


def forward_kernel(
    token_ref, embed_ref, gain_ref, proj_w_ref, mix_ref, read_ref,
    normed_ref, proj_ref, prob_ref, pred_ref, *base_ref,
):
    embedded = jnp.dot(
        token_ref[...], embed_ref[...], preferred_element_type=jnp.float32
    ).astype(jnp.bfloat16)
    wide = embedded.astype(jnp.float32)
    mean = jnp.mean(wide, axis=1, keepdims=True)
    removed = wide - mean
    variance = jnp.mean(removed * removed, axis=1, keepdims=True)
    normed = (removed * lax.rsqrt(variance + NORM_EPSILON) * gain_ref[...]).astype(jnp.bfloat16)
    normed_ref[...] = normed
    proj = jnp.dot(normed, proj_w_ref[...], preferred_element_type=jnp.float32).astype(jnp.bfloat16)
    proj_ref[...] = proj
    attended = []
    for seq in range(token_ref.shape[0] // SPD):
        rows = slice(seq * SPD, (seq + 1) * SPD)
        query, key, value = (proj[rows, i * HD : (i + 1) * HD] for i in range(3))
        scores = lax.dot_general(
            query, key, (((1,), (1,)), ((), ())), preferred_element_type=jnp.float32
        ) * (1.0 / math.sqrt(HD))
        raised = jnp.exp(scores - jnp.max(scores, axis=-1, keepdims=True))
        probs = raised / jnp.sum(raised, axis=-1, keepdims=True)
        prob_ref[rows, :] = probs
        attended.append(
            jnp.dot(
                probs.astype(jnp.bfloat16), value, preferred_element_type=jnp.float32
            ).astype(jnp.bfloat16)
        )
    attended = jnp.concatenate(attended, axis=0)
    pred_ref[...] = jnp.dot(
        jnp.concatenate([attended, attended], axis=1),
        mix_ref[...],
        preferred_element_type=jnp.float32,
    ).astype(pred_ref.dtype)
    if base_ref:
        base_ref[0][...] = jnp.dot(embedded, read_ref[...], preferred_element_type=jnp.float32)


def whole(array):
    return pl.BlockSpec(array.shape, lambda i: (0,) * array.ndim)


def by_rows(columns):
    return pl.BlockSpec((BLOCK_ROWS, columns), lambda i: (i, 0))


def run_forward(tokens, embed, gain, proj_w, mix, read, own):
    rows, token_width = tokens.shape
    model, heads = proj_w.shape
    out_width = read.shape[1]
    shapes = [
        jax.ShapeDtypeStruct((rows, model), jnp.bfloat16),
        jax.ShapeDtypeStruct((rows, heads), jnp.bfloat16),
        jax.ShapeDtypeStruct((rows, SPD), jnp.float32),
        jax.ShapeDtypeStruct((rows, out_width), jnp.float32 if own else jnp.bfloat16),
    ]
    if own:
        shapes.append(jax.ShapeDtypeStruct((rows, out_width), jnp.float32))
    flops = 2 * rows * model * (token_width + heads)
    return pl.pallas_call(
        forward_kernel,
        grid=(rows // BLOCK_ROWS,),
        out_shape=tuple(shapes),
        in_specs=[by_rows(token_width)]
        + [whole(array) for array in (embed, gain, proj_w, mix, read)],
        out_specs=tuple(by_rows(shape.shape[1]) for shape in shapes),
        compiler_params=pltpu.CompilerParams(vmem_limit_bytes=LIMIT),
        cost_estimate=pl.CostEstimate(
            flops=flops, bytes_accessed=rows * model * 8, transcendentals=rows * SPD
        ),
        name="forward_own" if own else "forward_other",
    )(tokens, embed, gain, proj_w, mix, read)


def backward_kernel(delta_ref, mix_t_ref, proj_ref, prob_ref, normed_ref, *rest):
    start_ref = rest[0] if len(rest) == 3 else None
    out_ref, total = rest[-2], rest[-1]
    step = pl.program_id(0)
    delta = delta_ref[...]
    grad_attended = jnp.dot(
        jnp.concatenate([delta, delta], axis=1),
        mix_t_ref[...],
        preferred_element_type=jnp.float32,
    ).astype(jnp.bfloat16)
    across = (((1,), (1,)), ((), ()))
    down = (((0,), (0,)), ((), ()))
    grads = []
    for seq in range(delta_ref.shape[0] // SPD):
        rows = slice(seq * SPD, (seq + 1) * SPD)
        query, key, value = (proj_ref[rows, i * HD : (i + 1) * HD] for i in range(3))
        upper = grad_attended[rows]
        probs = prob_ref[rows, :]
        grad_probs = lax.dot_general(upper, value, across, preferred_element_type=jnp.float32)
        grad_value = lax.dot_general(
            probs.astype(jnp.bfloat16), upper, down, preferred_element_type=jnp.float32
        )
        inner = jnp.sum(probs * grad_probs, axis=-1, keepdims=True)
        grad_scores = (probs * (grad_probs - inner) * (1.0 / math.sqrt(HD))).astype(jnp.bfloat16)
        grad_query = jnp.dot(grad_scores, key, preferred_element_type=jnp.float32)
        grad_key = lax.dot_general(grad_scores, query, down, preferred_element_type=jnp.float32)
        grads.append(
            jnp.concatenate([grad_query, grad_key, grad_value], axis=1).astype(jnp.bfloat16)
        )
    grads = jnp.concatenate(grads, axis=0)

    @pl.when(step == 0)
    def _():
        if start_ref is None:
            total[...] = jnp.zeros_like(total)
        else:
            total[...] = start_ref[...]

    total[...] += lax.dot_general(
        normed_ref[...], grads, down, preferred_element_type=jnp.float32
    )

    @pl.when(step == pl.num_programs(0) - 1)
    def _():
        if start_ref is None:
            out_ref[...] = total[...]
        else:
            for i in range(out_ref.shape[0]):
                out_ref[i] = total[:, i * HD : (i + 1) * HD].astype(out_ref.dtype)


def run_backward(delta, mix_t, proj, prob, normed, start):
    rows, model = normed.shape
    heads = proj.shape[1]
    if start is None:
        out = jax.ShapeDtypeStruct((model, heads), jnp.float32)
    else:
        out = jax.ShapeDtypeStruct((heads // HD, model, HD), jnp.bfloat16)
    operands = [delta, mix_t, proj, prob, normed]
    specs = [
        by_rows(delta.shape[1]), whole(mix_t), by_rows(heads), by_rows(SPD), by_rows(model),
    ]
    if start is not None:
        operands.append(start)
        specs.append(whole(start))
    return pl.pallas_call(
        backward_kernel,
        grid=(rows // BLOCK_ROWS,),
        out_shape=out,
        in_specs=specs,
        out_specs=whole(out),
        scratch_shapes=[pltpu.VMEM((model, heads), jnp.float32)],
        compiler_params=pltpu.CompilerParams(vmem_limit_bytes=LIMIT),
        cost_estimate=pl.CostEstimate(
            flops=2 * rows * model * heads, bytes_accessed=rows * model * 4, transcendentals=0
        ),
        name="backward_own" if start is None else "backward_other",
    )(*operands)


def sum_over_space(parts):
    count_x, count_z = lax.axis_size("x"), lax.axis_size("z")
    shape, columns = parts.shape, parts.shape[-1]
    parts = parts.reshape(count_x, -1, columns)
    part = jnp.sum(swap(parts, "x").astype(jnp.float32), axis=0)
    parts = part.astype(jnp.bfloat16).reshape(count_z, -1, columns)
    total = jnp.sum(swap(parts, "z").astype(jnp.float32), axis=0).astype(jnp.bfloat16)
    gathered = spread(total, "z").reshape(-1, columns)
    return spread(gathered, "x").reshape(shape)


def shards(
    start_field,
    material,
    conductivity,
    owners,
    tile_ids,
    embed_weight,
    layer_norm_gain,
    w_qkv,
    w_out,
    w_read,
):
    field = start_field[0]
    span_x, span_y, span_z = field.shape
    depth = TILE // 2
    token_width = embed_weight.shape[0]
    target_width = w_read.shape[1]

    embed_own = embed_weight.reshape(-1, depth, embed_weight.shape[1])
    embed_own = embed_own.transpose(1, 0, 2).reshape(embed_weight.shape)
    embed = lax.all_gather(embed_own, GROUP, axis=1, tiled=True)
    read = w_read.reshape(w_read.shape[0], -1, depth).transpose(0, 2, 1).reshape(w_read.shape)
    mixing = jnp.dot(w_out, read, preferred_element_type=jnp.float32)
    mixing_high = mixing.astype(jnp.bfloat16)
    mixing_low = (mixing - mixing_high.astype(jnp.float32)).astype(jnp.bfloat16)
    mix = jnp.concatenate([mixing_high, mixing_low], axis=0)
    mix_t = jnp.concatenate([mixing_high.T, mixing_low.T], axis=0)
    proj_w = w_qkv.transpose(1, 0, 2).reshape(w_qkv.shape[1], -1)
    gain_row = layer_norm_gain[None, :]

    pick, place = slots(owners[0, 0, :, :, 0], tile_ids[0, 0], span_z // TILE)
    final_local, send = run_slab(field, material, conductivity[0], pick)
    got = swap(send, SPACE)
    chips = lax.axis_size(CHIPS)
    copies = jnp.dot(
        jnp.tile(place, (chips, 1)), got, preferred_element_type=jnp.float32
    ).astype(jnp.bfloat16)
    samples = swap(copies, CHIPS)
    tokens, targets = samples[:, :token_width], samples[:, token_width:]

    tokens_other = swap_cores(tokens)
    weights = (embed, gain_row, proj_w, mix, read)
    normed, proj, prob, pred, base = run_forward(tokens, *weights, own=True)
    normed_other, proj_other, prob_other, pred_other = run_forward(
        tokens_other, *weights, own=False
    )
    chip_pred = (pred + swap_cores(pred_other).astype(jnp.float32)).astype(jnp.bfloat16)
    shares = spread(chip_pred, CHIPS).astype(jnp.float32)
    row_count = lax.axis_size(GROUP) * SPD
    loss_scale = math.sqrt(w_read.shape[0] / (lax.axis_size(SPACE) * row_count * target_width))
    prediction = jnp.sum(shares, axis=0) + base
    delta = ((prediction - targets.astype(jnp.float32)) * loss_scale).astype(jnp.bfloat16)

    delta_other = swap_cores(delta)
    half = run_backward(delta, mix_t, proj, prob, normed, None)
    grads = run_backward(delta_other, mix_t, proj_other, prob_other, normed_other, half)

    weight_total = sum_over_space(grads)
    gain_share = (
        jnp.sum(w_qkv.astype(jnp.float32) * weight_total.astype(jnp.float32), axis=(0, 2))
        / layer_norm_gain
    )
    gain_total = jnp.sum(spread(gain_share, GROUP), axis=0)
    return (final_local[None], weight_total, gain_total)


def solution(mesh):
    halves, space, members = (mesh.shape[name] for name in ("grp", "space", "mem"))
    fine = Mesh(
        mesh.devices.reshape(halves, space // 4, 4, members // 2, 2),
        ("grp", "z", "x", "yhi", "core"),
    )
    placed = (
        P(MEM, SPACE, "grp", None),
        P(SPACE, "grp", None),
        P(MEM, None),
        P(MEM, "grp", None, None, None),
        P(MEM, "grp", None, None),
        P(None, GROUP),
        P(),
        P(None, None, GROUP),
        P(GROUP, None),
        P(),
    )
    return jax.shard_map(
        shards,
        mesh=fine,
        in_specs=placed,
        out_specs=(P(MEM, SPACE, "grp", None), P(None, None, GROUP), P()),
        check_vma=False,
    )
```

time: 278 us -> 257 us (0.924)
  matrix products: 28.1 us -> 1.26 us
  Pallas kernels: 0 us -> 25.6 us
  waiting for transfers between devices: 46.5 us -> 32 us
  other arithmetic: 22.6 us -> 10.9 us
  blocking collectives: 101 us -> 107 us
    pallas_call x0 -> x5, Pallas kernels: none -> 25.6 us  [the longest x2 10 us: run_forward(): pl.pallas_call(forward_kernel, grid=(rows // BLOCK_ROWS,), out_shape=tupl...]
    dot_general x12 -> x2, matrix products: 25.4 us -> 1.26 us  [the longest x1 0.88 us: shards(): mixing = jnp.dot(w_out, read, preferred_element_type=jnp.float32)]
    all_to_all x3 -> x2, waiting for transfers between devices: 44.2 us -> 29.5 us  [swap(): return lax.all_to_all(parts, axis, split_axis=0, concat_axis=0, tiled=True)]
    unnamed x23 -> x66, local copies, waits for them, and re-layouts: 2.3 us -> 13.2 us
    ppermute x3 -> x6, starting transfers between devices: 11.4 us -> 17.8 us  [the longest x3 6.4 us: swap_cores(): return lax.ppermute(own, 'core', [(0, 1), (1, 0)])]
    another operation x4 -> x1, local copies, waits for them, and re-layouts: 6.29 us -> 0.02 us  [shards(): jnp.tile(place, (chips, 1))]
    all_to_all x6, blocking collectives: 101 us -> 107 us  [swap(): return lax.all_to_all(parts, axis, split_axis=0, concat_axis=0, tiled=True)]
    another operation x1 -> x3, other arithmetic: 6.21 us -> 1.11 us  [the longest x2 1.03 us: run_slab(): block = jnp.stack([field, material.astype(jnp.float32)])]
  transfers between devices with their start and end apart: 7 -> 9, of which waited for: 5 -> 4; matrix products, arithmetic and copies ran while one was open for 9% -> 7% of each run, Pallas kernels for 0% -> 7%
where the time goes in v2:
time: 257 us; the launch traced here: 256 us
  blocking collectives  107 us (42%)
  starting transfers between devices  42.1 us (16%)
  waiting for transfers between devices  32 us (12%)
  Pallas kernels  25.6 us (10%)
  local copies, waits for them, and re-layouts  23 us (9%)
  between operations  14.6 us (6%)
  other arithmetic  10.9 us (4%)
    all_to_all x6, blocking collectives, swap(): return lax.all_to_all(parts, axis, split_axis=0, concat_axis=0, tiled=True)  107 us
    all_to_all x2, waiting for transfers between devices, swap(): return lax.all_to_all(parts, axis, split_axis=0, concat_axis=0, tiled=True)  29.5 us
    all_to_all x2, starting transfers between devices, swap(): return lax.all_to_all(parts, axis, split_axis=0, concat_axis=0, tiled=True)  24.2 us
    unnamed x66, local copies, waits for them, and re-layouts  13.2 us
    pallas_call x2, Pallas kernels, run_forward(): pl.pallas_call(forward_kernel, grid=(rows // BLOCK_ROWS,), out_shape=tupl...  10 us
    pallas_call x1, Pallas kernels, run_slab(): pl.pallas_call(functools.partial(slab_kernel, total_x=lax.axis_size(SPACE...  9.45 us
    ppermute x3, starting transfers between devices, swap_cores(): return lax.ppermute(own, 'core', [(0, 1), (1, 0)])  6.4 us
    pallas_call x2, Pallas kernels, run_backward(): pl.pallas_call(backward_kernel, grid=(rows // BLOCK_ROWS,), out_shape=out...  6.11 us
  transfers between devices with their start and end apart: 9, of which 4 were waited for; matrix products, arithmetic and copies ran while one was open for 7% of the time, Pallas kernels for 7%

profile of v2, /device:TPU:32, one launch (start us, length us, event | category | flops | bytes accessed | tf_op | source)
XLA Modules:
  0.0 256.2 jit_solution(8359755836219964197)
XLA Ops:
  7.3 1.0 convert_bitcast_fusion
  8.3 1.0 fusion.3
  9.3 3.5 %collective-permute-start = (f32[2,16,3,256]{3,2,1,0:T(4,128)S(1)}, f32[2,16,3,256]{3,2,1,0:T(4,128)S(1)}, u32[]{:S(2)}, u32[]{:S(2)}) collective-permute-start(f32[2,16,3,256]{3,2,1,0:T(4,128)S(1)} %fusion.3), channel_id=1, source_target_pairs={{0,256},{256,0},{1,257},{257,1},{2,258},{258,2},{3,259},{259,3},{4... | collective-permute-start | bytes 294920 | tf_op jit(solution)/shard_map/ppermute | solution.py:47
  12.8 1.1 copy.66
  14.0 0.8 copy.68
  14.8 2.6 %convert_reduce_fusion = s32[64,128]{1,0:T(8,128)S(1)} fusion(s32[64,128]{1,0:T(8,128)S(1)} %bitcast.66, pred[128,128]{1,0:T(8,128)(4,1)S(1)} %iota_compare_fusion.3), kind=kLoop, calls=%fused_computation | loop fusion | flops 4186112 | bytes 81920 | tf_op jit(solution)/shard_map/reduce_sum | solution.py:249
  17.9 3.4 %collective-permute-start.1 = (f32[2,3,22,256]{3,2,1,0:T(8,128)S(1)}, f32[2,3,22,256]{3,2,1,0:T(8,128)S(1)}, u32[]{:S(2)}, u32[]{:S(2)}) collective-permute-start(f32[2,3,22,256]{3,2,1,0:T(8,128)S(1)} %pad_maximum_fusion.1), channel_id=1, source_target_pairs={{0,4},{4,8},{8,12},{12,16},{16,20},{20,24},{24,28},{28,32},{32,36}... | collective-permute-start | bytes 405512 | tf_op jit(solution)/shard_map/ppermute | solution.py:53
  21.3 4.6 %collective-permute-start.2 = (f32[2,3,22,256]{3,2,1,0:T(8,128)S(1)}, f32[2,3,22,256]{3,2,1,0:T(8,128)S(1)}, u32[]{:S(2)}, u32[]{:S(2)}) collective-permute-start(f32[2,3,22,256]{3,2,1,0:T(8,128)S(1)} %fusion.1), channel_id=1, source_target_pairs={{4,0},{8,4},{12,8},{16,12},{20,16},{24,20},{28,24},{32,28},{36,32}... | collective-permute-start | bytes 405512 | tf_op jit(solution)/shard_map/ppermute | solution.py:54
  26.1 1.2 collective-permute-done.1.low_ref
  27.2 1.3 collective-permute-done.2.high_ref
  28.5 9.4 %slab.1 = (f32[16,16,256]{2,1,0:T(8,128)}, bf16[256,640]{1,0:T(8,128)(2,1)S(1)}) custom-call(s32[2]{0:T(128)S(1)} %pad_add_fusion.place_ref, f32[8]{0:T(128)S(1)} %bitcast.50, f32[16,16,256]{2,1,0:T(8,128)S(1)} %bitcast.49, s32[16,16,256]{2,1,0:T(8,128)S(1)} %copy-done.5, f32[2,16,3,256]{3,2,1,0:T(4,128)S(1)} %collective-permute-done.side_ref, ...), custom_call_target="tpu_custom_call" | custom-call | tf_op jit(solution)/shard_map/slab/pallas_call | solution.py:216
  38.0 0.8 all_to_all.35
  38.8 20.1 %all-to-all-start = ((bf16[64,4,640]{2,1,0:T(4,128)(2,1)}), bf16[64,4,640]{2,1,0:T(4,128)(2,1)S(1)}, u32[]{:S(2)}, u32[]{:S(2)}) async-start(bf16[64,4,640]{2,1,0:T(4,128)(2,1)} %all_to_all.35), calls=%async_computation | async-start | bytes 655360 | tf_op jit(solution)/shard_map/all_to_all | solution.py:32
  59.0 22.8 %all-to-all-done = bf16[64,4,640]{2,1,0:T(4,128)(2,1)S(1)} async-done(((bf16[64,4,640]{2,1,0:T(4,128)(2,1)}), bf16[64,4,640]{2,1,0:T(4,128)(2,1)S(1)}, u32[]{:S(2)}, u32[]{:S(2)}) %all-to-all-start) | async-done | bytes 327712 | tf_op jit(solution)/shard_map/all_to_all | solution.py:32
  82.3 12.5 %all_to_all.55 = bf16[4,128,640]{2,1,0:T(8,128)(2,1)S(1)} all-to-all(bf16[4,128,640]{2,1,0:T(8,128)(2,1)S(1)} %bitcast.58), channel_id=1, replica_groups=mesh['grp'=2,'z'=16,'x'=4,'yhi'=2,'core'=2] {'grp','yhi'}, dimensions={0} | all-to-all | bytes 1310720 | tf_op jit(solution)/shard_map/all_to_all | solution.py:32
  94.8 0.8 copy-done.24
  95.6 1.9 collective-permute-start.3
  97.9 0.9 copy.74.read_ref
  98.8 1.4 copy.69
  100.2 2.4 copy.73.proj_w_ref
  102.6 0.9 subtract_convert_fusion
  104.1 1.7 copy.72.embed_ref
  105.9 0.8 copy-done.20
  106.7 1.3 copy-done.3
  107.9 1.0 copy-done.12
  108.9 0.8 copy-done.18
  109.8 1.0 copy-done.21
  110.8 4.1 %forward_other.1 = (bf16[512,1536]{1,0:T(8,128)(2,1)S(1)}, bf16[512,384]{1,0:T(8,128)(2,1)S(1)}, f32[512,128]{1,0:T(8,128)S(1)}, bf16[512,128]{1,0:T(8,128)(2,1)S(1)}) custom-call(bf16[512,512]{1,0:T(8,128)(2,1)S(1)} %copy-done.21, bf16[512,1536]{1,0:T(8,128)(2,1)S(1)} %copy.72.embed_ref, f32[1,1536]{1,0:T(1,128)S(1)} %broadcast_in_dim.38.gain_ref, ...), custom_call_target="tpu_custom_call" | custom-call | flops 1409286144 | bytes 6291456 | tf_op jit(solution)/shard_map/forward_other/pallas_call | solution.py:325
  114.9 0.8 copy-done.8
  116.4 2.4 collective-permute-start.4
  118.8 5.9 %forward_own.1 = (bf16[512,1536]{1,0:T(8,128)(2,1)S(1)}, bf16[512,384]{1,0:T(8,128)(2,1)S(1)}, f32[512,128]{1,0:T(8,128)S(1)}, f32[512,128]{1,0:T(8,128)S(1)}, f32[512,128]{1,0:T(8,128)S(1)}) custom-call(bf16[512,512]{1,0:T(8,128)(2,1)S(1)} %copy-done.7, bf16[512,1536]{1,0:T(8,128)(2,1)} %copy-done.2, f32[1,1536]{1,0:T(1,128)S(1)} %broadcast_in_dim.38.gain_ref, ...), custom_call_target="tpu_custom_call" | custom-call | flops 1409286144 | bytes 6291456 | tf_op jit(solution)/shard_map/forward_own/pallas_call | solution.py:325
  124.8 0.7 copy-done.10
  127.0 0.9 broadcast_in_dim.39
  127.8 4.1 %all-to-all-start.2 = ((bf16[4,512,128]{2,1,0:T(8,128)(2,1)}), bf16[4,512,128]{2,1,0:T(8,128)(2,1)}, u32[]{:S(2)}, u32[]{:S(2)}) async-start(bf16[4,512,128]{2,1,0:T(8,128)(2,1)} %broadcast_in_dim.39), calls=%async_computation.2 | async-start | bytes 1048576 | tf_op jit(solution)/shard_map/all_to_all | solution.py:32
  132.0 1.6 copy.78
  133.6 1.5 fusion.9
  135.0 6.7 %all-to-all-done.2 = bf16[4,512,128]{2,1,0:T(8,128)(2,1)} async-done(((bf16[4,512,128]{2,1,0:T(8,128)(2,1)}), bf16[4,512,128]{2,1,0:T(8,128)(2,1)}, u32[]{:S(2)}, u32[]{:S(2)}) %all-to-all-start.2) | async-done | bytes 524320 | tf_op jit(solution)/shard_map/all_to_all | solution.py:32
  141.7 1.2 convert_reduce_fusion.1
  142.9 1.0 multiply_convert_fusion.delta_ref
  144.0 2.1 collective-permute-start.5
  146.2 3.1 %backward_own.1.rest_0_ = f32[1536,384]{1,0:T(8,128)S(1)} custom-call(bf16[512,128]{1,0:T(8,128)(2,1)S(1)} %multiply_convert_fusion.delta_ref, bf16[256,128]{1,0:T(8,128)(2,1)S(1)} %pad_maximum_fusion.3.mix_t_ref, bf16[512,384]{1,0:T(8,128)(2,1)S(1)} %copy-done.11, f32[512,128]{1,0:T(8,128)S(1)} %copy-done.16, bf16[512,1536]{1,0:T(8,128)(2,1)S(1)} %get-tuple-element.25.normed_ref), custom_call_target="tpu_custom_call" | custom-call | flops 603979776 | bytes 3145728 | tf_op jit(solution)/shard_map/backward_own/pallas_call | solution.py:405
  149.3 3.0 %backward_other.1 = bf16[3,1536,128]{2,1,0:T(8,128)(2,1)S(1)} custom-call(bf16[512,128]{1,0:T(8,128)(2,1)S(1)} %collective-permute-done.5.delta_ref, bf16[256,128]{1,0:T(8,128)(2,1)S(1)} %pad_maximum_fusion.3.mix_t_ref, bf16[512,384]{1,0:T(8,128)(2,1)S(1)} %copy-done.9, f32[512,128]{1,0:T(8,128)S(1)} %copy-done.14, ...), custom_call_target="tpu_custom_call" | custom-call | flops 603979776 | bytes 3145728 | tf_op jit(solution)/shard_map/backward_other/pallas_call | solution.py:405
  152.3 20.0 %all_to_all.56 = bf16[4,1152,128]{2,1,0:T(8,128)(2,1)S(1)} all-to-all(bf16[4,1152,128]{2,1,0:T(8,128)(2,1)S(1)} %bitcast.48), channel_id=1, replica_groups=mesh['grp'=2,'z'=16,'x'=4,'yhi'=2,'core'=2] {'x'}, dimensions={0} | all-to-all | bytes 2359296 | tf_op jit(solution)/shard_map/all_to_all | solution.py:32
  172.7 22.7 %all_to_all.57 = bf16[16,72,128]{2,1,0:T(8,128)(2,1)S(1)} all-to-all(bf16[16,72,128]{2,1,0:T(8,128)(2,1)S(1)} %bitcast.60), channel_id=1, replica_groups=mesh['grp'=2,'z'=16,'x'=4,'yhi'=2,'core'=2] {'z'}, dimensions={0} | all-to-all | bytes 589824 | tf_op jit(solution)/shard_map/all_to_all | solution.py:32
  195.4 25.0 %all_to_all.58 = bf16[16,72,128]{2,1,0:T(8,128)(2,1)S(1)} all-to-all(bf16[16,72,128]{2,1,0:T(8,128)(2,1)S(1)} %broadcast_in_dim.66), channel_id=1, replica_groups=mesh['grp'=2,'z'=16,'x'=4,'yhi'=2,'core'=2] {'z'}, dimensions={0} | all-to-all | bytes 589824 | tf_op jit(solution)/shard_map/all_to_all | solution.py:32
  220.6 18.7 %all_to_all.59 = bf16[4,1152,128]{2,1,0:T(8,128)(2,1)S(1)} all-to-all(bf16[4,1152,128]{2,1,0:T(8,128)(2,1)S(1)} %broadcast_in_dim.68), channel_id=1, replica_groups=mesh['grp'=2,'z'=16,'x'=4,'yhi'=2,'core'=2] {'x'}, dimensions={0} | all-to-all | bytes 2359296 | tf_op jit(solution)/shard_map/all_to_all | solution.py:32
  239.7 8.0 %all_to_all.60 = f32[8,1,1536]{2,1,0:T(1,128)S(1)} all-to-all(f32[8,1,1536]{2,1,0:T(1,128)S(1)} %broadcast_in_dim.69), channel_id=1, replica_groups=mesh['grp'=2,'z'=16,'x'=4,'yhi'=2,'core'=2] {'grp','yhi','core'}, dimensions={0} | all-to-all | bytes 98304 | tf_op jit(solution)/shard_map/all_to_all | solution.py:32
  248.4 1.0 copy.82
  (95 shorter events, 6.2 us)
Async XLA Ops:
  7.2 95.4 %copy-start = (bf16[128,1536]{1,0:T(8,128)(2,1)S(1)}, bf16[128,1536]{1,0:T(8,128)(2,1)}, u32[]{:S(2)}) copy-start(bf16[128,1536]{1,0:T(8,128)(2,1)} %param.20) | copy-start | bytes 1179652
  7.2 7.6 %copy-start.26 = (s32[1,1,64,128,1]{3,4,2,1,0:T(1,128)S(1)}, s32[1,1,64,128,1]{3,4,2,1,0:T(1,128)}, u32[]{:S(2)}) copy-start(s32[1,1,64,128,1]{3,4,2,1,0:T(1,128)} %param.15) | copy-start | bytes 98308
  7.2 10.2 %copy-start.30 = (s32[1,1,64,128]{3,2,1,0:T(8,128)S(1)}, s32[1,1,64,128]{3,2,1,0:T(8,128)}, u32[]{:S(2)}) copy-start(s32[1,1,64,128]{3,2,1,0:T(8,128)} %param.16) | copy-start | bytes 98308
  7.2 96.9 %all-gather.2.cloned.1.call-start = ((), (), s32[]{:S(2)}) async-start(), calls=%async_computation.8 | async-start | bytes 1769472 | tf_op jit(solution)/shard_map/all_gather | solution.py:451
  7.3 10.6 %copy-start.1 = (f32[1,16,16,256]{3,2,1,0:T(8,128)S(1)}, f32[1,16,16,256]{3,2,1,0:T(8,128)}, u32[]{:S(2)}) copy-start(f32[1,16,16,256]{3,2,1,0:T(8,128)} %param.12) | copy-start | bytes 786436
  9.3 8.5 %collective-permute-start = (f32[2,16,3,256]{3,2,1,0:T(4,128)S(1)}, f32[2,16,3,256]{3,2,1,0:T(4,128)S(1)}, u32[]{:S(2)}, u32[]{:S(2)}) collective-permute-start(f32[2,16,3,256]{3,2,1,0:T(4,128)S(1)} %fusion.3), channel_id=1, source_target_pairs={{0,256},{256,0},{1,257},{257,1},{2,258},{258,2},{3,259},{259,3},{4... | collective-permute-start | bytes 294920 | tf_op jit(solution)/shard_map/ppermute | solution.py:47
  13.9 14.7 %copy-start.5 = (s32[16,16,256]{2,1,0:T(8,128)S(1)}, s32[16,16,256]{2,1,0:T(8,128)}, u32[]{:S(2)}) copy-start(s32[16,16,256]{2,1,0:T(8,128)} %material_ref.1) | copy-start | bytes 786436
  13.9 14.7 %copy-start.19 = (f32[1,8]{1,0:T(1,128)S(1)}, f32[1,8]{1,0:T(1,128)}, u32[]{:S(2)}) copy-start(f32[1,8]{1,0:T(1,128)} %param.14) | copy-start | bytes 100
  17.9 9.3 %collective-permute-start.1 = (f32[2,3,22,256]{3,2,1,0:T(8,128)S(1)}, f32[2,3,22,256]{3,2,1,0:T(8,128)S(1)}, u32[]{:S(2)}, u32[]{:S(2)}) collective-permute-start(f32[2,3,22,256]{3,2,1,0:T(8,128)S(1)} %pad_maximum_fusion.1), channel_id=1, source_target_pairs={{0,4},{4,8},{8,12},{12,16},{16,20},{20,24},{24,28},{28,32},{32,36}... | collective-permute-start | bytes 405512 | tf_op jit(solution)/shard_map/ppermute | solution.py:53
  21.3 7.2 %collective-permute-start.2 = (f32[2,3,22,256]{3,2,1,0:T(8,128)S(1)}, f32[2,3,22,256]{3,2,1,0:T(8,128)S(1)}, u32[]{:S(2)}, u32[]{:S(2)}) collective-permute-start(f32[2,3,22,256]{3,2,1,0:T(8,128)S(1)} %fusion.1), channel_id=1, source_target_pairs={{4,0},{8,4},{12,8},{16,12},{20,16},{24,20},{28,24},{32,28},{36,32}... | collective-permute-start | bytes 405512 | tf_op jit(solution)/shard_map/ppermute | solution.py:54
  38.8 43.0 %all-to-all-start = ((bf16[64,4,640]{2,1,0:T(4,128)(2,1)}), bf16[64,4,640]{2,1,0:T(4,128)(2,1)S(1)}, u32[]{:S(2)}, u32[]{:S(2)}) async-start(bf16[64,4,640]{2,1,0:T(4,128)(2,1)} %all_to_all.35), calls=%async_computation | async-start | bytes 655360 | tf_op jit(solution)/shard_map/all_to_all | solution.py:32
  81.9 15.6 %copy-start.29 = (f32[1536]{0:T(1024)S(1)}, f32[1536]{0:T(1024)}, u32[]{:S(2)}) copy-start(f32[1536]{0:T(1024)} %param.18) | copy-start | bytes 18436
  81.9 15.6 %copy-start.25 = (bf16[1536,128]{1,0:T(8,128)(2,1)S(1)}, bf16[1536,128]{1,0:T(8,128)(2,1)}, u32[]{:S(2)}) copy-start(bf16[1536,128]{1,0:T(8,128)(2,1)} %param.21) | copy-start | bytes 1179652
  94.8 0.9 copy-start.24
  94.8 4.1 %copy-start.22 = (bf16[3,1536,128]{2,1,0:T(8,128)(2,1)S(1)}, bf16[3,1536,128]{2,1,0:T(8,128)(2,1)}, u32[]{:S(2)}) copy-start(bf16[3,1536,128]{2,1,0:T(8,128)(2,1)} %param.19) | copy-start | bytes 3538948
  95.6 4.6 %copy-start.6 = (bf16[512,512]{1,0:T(8,128)(2,1)}, bf16[512,512]{1,0:T(8,128)(2,1)S(1)}, u32[]{:S(2)}) copy-start(bf16[512,512]{1,0:T(8,128)(2,1)S(1)} %slice.49.token_ref) | copy-start | bytes 1572868
  95.6 10.2 %collective-permute-start.3 = (bf16[512,512]{1,0:T(8,128)(2,1)S(1)}, bf16[512,512]{1,0:T(8,128)(2,1)S(1)}, u32[]{:S(2)}, u32[]{:S(2)}) collective-permute-start(bf16[512,512]{1,0:T(8,128)(2,1)S(1)} %slice.49.token_ref), channel_id=1, source_target_pairs={{0,1},{1,0},{2,3},{3,2},{4,5},{5,4},{6,7},{7,6},{8,9},{9,8},{10,11... | collective-permute-start | bytes 1572872 | tf_op jit(solution)/shard_map/ppermute | solution.py:41
  105.8 9.1 %copy-start.2 = (bf16[512,1536]{1,0:T(8,128)(2,1)}, bf16[512,1536]{1,0:T(8,128)(2,1)S(1)}, u32[]{:S(2)}) copy-start(bf16[512,1536]{1,0:T(8,128)(2,1)S(1)} %copy.72.embed_ref) | copy-start | bytes 4718596
  105.8 0.8 copy-start.20
  106.7 1.3 copy-start.3
  107.9 1.0 copy-start.12
  108.9 0.8 copy-start.18
  109.8 1.0 copy-start.21
  110.8 8.0 %copy-start.4 = (bf16[1536,384]{1,0:T(8,128)(2,1)S(1)}, bf16[1536,384]{1,0:T(8,128)(2,1)}, u32[]{:S(2)}) copy-start(bf16[1536,384]{1,0:T(8,128)(2,1)} %copy.73.proj_w_ref) | copy-start | bytes 3538948
  110.8 8.0 %copy-start.7 = (bf16[512,512]{1,0:T(8,128)(2,1)S(1)}, bf16[512,512]{1,0:T(8,128)(2,1)}, u32[]{:S(2)}) copy-start(bf16[512,512]{1,0:T(8,128)(2,1)} %copy-done.6) | copy-start | bytes 1572868
  114.9 0.8 copy-start.8
  115.7 0.7 copy-start.13
  116.4 10.6 %collective-permute-start.4 = (bf16[512,128]{1,0:T(8,128)(2,1)S(1)}, bf16[512,128]{1,0:T(8,128)(2,1)S(1)}, u32[]{:S(2)}, u32[]{:S(2)}) collective-permute-start(bf16[512,128]{1,0:T(8,128)(2,1)S(1)} %get-tuple-element.18), channel_id=1, source_target_pairs={{0,1},{1,0},{2,3},{3,2},{4,5},{5,4},{6,7},{7,6},{8,9},{9,8},{10,11... | collective-permute-start | bytes 393224 | tf_op jit(solution)/shard_map/ppermute | solution.py:41
  124.8 0.8 copy-start.10
  125.5 0.7 copy-start.15
  126.2 0.7 copy-start.17
  127.8 13.9 %all-to-all-start.2 = ((bf16[4,512,128]{2,1,0:T(8,128)(2,1)}), bf16[4,512,128]{2,1,0:T(8,128)(2,1)}, u32[]{:S(2)}, u32[]{:S(2)}) async-start(bf16[4,512,128]{2,1,0:T(8,128)(2,1)} %broadcast_in_dim.39), calls=%async_computation.2 | async-start | bytes 1048576 | tf_op jit(solution)/shard_map/all_to_all | solution.py:32
  141.7 4.4 %copy-start.27 = (bf16[128,128]{1,0:T(8,128)(2,1)S(1)}, bf16[128,128]{1,0:T(8,128)(2,1)}, u32[]{:S(2)}) copy-start(bf16[128,128]{1,0:T(8,128)(2,1)} %get-tuple-element.37) | copy-start | bytes 98308
  141.7 4.4 %copy-start.28 = (bf16[128,128]{1,0:T(8,128)(2,1)S(1)}, bf16[128,128]{1,0:T(8,128)(2,1)}, u32[]{:S(2)}) copy-start(bf16[128,128]{1,0:T(8,128)(2,1)} %get-tuple-element.38) | copy-start | bytes 98308
  141.7 4.4 %copy-start.11 = (bf16[512,384]{1,0:T(8,128)(2,1)S(1)}, bf16[512,384]{1,0:T(8,128)(2,1)}, u32[]{:S(2)}) copy-start(bf16[512,384]{1,0:T(8,128)(2,1)} %copy-done.10) | copy-start | bytes 1179652
  141.7 4.4 %copy-start.16 = (f32[512,128]{1,0:T(8,128)S(1)}, f32[512,128]{1,0:T(8,128)}, u32[]{:S(2)}) copy-start(f32[512,128]{1,0:T(8,128)} %copy-done.15) | copy-start | bytes 786436
  144.0 5.3 %collective-permute-start.5 = (bf16[512,128]{1,0:T(8,128)(2,1)S(1)}, bf16[512,128]{1,0:T(8,128)(2,1)S(1)}, u32[]{:S(2)}, u32[]{:S(2)}) collective-permute-start(bf16[512,128]{1,0:T(8,128)(2,1)S(1)} %multiply_convert_fusion.delta_ref), channel_id=1, source_target_pairs={{0,1},{1,0},{2,3},{3,2},{4,5},{5,4},{6,7},{7,6},{8,9},{9,8},{10,11... | collective-permute-start | bytes 393224 | tf_op jit(solution)/shard_map/ppermute | solution.py:41
  146.1 3.1 %copy-start.9 = (bf16[512,384]{1,0:T(8,128)(2,1)S(1)}, bf16[512,384]{1,0:T(8,128)(2,1)}, u32[]{:S(2)}) copy-start(bf16[512,384]{1,0:T(8,128)(2,1)} %copy-done.8) | copy-start | bytes 1179652
  146.1 3.1 %copy-start.14 = (f32[512,128]{1,0:T(8,128)S(1)}, f32[512,128]{1,0:T(8,128)}, u32[]{:S(2)}) copy-start(f32[512,128]{1,0:T(8,128)} %copy-done.13) | copy-start | bytes 786436
  220.4 18.9 %copy-start.23 = (bf16[3,1536,128]{2,1,0:T(8,128)(2,1)S(1)}, bf16[3,1536,128]{2,1,0:T(8,128)(2,1)}, u32[]{:S(2)}) copy-start(bf16[3,1536,128]{2,1,0:T(8,128)(2,1)} %param.19) | copy-start | bytes 3538948
Sparse Core Ops, SparseCore 0:
  14.9 46.6 all-gather.1

commit v3 on v2

--- a/solution.py
+++ b/solution.py
@@ -20,11 +20,11 @@
 GROUP = ("grp", "yhi", "core")
 CHIPS = ("grp", "yhi")
 
-PAD = 8
+PAD = 4
 BLOCK_ROWS = 256
 VMEM = pl.BlockSpec(memory_space=pltpu.VMEM)
 SMEM = pl.BlockSpec(memory_space=pltpu.SMEM)
-LIMIT = 48 * 1024 * 1024
+LIMIT = 20 * 1024 * 1024
 EXACT = lax.Precision.HIGHEST
 
 
@@ -37,14 +37,19 @@
     return swap(jnp.broadcast_to(own[None], (count,) + own.shape), axis)
 
 
+def swap_with(own, axis):
+    return lax.ppermute(own, axis, [(0, 1), (1, 0)])
+
+
 def swap_cores(own):
-    return lax.ppermute(own, "core", [(0, 1), (1, 0)])
-
-
-def halos(block, width):
+    return swap_with(own, "core")
+
+
+def halos(block, width, beside):
     half = lax.axis_index("grp")
     face = jnp.where(half == 0, block[:, :, -width:], block[:, :, :width])
-    side = lax.ppermute(face, "grp", [(0, 1), (1, 0)])
+    side = swap_with(face, "grp")
+    side, beside = lax.optimization_barrier((side, beside))
     count = lax.axis_size(SPACE)
     forward = [(i, i + 1) for i in range(count - 1)]
     backward = [(i + 1, i) for i in range(count - 1)]
@@ -52,7 +57,18 @@
     bottom = jnp.concatenate([side[:, :width], block[:, :width], side[:, :width]], axis=2)
     low = lax.ppermute(top, SPACE, forward)
     high = lax.ppermute(bottom, SPACE, backward)
-    return side, low, high
+    return side, low, high, beside
+
+
+def over(first, last, body):
+    def turn(i, _):
+        body(first + 2 * i)
+        body(first + 2 * i + 1)
+        return 0
+
+    lax.fori_loop(0, (last - first) // 2, turn, 0)
+    if (last - first) % 2:
+        body(last - 1)
 
 
 def slab_kernel(
@@ -108,7 +124,7 @@
         in_x = ((at >= 0) & (at < total_x)).astype(jnp.int32)
         return inside_y & (jnp.full((rows, span_z), in_x) > 0)
 
-    def set_cond(plane, _):
+    def set_cond(plane):
         kind = cond[plane]
         value = jnp.zeros_like(kind)
         for level in range(table_ref.shape[0]):
@@ -116,11 +132,10 @@
         keep = inside(plane)
         cond[plane] = jnp.where(keep, value, 0.0)
         field_a[plane] = jnp.where(keep, field_a[plane], 0.0)
-        return 0
-
-    lax.fori_loop(0, planes, set_cond, 0)
-
-    def set_coef(plane, _):
+
+    over(0, planes, set_cond)
+
+    def set_coef(plane):
         mine = 0.5 * cond[plane]
         keep = inside(plane)
         ups = mine + pltpu.roll(mine, 1, 0)
@@ -137,12 +152,11 @@
         coef[4, plane] = jnp.where(keep, downs, 0.0)
         coef[5, plane] = jnp.where(keep & ~first_z, before, 0.0)
         coef[6, plane] = jnp.where(keep & ~last_z, after, 0.0)
-        return 0
-
-    lax.fori_loop(1, planes - 1, set_coef, 0)
+
+    over(1, planes - 1, set_coef)
 
     def step(source, target):
-        def one(plane, _):
+        def one(plane):
             mid = source[plane]
             value = coef[0, plane] * mid
             value = value + coef[1, plane] * source[plane - 1]
@@ -152,13 +166,12 @@
             value = value + coef[5, plane] * pltpu.roll(mid, 1, 1)
             value = value + coef[6, plane] * pltpu.roll(mid, span_z - 1, 1)
             target[plane] = value
-            return 0
 
         return one
 
     for number in range(STEPS):
         source, target = (field_a, field_b) if number % 2 == 0 else (field_b, field_a)
-        lax.fori_loop(1 + number, planes - 1 - number, step(source, target), 0)
+        over(1 + number, planes - 1 - number, step(source, target))
 
     before_last, last = (field_a, field_b) if STEPS % 2 == 1 else (field_b, field_a)
     final_ref[...] = last[own_x, own_y, :]
@@ -192,9 +205,8 @@
     fine_rows, rough_rows = fine.shape[0], rough.shape[0]
     for k in range(depth):
         cut = slice(tiles * k, tiles * (k + 1))
-        rows_t[fine_rows * k : fine_rows * (k + 1), :] = fine[:, cut]
-        start = fine_rows * depth + rough_rows * k
-        rows_t[start : start + rough_rows, :] = rough[:, cut]
+        rows_t[pl.ds(k, fine_rows, stride=depth), :] = fine[:, cut]
+        rows_t[pl.ds(fine_rows * depth + k, rough_rows, stride=depth), :] = rough[:, cut]
     send_ref[...] = lax.dot_general(
         pick_ref[...],
         rows_t[...].astype(jnp.bfloat16),
@@ -203,17 +215,19 @@
     ).astype(jnp.bfloat16)
 
 
-def run_slab(field, material, table, pick):
+def run_slab(field, material, table, owner_list, tile_list, embed_own):
     span_x, span_y, span_z = field.shape
     width = STEPS
     block = jnp.stack([field, material.astype(jnp.float32)])
-    side, low, high = halos(block, width)
-    place = jnp.stack([lax.axis_index(SPACE), lax.axis_index("grp")]).astype(jnp.int32)
+    side, low, high, (owner_list, embed_own) = halos(block, width, (owner_list, embed_own))
+    embed = jnp.stack([embed_own, swap_with(embed_own, "yhi")])
+    pick, place = slots(owner_list, tile_list, span_z // TILE)
+    origin = jnp.stack([lax.axis_index(SPACE), lax.axis_index("grp")]).astype(jnp.int32)
     planes, rows = span_x + 2 * width, span_y + 2 * PAD
     tiles = span_z // TILE
     values = (span_x * span_y // 4 + span_x * span_y // 16) * TILE // 2
     extended = pltpu.VMEM((planes, rows, span_z), jnp.float32)
-    return pl.pallas_call(
+    final, send = pl.pallas_call(
         functools.partial(
             slab_kernel,
             total_x=lax.axis_size(SPACE) * span_x,
@@ -236,7 +250,8 @@
         ],
         compiler_params=pltpu.CompilerParams(vmem_limit_bytes=LIMIT),
         name="slab",
-    )(place, table, field, material, side, low, high, pick)
+    )(origin, table, field, material, side, low, high, pick)
+    return final, send, place, embed
 
 
 def slots(owner_list, tile_list, tile_count):
@@ -261,12 +276,18 @@
     return pick, place
 
 
+def mixing_parts(out_ref, read_ref):
+    mixing = jnp.dot(out_ref[...], read_ref[...], preferred_element_type=jnp.float32)
+    high = mixing.astype(jnp.bfloat16)
+    return high, (mixing - high.astype(jnp.float32)).astype(jnp.bfloat16)
+
+
 def forward_kernel(
-    token_ref, embed_ref, gain_ref, proj_w_ref, mix_ref, read_ref,
+    sample_ref, embed_ref, gain_ref, proj_w_ref, out_ref, read_ref,
     normed_ref, proj_ref, prob_ref, pred_ref, *base_ref,
 ):
     embedded = jnp.dot(
-        token_ref[...], embed_ref[...], preferred_element_type=jnp.float32
+        sample_ref[:, : embed_ref.shape[0]], embed_ref[...], preferred_element_type=jnp.float32
     ).astype(jnp.bfloat16)
     wide = embedded.astype(jnp.float32)
     mean = jnp.mean(wide, axis=1, keepdims=True)
@@ -274,10 +295,11 @@
     variance = jnp.mean(removed * removed, axis=1, keepdims=True)
     normed = (removed * lax.rsqrt(variance + NORM_EPSILON) * gain_ref[...]).astype(jnp.bfloat16)
     normed_ref[...] = normed
-    proj = jnp.dot(normed, proj_w_ref[...], preferred_element_type=jnp.float32).astype(jnp.bfloat16)
+    proj_w = jnp.concatenate([proj_w_ref[i] for i in range(3)], axis=1)
+    proj = jnp.dot(normed, proj_w, preferred_element_type=jnp.float32).astype(jnp.bfloat16)
     proj_ref[...] = proj
     attended = []
-    for seq in range(token_ref.shape[0] // SPD):
+    for seq in range(sample_ref.shape[0] // SPD):
         rows = slice(seq * SPD, (seq + 1) * SPD)
         query, key, value = (proj[rows, i * HD : (i + 1) * HD] for i in range(3))
         scores = lax.dot_general(
@@ -292,63 +314,90 @@
             ).astype(jnp.bfloat16)
         )
     attended = jnp.concatenate(attended, axis=0)
+    high, low = mixing_parts(out_ref, read_ref)
     pred_ref[...] = jnp.dot(
         jnp.concatenate([attended, attended], axis=1),
-        mix_ref[...],
+        jnp.concatenate([high, low], axis=0),
         preferred_element_type=jnp.float32,
     ).astype(pred_ref.dtype)
     if base_ref:
-        base_ref[0][...] = jnp.dot(embedded, read_ref[...], preferred_element_type=jnp.float32)
+        targets = sample_ref[:, embed_ref.shape[0] :].astype(jnp.float32)
+        base_ref[0][...] = (
+            jnp.dot(embedded, read_ref[...], preferred_element_type=jnp.float32) - targets
+        )
 
 
 def whole(array):
-    return pl.BlockSpec(array.shape, lambda i: (0,) * array.ndim)
+    return pl.BlockSpec(
+        array.shape, lambda i: (0,) * array.ndim, pipeline_mode=pl.Buffered(buffer_count=1)
+    )
 
 
 def by_rows(columns):
     return pl.BlockSpec((BLOCK_ROWS, columns), lambda i: (i, 0))
 
 
-def run_forward(tokens, embed, gain, proj_w, mix, read, own):
-    rows, token_width = tokens.shape
-    model, heads = proj_w.shape
-    out_width = read.shape[1]
+def run_forward(samples, embed, gain, w_qkv, w_out, w_read, own):
+    rows, sample_width = samples.shape
+    kinds, model, head = w_qkv.shape
+    out_width = w_read.shape[1]
     shapes = [
         jax.ShapeDtypeStruct((rows, model), jnp.bfloat16),
-        jax.ShapeDtypeStruct((rows, heads), jnp.bfloat16),
+        jax.ShapeDtypeStruct((rows, kinds * head), jnp.bfloat16),
         jax.ShapeDtypeStruct((rows, SPD), jnp.float32),
         jax.ShapeDtypeStruct((rows, out_width), jnp.float32 if own else jnp.bfloat16),
     ]
     if own:
         shapes.append(jax.ShapeDtypeStruct((rows, out_width), jnp.float32))
-    flops = 2 * rows * model * (token_width + heads)
+    weights = (embed, gain, w_qkv, w_out, w_read)
     return pl.pallas_call(
         forward_kernel,
         grid=(rows // BLOCK_ROWS,),
         out_shape=tuple(shapes),
-        in_specs=[by_rows(token_width)]
-        + [whole(array) for array in (embed, gain, proj_w, mix, read)],
+        in_specs=[by_rows(sample_width)] + [whole(array) for array in weights],
         out_specs=tuple(by_rows(shape.shape[1]) for shape in shapes),
         compiler_params=pltpu.CompilerParams(vmem_limit_bytes=LIMIT),
         cost_estimate=pl.CostEstimate(
-            flops=flops, bytes_accessed=rows * model * 8, transcendentals=rows * SPD
+            flops=2 * rows * model * (embed.shape[0] + kinds * head),
+            bytes_accessed=rows * model * 8,
+            transcendentals=rows * SPD,
         ),
         name="forward_own" if own else "forward_other",
-    )(tokens, embed, gain, proj_w, mix, read)
-
-
-def backward_kernel(delta_ref, mix_t_ref, proj_ref, prob_ref, normed_ref, *rest):
+    )(samples, *weights)
+
+
+def delta_kernel(share_ref, base_ref, delta_ref, *, scale):
+    total = base_ref[...]
+    for i in range(share_ref.shape[0]):
+        total = total + share_ref[i].astype(jnp.float32)
+    delta_ref[...] = (total * scale).astype(delta_ref.dtype)
+
+
+def run_delta(shares, base, scale):
+    return pl.pallas_call(
+        functools.partial(delta_kernel, scale=scale),
+        out_shape=jax.ShapeDtypeStruct(base.shape, jnp.bfloat16),
+        in_specs=[VMEM, VMEM],
+        out_specs=VMEM,
+        compiler_params=pltpu.CompilerParams(vmem_limit_bytes=LIMIT),
+        name="delta",
+    )(shares, base)
+
+
+def backward_kernel(delta_ref, out_ref, read_ref, proj_ref, prob_ref, normed_ref, *rest):
     start_ref = rest[0] if len(rest) == 3 else None
-    out_ref, total = rest[-2], rest[-1]
+    grad_ref, total = rest[-2], rest[-1]
     step = pl.program_id(0)
+    across = (((1,), (1,)), ((), ()))
+    down = (((0,), (0,)), ((), ()))
     delta = delta_ref[...]
-    grad_attended = jnp.dot(
+    high, low = mixing_parts(out_ref, read_ref)
+    grad_attended = lax.dot_general(
         jnp.concatenate([delta, delta], axis=1),
-        mix_t_ref[...],
+        jnp.concatenate([high, low], axis=1),
+        across,
         preferred_element_type=jnp.float32,
     ).astype(jnp.bfloat16)
-    across = (((1,), (1,)), ((), ()))
-    down = (((0,), (0,)), ((), ()))
     grads = []
     for seq in range(delta_ref.shape[0] // SPD):
         rows = slice(seq * SPD, (seq + 1) * SPD)
@@ -382,22 +431,23 @@
     @pl.when(step == pl.num_programs(0) - 1)
     def _():
         if start_ref is None:
-            out_ref[...] = total[...]
+            grad_ref[...] = total[...]
         else:
-            for i in range(out_ref.shape[0]):
-                out_ref[i] = total[:, i * HD : (i + 1) * HD].astype(out_ref.dtype)
-
-
-def run_backward(delta, mix_t, proj, prob, normed, start):
+            for i in range(grad_ref.shape[0]):
+                grad_ref[i] = total[:, i * HD : (i + 1) * HD].astype(grad_ref.dtype)
+
+
+def run_backward(delta, w_out, w_read, proj, prob, normed, start):
     rows, model = normed.shape
     heads = proj.shape[1]
     if start is None:
         out = jax.ShapeDtypeStruct((model, heads), jnp.float32)
     else:
         out = jax.ShapeDtypeStruct((heads // HD, model, HD), jnp.bfloat16)
-    operands = [delta, mix_t, proj, prob, normed]
+    operands = [delta, w_out, w_read, proj, prob, normed]
     specs = [
-        by_rows(delta.shape[1]), whole(mix_t), by_rows(heads), by_rows(SPD), by_rows(model),
+        by_rows(delta.shape[1]), whole(w_out), whole(w_read),
+        by_rows(heads), by_rows(SPD), by_rows(model),
     ]
     if start is not None:
         operands.append(start)
@@ -417,15 +467,47 @@
     )(*operands)
 
 
-def sum_over_space(parts):
+def split(values, rows):
+    columns = 128
+    high = values.astype(jnp.bfloat16)
+    low = (values - high.astype(jnp.float32)).astype(jnp.bfloat16)
+    both = jnp.stack([high, low], axis=-2)
+    both = both.reshape(both.shape[:-2] + (-1, min(columns, both.shape[-1])))
+    pad = [(0, 0)] * (both.ndim - 2)
+    return jnp.pad(both, pad + [(0, rows - both.shape[-2]), (0, columns - both.shape[-1])])
+
+
+def sum_over_devices(parts, gain):
     count_x, count_z = lax.axis_size("x"), lax.axis_size("z")
-    shape, columns = parts.shape, parts.shape[-1]
-    parts = parts.reshape(count_x, -1, columns)
-    part = jnp.sum(swap(parts, "x").astype(jnp.float32), axis=0)
-    parts = part.astype(jnp.bfloat16).reshape(count_z, -1, columns)
-    total = jnp.sum(swap(parts, "z").astype(jnp.float32), axis=0).astype(jnp.bfloat16)
-    gathered = spread(total, "z").reshape(-1, columns)
-    return spread(gathered, "x").reshape(shape)
+    shape, columns, width = parts.shape, parts.shape[-1], gain.shape[0]
+    chunk = width // count_z
+    spare = 8
+
+    part = jnp.sum(swap(parts.reshape(count_x, -1, columns), "x").astype(jnp.float32), axis=0)
+    for axis in ("core", "grp", "yhi"):
+        gain = gain + swap_with(gain, axis)
+
+    sent = jnp.concatenate(
+        [
+            part.astype(jnp.bfloat16).reshape(count_z, -1, columns),
+            split(gain.reshape(count_z, chunk), spare),
+        ],
+        axis=1,
+    )
+    total = jnp.sum(swap(sent, "z").astype(jnp.float32), axis=0)
+    rows = total.shape[0] - spare
+    own_gain = total[rows, :chunk] + total[rows + 1, :chunk]
+    sent = jnp.concatenate([total[:rows].astype(jnp.bfloat16), split(own_gain, spare)], axis=0)
+    got = spread(sent, "z").reshape(count_z, -1, columns)
+    gain = (
+        got[:, rows, :chunk].astype(jnp.float32) + got[:, rows + 1, :chunk].astype(jnp.float32)
+    ).reshape(width)
+    gain_rows = 2 * width // columns
+    sent = jnp.concatenate([got[:, :rows].reshape(-1, columns), split(gain, gain_rows)], axis=0)
+    got = spread(sent, "x").reshape(count_x, -1, columns)
+    gain = jnp.sum(got[:, -gain_rows:].astype(jnp.float32), axis=0)
+    gain = (gain[: gain_rows // 2] + gain[gain_rows // 2 :]).reshape(width)
+    return got[:, :-gain_rows].reshape(shape), gain
 
 
 def shards(
@@ -440,57 +522,55 @@
     w_out,
     w_read,
 ):
-    field = start_field[0]
-    span_x, span_y, span_z = field.shape
-    depth = TILE // 2
-    token_width = embed_weight.shape[0]
-    target_width = w_read.shape[1]
-
-    embed_own = embed_weight.reshape(-1, depth, embed_weight.shape[1])
-    embed_own = embed_own.transpose(1, 0, 2).reshape(embed_weight.shape)
-    embed = lax.all_gather(embed_own, GROUP, axis=1, tiled=True)
-    read = w_read.reshape(w_read.shape[0], -1, depth).transpose(0, 2, 1).reshape(w_read.shape)
-    mixing = jnp.dot(w_out, read, preferred_element_type=jnp.float32)
-    mixing_high = mixing.astype(jnp.bfloat16)
-    mixing_low = (mixing - mixing_high.astype(jnp.float32)).astype(jnp.bfloat16)
-    mix = jnp.concatenate([mixing_high, mixing_low], axis=0)
-    mix_t = jnp.concatenate([mixing_high.T, mixing_low.T], axis=0)
-    proj_w = w_qkv.transpose(1, 0, 2).reshape(w_qkv.shape[1], -1)
     gain_row = layer_norm_gain[None, :]
-
-    pick, place = slots(owners[0, 0, :, :, 0], tile_ids[0, 0], span_z // TILE)
-    final_local, send = run_slab(field, material, conductivity[0], pick)
+    final_local, send, place, embed = run_slab(
+        start_field[0],
+        material,
+        conductivity[0],
+        owners[0, 0, :, :, 0],
+        tile_ids[0, 0],
+        embed_weight,
+    )
+    send, embed = lax.optimization_barrier((send, embed))
     got = swap(send, SPACE)
+    embed = jnp.stack([embed, swap_with(embed, "grp")])
+    embed = jnp.stack([embed, swap_cores(embed)]).reshape((-1,) + embed_weight.shape)
+    away = lax.axis_index(GROUP) ^ jnp.arange(embed.shape[0], dtype=jnp.int32)
+    embed = embed[((away & 1) << 2) + ((away >> 2 & 1) << 1) + (away >> 1 & 1)]
+    embed = embed.transpose(1, 0, 2).reshape(embed_weight.shape[0], -1)
+
     chips = lax.axis_size(CHIPS)
     copies = jnp.dot(
         jnp.tile(place, (chips, 1)), got, preferred_element_type=jnp.float32
     ).astype(jnp.bfloat16)
+    copies, embed = lax.optimization_barrier((copies, embed))
     samples = swap(copies, CHIPS)
-    tokens, targets = samples[:, :token_width], samples[:, token_width:]
-
-    tokens_other = swap_cores(tokens)
-    weights = (embed, gain_row, proj_w, mix, read)
-    normed, proj, prob, pred, base = run_forward(tokens, *weights, own=True)
+
+    samples_other = swap_cores(samples)
+    weights = (embed, gain_row, w_qkv, w_out, w_read)
+    normed, proj, prob, pred, base = run_forward(samples, *weights, own=True)
     normed_other, proj_other, prob_other, pred_other = run_forward(
-        tokens_other, *weights, own=False
+        samples_other, *weights, own=False
     )
     chip_pred = (pred + swap_cores(pred_other).astype(jnp.float32)).astype(jnp.bfloat16)
-    shares = spread(chip_pred, CHIPS).astype(jnp.float32)
+    shares = spread(chip_pred, CHIPS).reshape((chips,) + base.shape)
     row_count = lax.axis_size(GROUP) * SPD
-    loss_scale = math.sqrt(w_read.shape[0] / (lax.axis_size(SPACE) * row_count * target_width))
-    prediction = jnp.sum(shares, axis=0) + base
-    delta = ((prediction - targets.astype(jnp.float32)) * loss_scale).astype(jnp.bfloat16)
+    loss_scale = math.sqrt(
+        w_read.shape[0] / (lax.axis_size(SPACE) * row_count * w_read.shape[1])
+    )
+    delta = run_delta(shares, base, loss_scale)
 
     delta_other = swap_cores(delta)
-    half = run_backward(delta, mix_t, proj, prob, normed, None)
-    grads = run_backward(delta_other, mix_t, proj_other, prob_other, normed_other, half)
-
-    weight_total = sum_over_space(grads)
+    half = run_backward(delta, w_out, w_read, proj, prob, normed, None)
+    grads = run_backward(
+        delta_other, w_out, w_read, proj_other, prob_other, normed_other, half
+    )
+
     gain_share = (
-        jnp.sum(w_qkv.astype(jnp.float32) * weight_total.astype(jnp.float32), axis=(0, 2))
+        jnp.sum(w_qkv.astype(jnp.float32) * grads.astype(jnp.float32), axis=(0, 2))
         / layer_norm_gain
     )
-    gain_total = jnp.sum(spread(gain_share, GROUP), axis=0)
+    weight_total, gain_total = sum_over_devices(grads, gain_share)
     return (final_local[None], weight_total, gain_total)
 
 

time: 257 us -> 222 us (0.86)
  local copies, waits for them, and re-layouts: 23 us -> 6.41 us
  starting transfers between devices: 42.1 us -> 57 us
  between operations: 14.6 us -> 1.26 us
  blocking collectives: 107 us -> 93.8 us
  waiting for transfers between devices: 32 us -> 28.7 us
    ppermute x4 -> x10, starting transfers between devices: 9.88 us -> 27.1 us  [swap_with(): return lax.ppermute(own, axis, [(0, 1), (1, 0)])]
    all_to_all x2, waiting for transfers between devices: 29.5 us -> 15.9 us  [swap(): return lax.all_to_all(parts, axis, split_axis=0, concat_axis=0, tiled=True)]
    unnamed x66 -> x20, local copies, waits for them, and re-layouts: 13.2 us -> 0.05 us
    all_to_all x6 -> x5, blocking collectives: 107 us -> 93.8 us  [swap(): return lax.all_to_all(parts, axis, split_axis=0, concat_axis=0, tiled=True)]
    ppermute x4 -> x10, waiting for transfers between devices: 0.01 us -> 12.9 us  [swap_with(): return lax.ppermute(own, axis, [(0, 1), (1, 0)])]
    reshape x3 -> x2, local copies, waits for them, and re-layouts: 4.12 us -> 0.1 us  [the longest x1 0.09 us: sum_over_devices(): gain.reshape(count_z, chunk)]
    pallas_call x1, Pallas kernels: 9.45 us -> 6.3 us  [run_slab(): pl.pallas_call(functools.partial(slab_kernel, total_x=lax.axis_size(SPACE...]
  transfers between devices with their start and end apart: 9 -> 14, of which waited for: 4 -> 7; matrix products, arithmetic and copies ran while one was open for 7% -> 3% of each run, Pallas kernels for 7% -> 7%
where the time goes in v3:
time: 222 us
  blocking collectives  93.8 us (42%)
  starting transfers between devices  57 us (26%)
  waiting for transfers between devices  28.7 us (13%)
  Pallas kernels  24.8 us (11%)
  other arithmetic  9.13 us (4%)
  local copies, waits for them, and re-layouts  6.41 us (3%)
    all_to_all x5, blocking collectives, swap(): return lax.all_to_all(parts, axis, split_axis=0, concat_axis=0, tiled=True)  93.8 us
    ppermute x10, starting transfers between devices, swap_with(): return lax.ppermute(own, axis, [(0, 1), (1, 0)])  27.1 us
    all_to_all x2, starting transfers between devices, swap(): return lax.all_to_all(parts, axis, split_axis=0, concat_axis=0, tiled=True)  21.9 us
    all_to_all x2, waiting for transfers between devices, swap(): return lax.all_to_all(parts, axis, split_axis=0, concat_axis=0, tiled=True)  15.9 us
    ppermute x10, waiting for transfers between devices, swap_with(): return lax.ppermute(own, axis, [(0, 1), (1, 0)])  12.9 us
    pallas_call x2, Pallas kernels, run_forward(): pl.pallas_call(forward_kernel, grid=(rows // BLOCK_ROWS,), out_shape=tupl...  11.1 us
    pallas_call x2, Pallas kernels, run_backward(): pl.pallas_call(backward_kernel, grid=(rows // BLOCK_ROWS,), out_shape=out...  7.28 us
    pallas_call x1, Pallas kernels, run_slab(): pl.pallas_call(functools.partial(slab_kernel, total_x=lax.axis_size(SPACE...  6.3 us
  transfers between devices with their start and end apart: 14, of which 7 were waited for; matrix products, arithmetic and copies ran while one was open for 3% of the time, Pallas kernels for 7%

profile of v3, /device:TPU:32, one launch (start us, length us, event | category | flops | bytes accessed | tf_op | source)
XLA Modules:
  0.0 221.5 jit_solution(5739190732070624080)
XLA Ops:
  0.7 1.0 convert_bitcast_fusion
  1.7 1.0 fusion.3
  2.8 3.5 %collective-permute-start = (f32[2,16,3,256]{3,2,1,0:T(4,128)S(1)}, f32[2,16,3,256]{3,2,1,0:T(4,128)S(1)}, u32[]{:S(2)}, u32[]{:S(2)}) collective-permute-start(f32[2,16,3,256]{3,2,1,0:T(4,128)S(1)} %fusion.3), channel_id=1, source_target_pairs={{0,256},{256,0},{1,257},{257,1},{2,258},{258,2},{3,259},{259,3},{4... | collective-permute-start | bytes 294920 | tf_op jit(solution)/shard_map/ppermute | solution.py:41
  6.3 0.8 fusion.8
  7.2 2.7 %collective-permute-done.side_ref = f32[2,16,3,256]{3,2,1,0:T(4,128)S(1)} collective-permute-done((f32[2,16,3,256]{3,2,1,0:T(4,128)S(1)}, f32[2,16,3,256]{3,2,1,0:T(4,128)S(1)}, u32[]{:S(2)}, u32[]{:S(2)}) %collective-permute-start) | collective-permute-done | bytes 98336 | tf_op jit(solution)/shard_map/ppermute | solution.py:41
  9.9 2.6 %convert_reduce_fusion = s32[64,128]{1,0:T(8,128)S(1)} fusion(s32[64,128]{1,0:T(8,128)S(1)} %bitcast.57, pred[128,128]{1,0:T(8,128)(4,1)S(1)} %iota_compare_fusion.5), kind=kLoop, calls=%fused_computation.1 | loop fusion | flops 4186112 | bytes 81920 | tf_op jit(solution)/shard_map/reduce_sum | solution.py:264
  12.5 0.1 select_reduce_fusion
  12.7 0.1 sub.31
  12.9 3.4 %collective-permute-start.1 = (f32[2,3,22,256]{3,2,1,0:T(8,128)S(1)}, f32[2,3,22,256]{3,2,1,0:T(8,128)S(1)}, u32[]{:S(2)}, u32[]{:S(2)}) collective-permute-start(f32[2,3,22,256]{3,2,1,0:T(8,128)S(1)} %pad_maximum_fusion.6), channel_id=1, source_target_pairs={{0,4},{4,8},{8,12},{12,16},{16,20},{20,24},{24,28},{28,32},{32,36}... | collective-permute-start | bytes 405512 | tf_op jit(solution)/shard_map/ppermute | solution.py:58
  16.4 4.6 %collective-permute-start.2 = (f32[2,3,22,256]{3,2,1,0:T(8,128)S(1)}, f32[2,3,22,256]{3,2,1,0:T(8,128)S(1)}, u32[]{:S(2)}, u32[]{:S(2)}) collective-permute-start(f32[2,3,22,256]{3,2,1,0:T(8,128)S(1)} %fusion.1), channel_id=1, source_target_pairs={{4,0},{8,4},{12,8},{16,12},{20,16},{24,20},{28,24},{32,28},{36,32}... | collective-permute-start | bytes 405512 | tf_op jit(solution)/shard_map/ppermute | solution.py:59
  20.9 5.1 %collective-permute-start.3 = (bf16[512,192]{0,1:T(8,128)(2,1)S(1)}, bf16[512,192]{0,1:T(8,128)(2,1)S(1)}, u32[]{:S(2)}, u32[]{:S(2)}) collective-permute-start(bf16[512,192]{0,1:T(8,128)(2,1)S(1)} %copy-done.7), channel_id=1, source_target_pairs={{0,2},{2,0},{1,3},{3,1},{4,6},{6,4},{5,7},{7,5},{8,10},{10,8},{9,1... | collective-permute-start | bytes 589832 | tf_op jit(solution)/shard_map/ppermute | solution.py:41
  26.2 6.3 %slab.1 = (f32[16,16,256]{2,1,0:T(8,128)}, bf16[256,640]{1,0:T(8,128)(2,1)S(1)}) custom-call(s32[2]{0:T(128)S(1)} %pad_add_fusion.place_ref, f32[8]{0:T(128)S(1)} %bitcast.45, f32[16,16,256]{2,1,0:T(8,128)S(1)} %bitcast.44, s32[16,16,256]{2,1,0:T(8,128)S(1)} %copy-done.4, f32[2,16,3,256]{3,2,1,0:T(4,128)S(1)} %collective-permute-done.side_ref, ...), custom_call_target="tpu_custom_call" | custom-call | tf_op jit(solution)/shard_map/slab/pallas_call | solution.py:230
  32.5 2.6 %collective-permute-start.4 = (bf16[2,512,192]{1,2,0:T(8,128)(2,1)S(1)}, bf16[2,512,192]{1,2,0:T(8,128)(2,1)S(1)}, u32[]{:S(2)}, u32[]{:S(2)}) collective-permute-start(bf16[2,512,192]{1,2,0:T(8,128)(2,1)S(1)} %pad_maximum_fusion.2), channel_id=1, source_target_pairs={{0,256},{256,0},{1,257},{257,1},{2,258},{258,2},{3,259},{259,3},{4... | collective-permute-start | bytes 1179656 | tf_op jit(solution)/shard_map/ppermute | solution.py:41
  35.1 0.8 all_to_all.30
  35.9 18.4 %all-to-all-start = ((bf16[64,4,640]{2,1,0:T(4,128)(2,1)}), bf16[64,4,640]{2,1,0:T(4,128)(2,1)S(1)}, u32[]{:S(2)}, u32[]{:S(2)}) async-start(bf16[64,4,640]{2,1,0:T(4,128)(2,1)} %all_to_all.30), calls=%async_computation | async-start | bytes 655360 | tf_op jit(solution)/shard_map/all_to_all | solution.py:32
  54.3 0.1 fusion.30
  54.4 1.9 collective-permute-start.5
  56.5 2.1 collective-permute-done.5
  58.6 0.1 pad_maximum_fusion
  58.8 1.8 gather_fusion
  60.6 15.9 %all-to-all-done = bf16[64,4,640]{2,1,0:T(4,128)(2,1)S(1)} async-done(((bf16[64,4,640]{2,1,0:T(4,128)(2,1)}), bf16[64,4,640]{2,1,0:T(4,128)(2,1)S(1)}, u32[]{:S(2)}, u32[]{:S(2)}) %all-to-all-start) | async-done | bytes 327712 | tf_op jit(solution)/shard_map/all_to_all | solution.py:32
  76.6 0.4 convolution_convert_fusion
  76.9 12.6 %all_to_all.48 = bf16[4,128,640]{2,1,0:T(8,128)(2,1)} all-to-all(bf16[4,128,640]{2,1,0:T(8,128)(2,1)S(1)} %bitcast.48), channel_id=1, replica_groups=mesh['grp'=2,'z'=16,'x'=4,'yhi'=2,'core'=2] {'grp','yhi'}, dimensions={0} | all-to-all | bytes 1310720 | tf_op jit(solution)/shard_map/all_to_all | solution.py:32
  89.5 1.9 collective-permute-start.6
  91.5 1.9 copy.16.embed_ref
  93.3 0.5 collective-permute-done.6.sample_ref
  93.8 5.3 %forward_other.1 = (bf16[512,1536]{1,0:T(8,128)(2,1)S(1)}, bf16[512,384]{1,0:T(8,128)(2,1)S(1)}, f32[512,128]{1,0:T(8,128)S(1)}, bf16[512,128]{1,0:T(8,128)(2,1)S(1)}) custom-call(bf16[512,640]{1,0:T(8,128)(2,1)} %collective-permute-done.6.sample_ref, bf16[512,1536]{1,0:T(8,128)(2,1)S(1)} %copy.16.embed_ref, f32[1,1536]{1,0:T(1,128)S(1)} %broadcast_in_dim.34.gain_ref, ...), custom_call_target="tpu_custom_call" | custom-call | flops 1409286144 | bytes 6291456 | tf_op jit(solution)/shard_map/forward_other/pallas_call | solution.py:353
  99.2 2.0 collective-permute-start.7
  101.2 5.8 %forward_own.1 = (bf16[512,1536]{1,0:T(8,128)(2,1)S(1)}, bf16[512,384]{1,0:T(8,128)(2,1)S(1)}, f32[512,128]{1,0:T(8,128)S(1)}, f32[512,128]{1,0:T(8,128)S(1)}, f32[512,128]{1,0:T(8,128)S(1)}) custom-call(bf16[512,640]{1,0:T(8,128)(2,1)} %bitcast.22.sample_ref, bf16[512,1536]{1,0:T(8,128)(2,1)S(1)} %copy.16.embed_ref, ...), custom_call_target="tpu_custom_call" | custom-call | flops 1409286144 | bytes 6291456 | tf_op jit(solution)/shard_map/forward_own/pallas_call | solution.py:353
  107.1 12.4 %all_to_all.49.share_ref = bf16[4,512,128]{2,1,0:T(8,128)(2,1)S(1)} all-to-all(bf16[4,512,128]{2,1,0:T(8,128)(2,1)S(1)} %broadcast_in_dim.35), channel_id=1, replica_groups=mesh['grp'=2,'z'=16,'x'=4,'yhi'=2,'core'=2] {'grp','yhi'}, dimensions={0} | all-to-all | bytes 1048576 | tf_op jit(solution)/shard_map/all_to_all | solution.py:32
  119.6 1.9 collective-permute-start.8
  121.6 3.2 %backward_own.1.rest_0_ = f32[1536,384]{1,0:T(8,128)S(1)} custom-call(bf16[512,128]{1,0:T(8,128)(2,1)S(1)} %delta.1.delta_ref, bf16[128,1536]{1,0:T(8,128)(2,1)S(1)} %copy-done.1, bf16[1536,128]{1,0:T(8,128)(2,1)S(1)} %copy-done.2, bf16[512,384]{1,0:T(8,128)(2,1)S(1)} %get-tuple-element.37.proj_ref, f32[512,128]{1,0:T(8,128)S(1)} %get-tuple-element.38.prob_ref, ...), custom_call_target="tpu_custom_call" | custom-call | flops 603979776 | bytes 3145728 | tf_op jit(solution)/shard_map/backward_own/pallas_call | solution.py:455
  124.7 4.1 %backward_other.1 = bf16[3,1536,128]{2,1,0:T(8,128)(2,1)} custom-call(bf16[512,128]{1,0:T(8,128)(2,1)S(1)} %collective-permute-done.8.delta_ref, bf16[128,1536]{1,0:T(8,128)(2,1)S(1)} %copy-done.1, bf16[1536,128]{1,0:T(8,128)(2,1)S(1)} %copy-done.2, bf16[512,384]{1,0:T(8,128)(2,1)S(1)} %get-tuple-element.34.proj_ref, ...), custom_call_target="tpu_custom_call" | custom-call | flops 603979776 | bytes 3145728 | tf_op jit(solution)/shard_map/backward_other/pallas_call | solution.py:455
  128.9 3.5 %all-to-all-start.3 = ((bf16[4,1152,128]{2,1,0:T(8,128)(2,1)}), bf16[4,1152,128]{2,1,0:T(8,128)(2,1)S(1)}, u32[]{:S(2)}, u32[]{:S(2)}) async-start(bf16[4,1152,128]{2,1,0:T(8,128)(2,1)} %bitcast.23), calls=%async_computation.3 | async-start | bytes 2359296 | tf_op jit(solution)/shard_map/all_to_all | solution.py:32
  132.4 1.7 multiply_reduce_fusion
  134.1 2.4 %collective-permute-start.9 = (f32[1536]{0:T(1024)S(1)}, f32[1536]{0:T(1024)S(1)}, u32[]{:S(2)}, u32[]{:S(2)}) collective-permute-start(f32[1536]{0:T(1024)S(1)} %div.3), channel_id=1, source_target_pairs={{0,1},{1,0},{2,3},{3,2},{4,5},{5,4},{6,7},{7,6},{8,9},{9,8},{10,11... | collective-permute-start | bytes 18440 | tf_op jit(solution)/shard_map/ppermute | solution.py:41
  136.5 0.8 collective-permute-done.9
  137.3 2.4 %collective-permute-start.10 = (f32[1536]{0:T(1024)S(1)}, f32[1536]{0:T(1024)S(1)}, u32[]{:S(2)}, u32[]{:S(2)}) collective-permute-start(f32[1536]{0:T(1024)S(1)} %add.119), channel_id=1, source_target_pairs={{0,256},{256,0},{1,257},{257,1},{2,258},{258,2},{3,259},{259,3},{4... | collective-permute-start | bytes 18440 | tf_op jit(solution)/shard_map/ppermute | solution.py:41
  139.7 3.1 %collective-permute-done.10 = f32[1536]{0:T(1024)S(1)} collective-permute-done((f32[1536]{0:T(1024)S(1)}, f32[1536]{0:T(1024)S(1)}, u32[]{:S(2)}, u32[]{:S(2)}) %collective-permute-start.10) | collective-permute-done | bytes 6176 | tf_op jit(solution)/shard_map/ppermute | solution.py:41
  142.8 3.4 %collective-permute-start.11 = (f32[1536]{0:T(1024)S(1)}, f32[1536]{0:T(1024)S(1)}, u32[]{:S(2)}, u32[]{:S(2)}) collective-permute-start(f32[1536]{0:T(1024)S(1)} %add.120), channel_id=1, source_target_pairs={{0,2},{2,0},{1,3},{3,1},{4,6},{6,4},{5,7},{7,5},{8,10},{10,8},{9,1... | collective-permute-start | bytes 18440 | tf_op jit(solution)/shard_map/ppermute | solution.py:41
  146.2 3.7 %collective-permute-done.11 = f32[1536]{0:T(1024)S(1)} collective-permute-done((f32[1536]{0:T(1024)S(1)}, f32[1536]{0:T(1024)S(1)}, u32[]{:S(2)}, u32[]{:S(2)}) %collective-permute-start.11) | collective-permute-done | bytes 6176 | tf_op jit(solution)/shard_map/ppermute | solution.py:41
  150.0 0.3 reduce_sum.59
  150.4 23.2 %all_to_all.50 = bf16[16,80,128]{2,1,0:T(8,128)(2,1)S(1)} all-to-all(bf16[16,80,128]{2,1,0:T(8,128)(2,1)S(1)} %pad_maximum_fusion.3), channel_id=1, replica_groups=mesh['grp'=2,'z'=16,'x'=4,'yhi'=2,'core'=2] {'z'}, dimensions={0} | all-to-all | bytes 655360 | tf_op jit(solution)/shard_map/all_to_all | solution.py:32
  173.8 26.8 %all_to_all.51 = bf16[16,80,128]{2,1,0:T(8,128)(2,1)S(1)} all-to-all(bf16[16,80,128]{2,1,0:T(8,128)(2,1)S(1)} %broadcast_in_dim.36), channel_id=1, replica_groups=mesh['grp'=2,'z'=16,'x'=4,'yhi'=2,'core'=2] {'z'}, dimensions={0} | all-to-all | bytes 655360 | tf_op jit(solution)/shard_map/all_to_all | solution.py:32
  200.8 0.2 broadcast_in_dim.37
  201.0 18.8 %all_to_all.52 = bf16[4,1176,128]{2,1,0:T(8,128)(2,1)S(1)} all-to-all(bf16[4,1176,128]{2,1,0:T(8,128)(2,1)S(1)} %broadcast_in_dim.37), channel_id=1, replica_groups=mesh['grp'=2,'z'=16,'x'=4,'yhi'=2,'core'=2] {'x'}, dimensions={0} | all-to-all | bytes 2408448 | tf_op jit(solution)/shard_map/all_to_all | solution.py:32
  219.8 0.6 fusion.15
  220.4 1.1 slice.88
  (70 shorter events, 1.4 us)
Async XLA Ops:
  0.6 12.2 %copy-start = (f32[1,16,16,256]{3,2,1,0:T(8,128)S(1)}, f32[1,16,16,256]{3,2,1,0:T(8,128)}, u32[]{:S(2)}) copy-start(f32[1,16,16,256]{3,2,1,0:T(8,128)} %param.12) | copy-start | bytes 786436
  0.6 6.4 %copy-start.9 = (s32[1,1,64,128]{3,2,1,0:T(8,128)S(1)}, s32[1,1,64,128]{3,2,1,0:T(8,128)}, u32[]{:S(2)}) copy-start(s32[1,1,64,128]{3,2,1,0:T(8,128)} %param.16) | copy-start | bytes 98308
  0.7 9.2 %copy-start.6 = (s32[1,1,64,128,1]{3,4,2,1,0:T(1,128)S(1)}, s32[1,1,64,128,1]{3,4,2,1,0:T(1,128)}, u32[]{:S(2)}) copy-start(s32[1,1,64,128,1]{3,4,2,1,0:T(1,128)} %param.15) | copy-start | bytes 98308
  0.7 20.2 %copy-start.7 = (bf16[512,192]{0,1:T(8,128)(2,1)S(1)}, bf16[512,192]{0,1:T(8,128)(2,1)}, u32[]{:S(2)}) copy-start(bf16[512,192]{0,1:T(8,128)(2,1)} %param.17) | copy-start | bytes 589828
  0.7 25.5 %copy-start.4 = (s32[16,16,256]{2,1,0:T(8,128)S(1)}, s32[16,16,256]{2,1,0:T(8,128)}, u32[]{:S(2)}) copy-start(s32[16,16,256]{2,1,0:T(8,128)} %material_ref.1) | copy-start | bytes 786436
  0.7 25.5 %copy-start.5 = (f32[1,8]{1,0:T(1,128)S(1)}, f32[1,8]{1,0:T(1,128)}, u32[]{:S(2)}) copy-start(f32[1,8]{1,0:T(1,128)} %param.14) | copy-start | bytes 100
  2.8 7.1 %collective-permute-start = (f32[2,16,3,256]{3,2,1,0:T(4,128)S(1)}, f32[2,16,3,256]{3,2,1,0:T(4,128)S(1)}, u32[]{:S(2)}, u32[]{:S(2)}) collective-permute-start(f32[2,16,3,256]{3,2,1,0:T(4,128)S(1)} %fusion.3), channel_id=1, source_target_pairs={{0,256},{256,0},{1,257},{257,1},{2,258},{258,2},{3,259},{259,3},{4... | collective-permute-start | bytes 294920 | tf_op jit(solution)/shard_map/ppermute | solution.py:41
  12.9 13.2 %collective-permute-start.1 = (f32[2,3,22,256]{3,2,1,0:T(8,128)S(1)}, f32[2,3,22,256]{3,2,1,0:T(8,128)S(1)}, u32[]{:S(2)}, u32[]{:S(2)}) collective-permute-start(f32[2,3,22,256]{3,2,1,0:T(8,128)S(1)} %pad_maximum_fusion.6), channel_id=1, source_target_pairs={{0,4},{4,8},{8,12},{12,16},{16,20},{20,24},{24,28},{28,32},{32,36}... | collective-permute-start | bytes 405512 | tf_op jit(solution)/shard_map/ppermute | solution.py:58
  16.4 9.8 %collective-permute-start.2 = (f32[2,3,22,256]{3,2,1,0:T(8,128)S(1)}, f32[2,3,22,256]{3,2,1,0:T(8,128)S(1)}, u32[]{:S(2)}, u32[]{:S(2)}) collective-permute-start(f32[2,3,22,256]{3,2,1,0:T(8,128)S(1)} %fusion.1), channel_id=1, source_target_pairs={{4,0},{8,4},{12,8},{16,12},{20,16},{24,20},{28,24},{32,28},{36,32}... | collective-permute-start | bytes 405512 | tf_op jit(solution)/shard_map/ppermute | solution.py:59
  20.9 11.6 %collective-permute-start.3 = (bf16[512,192]{0,1:T(8,128)(2,1)S(1)}, bf16[512,192]{0,1:T(8,128)(2,1)S(1)}, u32[]{:S(2)}, u32[]{:S(2)}) collective-permute-start(bf16[512,192]{0,1:T(8,128)(2,1)S(1)} %copy-done.7), channel_id=1, source_target_pairs={{0,2},{2,0},{1,3},{3,1},{4,6},{6,4},{5,7},{7,5},{8,10},{10,8},{9,1... | collective-permute-start | bytes 589832 | tf_op jit(solution)/shard_map/ppermute | solution.py:41
  32.5 21.8 %collective-permute-start.4 = (bf16[2,512,192]{1,2,0:T(8,128)(2,1)S(1)}, bf16[2,512,192]{1,2,0:T(8,128)(2,1)S(1)}, u32[]{:S(2)}, u32[]{:S(2)}) collective-permute-start(bf16[2,512,192]{1,2,0:T(8,128)(2,1)S(1)} %pad_maximum_fusion.2), channel_id=1, source_target_pairs={{0,256},{256,0},{1,257},{257,1},{2,258},{258,2},{3,259},{259,3},{4... | collective-permute-start | bytes 1179656 | tf_op jit(solution)/shard_map/ppermute | solution.py:41
  35.9 40.5 %all-to-all-start = ((bf16[64,4,640]{2,1,0:T(4,128)(2,1)}), bf16[64,4,640]{2,1,0:T(4,128)(2,1)S(1)}, u32[]{:S(2)}, u32[]{:S(2)}) async-start(bf16[64,4,640]{2,1,0:T(4,128)(2,1)} %all_to_all.30), calls=%async_computation | async-start | bytes 655360 | tf_op jit(solution)/shard_map/all_to_all | solution.py:32
  54.4 4.2 %collective-permute-start.5 = (bf16[2,2,512,192]{2,3,1,0:T(8,128)(2,1)S(1)}, bf16[2,2,512,192]{2,3,1,0:T(8,128)(2,1)S(1)}, u32[]{:S(2)}, u32[]{:S(2)}) collective-permute-start(bf16[2,2,512,192]{2,3,1,0:T(8,128)(2,1)S(1)} %get-tuple-element.52), channel_id=1, source_target_pairs={{0,1},{1,0},{2,3},{3,2},{4,5},{5,4},{6,7},{7,6},{8,9},{9,8},{10,11... | collective-permute-start | bytes 2359304 | tf_op jit(solution)/shard_map/ppermute | solution.py:41
  76.5 14.9 %copy-start.8 = (f32[1536]{0:T(1024)S(1)}, f32[1536]{0:T(1024)}, u32[]{:S(2)}) copy-start(f32[1536]{0:T(1024)} %param.18) | copy-start | bytes 18436
  89.5 4.3 %collective-permute-start.6 = (bf16[512,640]{1,0:T(8,128)(2,1)}, bf16[512,640]{1,0:T(8,128)(2,1)}, u32[]{:S(2)}, u32[]{:S(2)}) collective-permute-start(bf16[512,640]{1,0:T(8,128)(2,1)} %bitcast.22.sample_ref), channel_id=1, source_target_pairs={{0,1},{1,0},{2,3},{3,2},{4,5},{5,4},{6,7},{7,6},{8,9},{9,8},{10,11... | collective-permute-start | bytes 1966088 | tf_op jit(solution)/shard_map/ppermute | solution.py:41
  91.5 2.4 %copy-start.1 = (bf16[128,1536]{1,0:T(8,128)(2,1)S(1)}, bf16[128,1536]{1,0:T(8,128)(2,1)}, u32[]{:S(2)}) copy-start(bf16[128,1536]{1,0:T(8,128)(2,1)} %out_ref.7) | copy-start | bytes 1179652
  91.5 2.4 %copy-start.2 = (bf16[1536,128]{1,0:T(8,128)(2,1)S(1)}, bf16[1536,128]{1,0:T(8,128)(2,1)}, u32[]{:S(2)}) copy-start(bf16[1536,128]{1,0:T(8,128)(2,1)} %read_ref.7) | copy-start | bytes 1179652
  91.5 2.4 %copy-start.3 = (bf16[3,1536,128]{2,1,0:T(8,128)(2,1)S(1)}, bf16[3,1536,128]{2,1,0:T(8,128)(2,1)}, u32[]{:S(2)}) copy-start(bf16[3,1536,128]{2,1,0:T(8,128)(2,1)} %proj_w_ref.3) | copy-start | bytes 3538948
  99.2 7.8 %collective-permute-start.7 = (bf16[512,128]{1,0:T(8,128)(2,1)S(1)}, bf16[512,128]{1,0:T(8,128)(2,1)S(1)}, u32[]{:S(2)}, u32[]{:S(2)}) collective-permute-start(bf16[512,128]{1,0:T(8,128)(2,1)S(1)} %get-tuple-element.32), channel_id=1, source_target_pairs={{0,1},{1,0},{2,3},{3,2},{4,5},{5,4},{6,7},{7,6},{8,9},{9,8},{10,11... | collective-permute-start | bytes 393224 | tf_op jit(solution)/shard_map/ppermute | solution.py:41
  119.6 5.1 %collective-permute-start.8 = (bf16[512,128]{1,0:T(8,128)(2,1)S(1)}, bf16[512,128]{1,0:T(8,128)(2,1)S(1)}, u32[]{:S(2)}, u32[]{:S(2)}) collective-permute-start(bf16[512,128]{1,0:T(8,128)(2,1)S(1)} %delta.1.delta_ref), channel_id=1, source_target_pairs={{0,1},{1,0},{2,3},{3,2},{4,5},{5,4},{6,7},{7,6},{8,9},{9,8},{10,11... | collective-permute-start | bytes 393224 | tf_op jit(solution)/shard_map/ppermute | solution.py:41
  128.9 21.2 %all-to-all-start.3 = ((bf16[4,1152,128]{2,1,0:T(8,128)(2,1)}), bf16[4,1152,128]{2,1,0:T(8,128)(2,1)S(1)}, u32[]{:S(2)}, u32[]{:S(2)}) async-start(bf16[4,1152,128]{2,1,0:T(8,128)(2,1)} %bitcast.23), calls=%async_computation.3 | async-start | bytes 2359296 | tf_op jit(solution)/shard_map/all_to_all | solution.py:32
  134.1 3.2 %collective-permute-start.9 = (f32[1536]{0:T(1024)S(1)}, f32[1536]{0:T(1024)S(1)}, u32[]{:S(2)}, u32[]{:S(2)}) collective-permute-start(f32[1536]{0:T(1024)S(1)} %div.3), channel_id=1, source_target_pairs={{0,1},{1,0},{2,3},{3,2},{4,5},{5,4},{6,7},{7,6},{8,9},{9,8},{10,11... | collective-permute-start | bytes 18440 | tf_op jit(solution)/shard_map/ppermute | solution.py:41
  137.3 5.5 %collective-permute-start.10 = (f32[1536]{0:T(1024)S(1)}, f32[1536]{0:T(1024)S(1)}, u32[]{:S(2)}, u32[]{:S(2)}) collective-permute-start(f32[1536]{0:T(1024)S(1)} %add.119), channel_id=1, source_target_pairs={{0,256},{256,0},{1,257},{257,1},{2,258},{258,2},{3,259},{259,3},{4... | collective-permute-start | bytes 18440 | tf_op jit(solution)/shard_map/ppermute | solution.py:41
  142.8 7.0 %collective-permute-start.11 = (f32[1536]{0:T(1024)S(1)}, f32[1536]{0:T(1024)S(1)}, u32[]{:S(2)}, u32[]{:S(2)}) collective-permute-start(f32[1536]{0:T(1024)S(1)} %add.120), channel_id=1, source_target_pairs={{0,2},{2,0},{1,3},{3,1},{4,6},{6,4},{5,7},{7,5},{8,10},{10,8},{9,1... | collective-permute-start | bytes 18440 | tf_op jit(solution)/shard_map/ppermute | solution.py:41

commit v4 on v3

--- a/solution.py
+++ b/solution.py
@@ -21,7 +21,6 @@
 CHIPS = ("grp", "yhi")
 
 PAD = 4
-BLOCK_ROWS = 256
 VMEM = pl.BlockSpec(memory_space=pltpu.VMEM)
 SMEM = pl.BlockSpec(memory_space=pltpu.SMEM)
 LIMIT = 20 * 1024 * 1024
@@ -45,30 +44,37 @@
     return swap_with(own, "core")
 
 
-def halos(block, width, beside):
+def halos(field, material, width, beside):
     half = lax.axis_index("grp")
-    face = jnp.where(half == 0, block[:, :, -width:], block[:, :, :width])
+
+    def cut(span, axis):
+        return jnp.stack(
+            [
+                lax.slice_in_dim(field, *span, axis=axis),
+                lax.slice_in_dim(material, *span, axis=axis).astype(jnp.float32),
+            ]
+        )
+
+    span_x, span_y = field.shape[:2]
+    face = jnp.where(
+        half == 0, cut((span_y - width, span_y), 1), cut((0, width), 1)
+    )
     side = swap_with(face, "grp")
     side, beside = lax.optimization_barrier((side, beside))
     count = lax.axis_size(SPACE)
     forward = [(i, i + 1) for i in range(count - 1)]
     backward = [(i + 1, i) for i in range(count - 1)]
-    top = jnp.concatenate([side[:, -width:], block[:, -width:], side[:, -width:]], axis=2)
-    bottom = jnp.concatenate([side[:, :width], block[:, :width], side[:, :width]], axis=2)
+    top, bottom = side[:, -width:], side[:, :width]
+    top = jnp.concatenate([top, cut((span_x - width, span_x), 0), top], axis=2)
+    bottom = jnp.concatenate([bottom, cut((0, width), 0), bottom], axis=2)
     low = lax.ppermute(top, SPACE, forward)
     high = lax.ppermute(bottom, SPACE, backward)
     return side, low, high, beside
 
 
 def over(first, last, body):
-    def turn(i, _):
-        body(first + 2 * i)
-        body(first + 2 * i + 1)
-        return 0
-
-    lax.fori_loop(0, (last - first) // 2, turn, 0)
-    if (last - first) % 2:
-        body(last - 1)
+    for plane in range(first, last):
+        body(plane)
 
 
 def slab_kernel(
@@ -216,23 +222,23 @@
 
 
 def run_slab(field, material, table, owner_list, tile_list, embed_own):
+    pick, place = slots(owner_list, tile_list, field.shape[2] // TILE)
+    side, low, high, embed_own = halos(field, material, STEPS, embed_own)
+    embed = jnp.stack([embed_own, swap_with(embed_own, "yhi")])
+    origin = jnp.stack([lax.axis_index(SPACE), lax.axis_index("grp")]).astype(jnp.int32)
+    totals = (lax.axis_size(SPACE) * field.shape[0], lax.axis_size("grp") * field.shape[1])
+    final, send = call_slab(origin, table, field, material, side, low, high, pick, totals)
+    return final, send, place, embed
+
+
+def call_slab(origin, table, field, material, side, low, high, pick, totals):
     span_x, span_y, span_z = field.shape
-    width = STEPS
-    block = jnp.stack([field, material.astype(jnp.float32)])
-    side, low, high, (owner_list, embed_own) = halos(block, width, (owner_list, embed_own))
-    embed = jnp.stack([embed_own, swap_with(embed_own, "yhi")])
-    pick, place = slots(owner_list, tile_list, span_z // TILE)
-    origin = jnp.stack([lax.axis_index(SPACE), lax.axis_index("grp")]).astype(jnp.int32)
-    planes, rows = span_x + 2 * width, span_y + 2 * PAD
+    planes, rows = span_x + 2 * low.shape[1], span_y + 2 * PAD
     tiles = span_z // TILE
     values = (span_x * span_y // 4 + span_x * span_y // 16) * TILE // 2
     extended = pltpu.VMEM((planes, rows, span_z), jnp.float32)
-    final, send = pl.pallas_call(
-        functools.partial(
-            slab_kernel,
-            total_x=lax.axis_size(SPACE) * span_x,
-            total_y=lax.axis_size("grp") * span_y,
-        ),
+    return pl.pallas_call(
+        functools.partial(slab_kernel, total_x=totals[0], total_y=totals[1]),
         out_shape=(
             jax.ShapeDtypeStruct(field.shape, jnp.float32),
             jax.ShapeDtypeStruct((pick.shape[0], values), jnp.bfloat16),
@@ -251,25 +257,28 @@
         compiler_params=pltpu.CompilerParams(vmem_limit_bytes=LIMIT),
         name="slab",
     )(origin, table, field, material, side, low, high, pick)
-    return final, send, place, embed
 
 
 def slots(owner_list, tile_list, tile_count):
     shard_count, slot_count = owner_list.shape
     capacity = 2 * slot_count // shard_count
     my_index = lax.axis_index(SPACE)
-    same_owner = owner_list[:, :, None] == owner_list[:, None, :]
     slot_order = jnp.arange(slot_count, dtype=jnp.int32)
-    earlier = slot_order[None, :] < slot_order[:, None]
-    slot_rank = jnp.sum((same_owner & earlier[None]).astype(jnp.int32), axis=2)
+    earlier = slot_order[:, None] < slot_order[None, :]
     owned_here = owner_list == my_index
+    here_rank = jnp.dot(
+        owned_here.astype(jnp.bfloat16),
+        earlier.astype(jnp.bfloat16),
+        preferred_element_type=jnp.float32,
+    ).astype(jnp.int32)
     slot_ids = jnp.arange(capacity, dtype=jnp.int32)
-    slot_match = owned_here[:, None, :] & (slot_rank[:, None, :] == slot_ids[None, :, None])
+    slot_match = owned_here[:, None, :] & (here_rank[:, None, :] == slot_ids[None, :, None])
     chosen = jnp.sum(jnp.where(slot_match, tile_list[:, None, :] + 1, 0), axis=2) - 1
     tile_ids = jnp.arange(tile_count, dtype=jnp.int32)
     pick = (chosen.reshape(-1, 1) == tile_ids[None, :]).astype(jnp.bfloat16)
     own_owner = jnp.take(owner_list, my_index, axis=0)
-    own_rank = jnp.take(slot_rank, my_index, axis=0)
+    same_owner = own_owner[:, None] == own_owner[None, :]
+    own_rank = jnp.sum((same_owner & earlier).astype(jnp.int32), axis=0)
     flat_index = own_owner * capacity + own_rank
     flat_ids = jnp.arange(shard_count * capacity, dtype=jnp.int32)
     place = (flat_index[:, None] == flat_ids[None, :]).astype(jnp.bfloat16)
@@ -327,18 +336,8 @@
         )
 
 
-def whole(array):
-    return pl.BlockSpec(
-        array.shape, lambda i: (0,) * array.ndim, pipeline_mode=pl.Buffered(buffer_count=1)
-    )
-
-
-def by_rows(columns):
-    return pl.BlockSpec((BLOCK_ROWS, columns), lambda i: (i, 0))
-
-
 def run_forward(samples, embed, gain, w_qkv, w_out, w_read, own):
-    rows, sample_width = samples.shape
+    rows = samples.shape[0]
     kinds, model, head = w_qkv.shape
     out_width = w_read.shape[1]
     shapes = [
@@ -352,10 +351,9 @@
     weights = (embed, gain, w_qkv, w_out, w_read)
     return pl.pallas_call(
         forward_kernel,
-        grid=(rows // BLOCK_ROWS,),
         out_shape=tuple(shapes),
-        in_specs=[by_rows(sample_width)] + [whole(array) for array in weights],
-        out_specs=tuple(by_rows(shape.shape[1]) for shape in shapes),
+        in_specs=[VMEM] * (1 + len(weights)),
+        out_specs=(VMEM,) * len(shapes),
         compiler_params=pltpu.CompilerParams(vmem_limit_bytes=LIMIT),
         cost_estimate=pl.CostEstimate(
             flops=2 * rows * model * (embed.shape[0] + kinds * head),
@@ -385,9 +383,8 @@
 
 
 def backward_kernel(delta_ref, out_ref, read_ref, proj_ref, prob_ref, normed_ref, *rest):
-    start_ref = rest[0] if len(rest) == 3 else None
-    grad_ref, total = rest[-2], rest[-1]
-    step = pl.program_id(0)
+    start_ref = rest[0] if len(rest) == 2 else None
+    grad_ref = rest[-1]
     across = (((1,), (1,)), ((), ()))
     down = (((0,), (0,)), ((), ()))
     delta = delta_ref[...]
@@ -417,24 +414,13 @@
         )
     grads = jnp.concatenate(grads, axis=0)
 
-    @pl.when(step == 0)
-    def _():
-        if start_ref is None:
-            total[...] = jnp.zeros_like(total)
-        else:
-            total[...] = start_ref[...]
-
-    total[...] += lax.dot_general(
-        normed_ref[...], grads, down, preferred_element_type=jnp.float32
-    )
-
-    @pl.when(step == pl.num_programs(0) - 1)
-    def _():
-        if start_ref is None:
-            grad_ref[...] = total[...]
-        else:
-            for i in range(grad_ref.shape[0]):
-                grad_ref[i] = total[:, i * HD : (i + 1) * HD].astype(grad_ref.dtype)
+    total = lax.dot_general(normed_ref[...], grads, down, preferred_element_type=jnp.float32)
+    if start_ref is None:
+        grad_ref[...] = total
+    else:
+        total = total + start_ref[...]
+        for i in range(grad_ref.shape[0]):
+            grad_ref[i] = total[:, i * HD : (i + 1) * HD].astype(grad_ref.dtype)
 
 
 def run_backward(delta, w_out, w_read, proj, prob, normed, start):
@@ -445,20 +431,13 @@
     else:
         out = jax.ShapeDtypeStruct((heads // HD, model, HD), jnp.bfloat16)
     operands = [delta, w_out, w_read, proj, prob, normed]
-    specs = [
-        by_rows(delta.shape[1]), whole(w_out), whole(w_read),
-        by_rows(heads), by_rows(SPD), by_rows(model),
-    ]
     if start is not None:
         operands.append(start)
-        specs.append(whole(start))
     return pl.pallas_call(
         backward_kernel,
-        grid=(rows // BLOCK_ROWS,),
         out_shape=out,
-        in_specs=specs,
-        out_specs=whole(out),
-        scratch_shapes=[pltpu.VMEM((model, heads), jnp.float32)],
+        in_specs=[VMEM] * len(operands),
+        out_specs=VMEM,
         compiler_params=pltpu.CompilerParams(vmem_limit_bytes=LIMIT),
         cost_estimate=pl.CostEstimate(
             flops=2 * rows * model * heads, bytes_accessed=rows * model * 4, transcendentals=0

time: 222 us -> 216 us (0.973)
  Pallas kernels: 24.8 us -> 20.6 us
  waiting for transfers between devices: 28.7 us -> 24.7 us
    pallas_call x5, Pallas kernels: 24.7 us -> 20.5 us  [the longest x2 10.6 us: run_forward(): pl.pallas_call(forward_kernel, out_shape=tuple(shapes), in_specs=[VMEM] *...]
    ppermute x10, waiting for transfers between devices: 12.9 us -> 8.83 us  [swap_with(): return lax.ppermute(own, axis, [(0, 1), (1, 0)])]
    reduce_sum x1, other arithmetic: 2.56 us -> 0.1 us  [slots(): own_rank = jnp.sum((same_owner & earlier).astype(jnp.int32), axis=0)]
  transfers between devices with their start and end apart: 14 -> 14, of which waited for: 7 -> 6; matrix products, arithmetic and copies ran while one was open for 3% -> 5% of each run, Pallas kernels for 7% -> 6%
where the time goes in v4:
time: 216 us; the launch traced here: 215 us
  blocking collectives  93.8 us (43%)
  starting transfers between devices  57 us (26%)
  waiting for transfers between devices  24.7 us (11%)
  Pallas kernels  20.6 us (10%)
  other arithmetic  8.52 us (4%)
  local copies, waits for them, and re-layouts  8.33 us (4%)
    all_to_all x5, blocking collectives, swap(): return lax.all_to_all(parts, axis, split_axis=0, concat_axis=0, tiled=True)  93.8 us
    ppermute x10, starting transfers between devices, swap_with(): return lax.ppermute(own, axis, [(0, 1), (1, 0)])  27.7 us
    all_to_all x2, starting transfers between devices, swap(): return lax.all_to_all(parts, axis, split_axis=0, concat_axis=0, tiled=True)  21.3 us
    all_to_all x2, waiting for transfers between devices, swap(): return lax.all_to_all(parts, axis, split_axis=0, concat_axis=0, tiled=True)  15.8 us
    pallas_call x2, Pallas kernels, run_forward(): pl.pallas_call(forward_kernel, out_shape=tuple(shapes), in_specs=[VMEM] *...  10.6 us
    ppermute x10, waiting for transfers between devices, swap_with(): return lax.ppermute(own, axis, [(0, 1), (1, 0)])  8.83 us
    pallas_call x2, Pallas kernels, run_backward(): pl.pallas_call(backward_kernel, out_shape=out, in_specs=[VMEM] * len(oper...  5.85 us
    ppermute x1, starting transfers between devices, halos(): high = lax.ppermute(bottom, SPACE, backward)  4.55 us
  transfers between devices with their start and end apart: 14, of which 6 were waited for; matrix products, arithmetic and copies ran while one was open for 5% of the time, Pallas kernels for 6%

profile of v4, /device:TPU:32, one launch (start us, length us, event | category | flops | bytes accessed | tf_op | source)
XLA Modules:
  0.0 214.6 jit_solution(6614426034959305915)
XLA Ops:
  0.7 1.1 slice_bitcast_fusion
  1.8 1.0 convert_bitcast_fusion
  2.8 3.5 %collective-permute-start = (f32[2,16,3,256]{3,2,1,0:T(4,128)S(1)}, f32[2,16,3,256]{3,2,1,0:T(4,128)S(1)}, u32[]{:S(2)}, u32[]{:S(2)}) collective-permute-start(f32[2,16,3,256]{3,2,1,0:T(4,128)S(1)} %maximum_select_fusion), channel_id=1, source_target_pairs={{0,256},{256,0},{1,257},{257,1},{2,258},{258,2},{3,259},{259,3},{4... | collective-permute-start | bytes 294920 | tf_op jit(solution)/shard_map/ppermute | solution.py:40
  6.3 0.8 fusion.23
  7.2 0.8 convert_bitcast_fusion.2
  8.0 0.8 broadcast_compare_fusion
  9.0 0.8 add_bitcast_fusion
  10.1 3.4 %collective-permute-start.1 = (f32[2,3,22,256]{3,2,1,0:T(8,128)S(1)}, f32[2,3,22,256]{3,2,1,0:T(8,128)S(1)}, u32[]{:S(2)}, u32[]{:S(2)}) collective-permute-start(f32[2,3,22,256]{3,2,1,0:T(8,128)S(1)} %pad_maximum_fusion.5), channel_id=1, source_target_pairs={{0,4},{4,8},{8,12},{12,16},{16,20},{20,24},{24,28},{28,32},{32,36}... | collective-permute-start | bytes 405512 | tf_op jit(solution)/shard_map/ppermute | solution.py:70
  13.6 4.6 %collective-permute-start.2 = (f32[2,3,22,256]{3,2,1,0:T(8,128)S(1)}, f32[2,3,22,256]{3,2,1,0:T(8,128)S(1)}, u32[]{:S(2)}, u32[]{:S(2)}) collective-permute-start(f32[2,3,22,256]{3,2,1,0:T(8,128)S(1)} %pad_maximum_fusion.6), channel_id=1, source_target_pairs={{4,0},{8,4},{12,8},{16,12},{20,16},{24,20},{28,24},{32,28},{36,32}... | collective-permute-start | bytes 405512 | tf_op jit(solution)/shard_map/ppermute | solution.py:71
  18.2 5.0 %collective-permute-start.3 = (bf16[512,192]{0,1:T(8,128)(2,1)S(1)}, bf16[512,192]{0,1:T(8,128)(2,1)S(1)}, u32[]{:S(2)}, u32[]{:S(2)}) collective-permute-start(bf16[512,192]{0,1:T(8,128)(2,1)S(1)} %copy-done.6), channel_id=1, source_target_pairs={{0,2},{2,0},{1,3},{3,1},{4,6},{6,4},{5,7},{7,5},{8,10},{10,8},{9,1... | collective-permute-start | bytes 589832 | tf_op jit(solution)/shard_map/ppermute | solution.py:40
  23.3 4.1 %slab.1 = (f32[16,16,256]{2,1,0:T(8,128)}, bf16[256,640]{1,0:T(8,128)(2,1)S(1)}) custom-call(s32[2]{0:T(128)S(1)} %pad_add_fusion.place_ref, f32[8]{0:T(128)S(1)} %bitcast.54, f32[16,16,256]{2,1,0:T(8,128)S(1)} %bitcast.53, s32[16,16,256]{2,1,0:T(8,128)S(1)} %copy-done.4, f32[2,16,3,256]{3,2,1,0:T(4,128)S(1)} %collective-permute-done.side_ref, ...), custom_call_target="tpu_custom_call" | custom-call | tf_op jit(solution)/shard_map/slab/pallas_call | solution.py:240
  27.5 3.1 %collective-permute-start.4 = (bf16[2,512,192]{1,2,0:T(8,128)(2,1)S(1)}, bf16[2,512,192]{1,2,0:T(8,128)(2,1)S(1)}, u32[]{:S(2)}, u32[]{:S(2)}) collective-permute-start(bf16[2,512,192]{1,2,0:T(8,128)(2,1)S(1)} %pad_maximum_fusion.2), channel_id=1, source_target_pairs={{0,256},{256,0},{1,257},{257,1},{2,258},{258,2},{3,259},{259,3},{4... | collective-permute-start | bytes 1179656 | tf_op jit(solution)/shard_map/ppermute | solution.py:40
  30.6 0.8 all_to_all.30
  31.4 17.8 %all-to-all-start = ((bf16[64,4,640]{2,1,0:T(4,128)(2,1)}), bf16[64,4,640]{2,1,0:T(4,128)(2,1)S(1)}, u32[]{:S(2)}, u32[]{:S(2)}) async-start(bf16[64,4,640]{2,1,0:T(4,128)(2,1)} %all_to_all.30), calls=%async_computation | async-start | bytes 655360 | tf_op jit(solution)/shard_map/all_to_all | solution.py:31
  49.4 1.9 collective-permute-start.5
  51.3 0.7 fusion.19
  52.1 0.7 multiply_add_fusion
  52.8 0.7 collective-permute-done.5
  53.6 0.1 pad_maximum_fusion
  53.7 1.8 gather_fusion
  55.5 15.8 %all-to-all-done = bf16[64,4,640]{2,1,0:T(4,128)(2,1)S(1)} async-done(((bf16[64,4,640]{2,1,0:T(4,128)(2,1)}), bf16[64,4,640]{2,1,0:T(4,128)(2,1)S(1)}, u32[]{:S(2)}, u32[]{:S(2)}) %all-to-all-start) | async-done | bytes 327712 | tf_op jit(solution)/shard_map/all_to_all | solution.py:31
  71.5 0.4 convolution_convert_fusion
  71.9 12.6 %all_to_all.48 = bf16[4,128,640]{2,1,0:T(8,128)(2,1)} all-to-all(bf16[4,128,640]{2,1,0:T(8,128)(2,1)S(1)} %bitcast.57), channel_id=1, replica_groups=mesh['grp'=2,'z'=16,'x'=4,'yhi'=2,'core'=2] {'grp','yhi'}, dimensions={0} | all-to-all | bytes 1310720 | tf_op jit(solution)/shard_map/all_to_all | solution.py:31
  84.4 1.9 collective-permute-start.6
  86.4 1.9 copy.16.embed_ref
  88.3 0.5 collective-permute-done.6.sample_ref
  88.8 5.0 %forward_other.1 = (bf16[512,1536]{1,0:T(8,128)(2,1)S(1)}, bf16[512,384]{1,0:T(8,128)(2,1)S(1)}, f32[512,128]{1,0:T(8,128)S(1)}, bf16[512,128]{1,0:T(8,128)(2,1)S(1)}) custom-call(bf16[512,640]{1,0:T(8,128)(2,1)} %collective-permute-done.6.sample_ref, bf16[512,1536]{1,0:T(8,128)(2,1)S(1)} %copy.16.embed_ref, f32[1,1536]{1,0:T(1,128)S(1)} %broadcast_in_dim.65.gain_ref, ...), custom_call_target="tpu_custom_call" | custom-call | flops 1409286144 | bytes 6291456 | tf_op jit(solution)/shard_map/forward_other/pallas_call | solution.py:352
  93.8 2.2 %collective-permute-start.7 = (bf16[512,128]{1,0:T(8,128)(2,1)S(1)}, bf16[512,128]{1,0:T(8,128)(2,1)S(1)}, u32[]{:S(2)}, u32[]{:S(2)}) collective-permute-start(bf16[512,128]{1,0:T(8,128)(2,1)S(1)} %get-tuple-element.29), channel_id=1, source_target_pairs={{0,1},{1,0},{2,3},{3,2},{4,5},{5,4},{6,7},{7,6},{8,9},{9,8},{10,11... | collective-permute-start | bytes 393224 | tf_op jit(solution)/shard_map/ppermute | solution.py:40
  96.0 5.5 %forward_own.1 = (bf16[512,1536]{1,0:T(8,128)(2,1)S(1)}, bf16[512,384]{1,0:T(8,128)(2,1)S(1)}, f32[512,128]{1,0:T(8,128)S(1)}, f32[512,128]{1,0:T(8,128)S(1)}, f32[512,128]{1,0:T(8,128)S(1)}) custom-call(bf16[512,640]{1,0:T(8,128)(2,1)} %bitcast.25.sample_ref, bf16[512,1536]{1,0:T(8,128)(2,1)S(1)} %copy.16.embed_ref, ...), custom_call_target="tpu_custom_call" | custom-call | flops 1409286144 | bytes 6291456 | tf_op jit(solution)/shard_map/forward_own/pallas_call | solution.py:352
  101.7 12.4 %all_to_all.49.share_ref = bf16[4,512,128]{2,1,0:T(8,128)(2,1)S(1)} all-to-all(bf16[4,512,128]{2,1,0:T(8,128)(2,1)S(1)} %broadcast_in_dim.66), channel_id=1, replica_groups=mesh['grp'=2,'z'=16,'x'=4,'yhi'=2,'core'=2] {'grp','yhi'}, dimensions={0} | all-to-all | bytes 1048576 | tf_op jit(solution)/shard_map/all_to_all | solution.py:31
  114.2 1.9 collective-permute-start.8
  116.1 2.4 %backward_own.1.rest_0_ = f32[1536,384]{1,0:T(8,128)S(1)} custom-call(bf16[512,128]{1,0:T(8,128)(2,1)S(1)} %delta.1.delta_ref, bf16[128,1536]{1,0:T(8,128)(2,1)S(1)} %copy-done, bf16[1536,128]{1,0:T(8,128)(2,1)S(1)} %copy-done.1, bf16[512,384]{1,0:T(8,128)(2,1)S(1)} %get-tuple-element.34.proj_ref, f32[512,128]{1,0:T(8,128)S(1)} %get-tuple-element.35.prob_ref, ...), custom_call_target="tpu_custom_call" | custom-call | flops 603979776 | bytes 3145728 | tf_op jit(solution)/shard_map/backward_own/pallas_call | solution.py:436
  118.5 3.4 %backward_other.1 = bf16[3,1536,128]{2,1,0:T(8,128)(2,1)} custom-call(bf16[512,128]{1,0:T(8,128)(2,1)S(1)} %collective-permute-done.8.delta_ref, bf16[128,1536]{1,0:T(8,128)(2,1)S(1)} %copy-done, bf16[1536,128]{1,0:T(8,128)(2,1)S(1)} %copy-done.1, bf16[512,384]{1,0:T(8,128)(2,1)S(1)} %get-tuple-element.31.proj_ref, ...), custom_call_target="tpu_custom_call" | custom-call | flops 603979776 | bytes 3145728 | tf_op jit(solution)/shard_map/backward_other/pallas_call | solution.py:436
  122.0 3.5 %all-to-all-start.3 = ((bf16[4,1152,128]{2,1,0:T(8,128)(2,1)}), bf16[4,1152,128]{2,1,0:T(8,128)(2,1)S(1)}, u32[]{:S(2)}, u32[]{:S(2)}) async-start(bf16[4,1152,128]{2,1,0:T(8,128)(2,1)} %bitcast.26), calls=%async_computation.3 | async-start | bytes 2359296 | tf_op jit(solution)/shard_map/all_to_all | solution.py:31
  125.5 1.7 multiply_reduce_fusion
  127.2 2.4 %collective-permute-start.9 = (f32[1536]{0:T(1024)S(1)}, f32[1536]{0:T(1024)S(1)}, u32[]{:S(2)}, u32[]{:S(2)}) collective-permute-start(f32[1536]{0:T(1024)S(1)} %div.3), channel_id=1, source_target_pairs={{0,1},{1,0},{2,3},{3,2},{4,5},{5,4},{6,7},{7,6},{8,9},{9,8},{10,11... | collective-permute-start | bytes 18440 | tf_op jit(solution)/shard_map/ppermute | solution.py:40
  129.6 0.8 collective-permute-done.9
  130.4 2.4 %collective-permute-start.10 = (f32[1536]{0:T(1024)S(1)}, f32[1536]{0:T(1024)S(1)}, u32[]{:S(2)}, u32[]{:S(2)}) collective-permute-start(f32[1536]{0:T(1024)S(1)} %add.125), channel_id=1, source_target_pairs={{0,256},{256,0},{1,257},{257,1},{2,258},{258,2},{3,259},{259,3},{4... | collective-permute-start | bytes 18440 | tf_op jit(solution)/shard_map/ppermute | solution.py:40
  132.8 3.1 %collective-permute-done.10 = f32[1536]{0:T(1024)S(1)} collective-permute-done((f32[1536]{0:T(1024)S(1)}, f32[1536]{0:T(1024)S(1)}, u32[]{:S(2)}, u32[]{:S(2)}) %collective-permute-start.10) | collective-permute-done | bytes 6176 | tf_op jit(solution)/shard_map/ppermute | solution.py:40
  136.0 3.4 %collective-permute-start.11 = (f32[1536]{0:T(1024)S(1)}, f32[1536]{0:T(1024)S(1)}, u32[]{:S(2)}, u32[]{:S(2)}) collective-permute-start(f32[1536]{0:T(1024)S(1)} %add.126), channel_id=1, source_target_pairs={{0,2},{2,0},{1,3},{3,1},{4,6},{6,4},{5,7},{7,5},{8,10},{10,8},{9,1... | collective-permute-start | bytes 18440 | tf_op jit(solution)/shard_map/ppermute | solution.py:40
  139.3 3.7 %collective-permute-done.11 = f32[1536]{0:T(1024)S(1)} collective-permute-done((f32[1536]{0:T(1024)S(1)}, f32[1536]{0:T(1024)S(1)}, u32[]{:S(2)}, u32[]{:S(2)}) %collective-permute-start.11) | collective-permute-done | bytes 6176 | tf_op jit(solution)/shard_map/ppermute | solution.py:40
  143.2 0.3 reduce_sum.59
  143.5 23.2 %all_to_all.50 = bf16[16,80,128]{2,1,0:T(8,128)(2,1)S(1)} all-to-all(bf16[16,80,128]{2,1,0:T(8,128)(2,1)S(1)} %pad_maximum_fusion.3), channel_id=1, replica_groups=mesh['grp'=2,'z'=16,'x'=4,'yhi'=2,'core'=2] {'z'}, dimensions={0} | all-to-all | bytes 655360 | tf_op jit(solution)/shard_map/all_to_all | solution.py:31
  166.9 26.8 %all_to_all.51 = bf16[16,80,128]{2,1,0:T(8,128)(2,1)S(1)} all-to-all(bf16[16,80,128]{2,1,0:T(8,128)(2,1)S(1)} %broadcast_in_dim.67), channel_id=1, replica_groups=mesh['grp'=2,'z'=16,'x'=4,'yhi'=2,'core'=2] {'z'}, dimensions={0} | all-to-all | bytes 655360 | tf_op jit(solution)/shard_map/all_to_all | solution.py:31
  193.9 0.2 broadcast_in_dim.68
  194.1 18.8 %all_to_all.52 = bf16[4,1176,128]{2,1,0:T(8,128)(2,1)S(1)} all-to-all(bf16[4,1176,128]{2,1,0:T(8,128)(2,1)S(1)} %broadcast_in_dim.68), channel_id=1, replica_groups=mesh['grp'=2,'z'=16,'x'=4,'yhi'=2,'core'=2] {'x'}, dimensions={0} | all-to-all | bytes 2408448 | tf_op jit(solution)/shard_map/all_to_all | solution.py:31
  213.0 0.6 fusion.10
  213.6 1.1 slice.100
  (70 shorter events, 2.0 us)
Async XLA Ops:
  0.6 22.7 %copy-start.3 = (f32[1,16,16,256]{3,2,1,0:T(8,128)S(1)}, f32[1,16,16,256]{3,2,1,0:T(8,128)}, u32[]{:S(2)}) copy-start(f32[1,16,16,256]{3,2,1,0:T(8,128)} %param.10) | copy-start | bytes 786436
  0.6 22.7 %copy-start.4 = (s32[16,16,256]{2,1,0:T(8,128)S(1)}, s32[16,16,256]{2,1,0:T(8,128)}, u32[]{:S(2)}) copy-start(s32[16,16,256]{2,1,0:T(8,128)} %material_ref.1) | copy-start | bytes 786436
  0.7 17.5 %copy-start.6 = (bf16[512,192]{0,1:T(8,128)(2,1)S(1)}, bf16[512,192]{0,1:T(8,128)(2,1)}, u32[]{:S(2)}) copy-start(bf16[512,192]{0,1:T(8,128)(2,1)} %param.15) | copy-start | bytes 589828
  0.7 22.7 %copy-start.5 = (f32[1,8]{1,0:T(1,128)S(1)}, f32[1,8]{1,0:T(1,128)}, u32[]{:S(2)}) copy-start(f32[1,8]{1,0:T(1,128)} %param.12) | copy-start | bytes 100
  2.8 7.3 %collective-permute-start = (f32[2,16,3,256]{3,2,1,0:T(4,128)S(1)}, f32[2,16,3,256]{3,2,1,0:T(4,128)S(1)}, u32[]{:S(2)}, u32[]{:S(2)}) collective-permute-start(f32[2,16,3,256]{3,2,1,0:T(4,128)S(1)} %maximum_select_fusion), channel_id=1, source_target_pairs={{0,256},{256,0},{1,257},{257,1},{2,258},{258,2},{3,259},{259,3},{4... | collective-permute-start | bytes 294920 | tf_op jit(solution)/shard_map/ppermute | solution.py:40
  10.1 13.2 %collective-permute-start.1 = (f32[2,3,22,256]{3,2,1,0:T(8,128)S(1)}, f32[2,3,22,256]{3,2,1,0:T(8,128)S(1)}, u32[]{:S(2)}, u32[]{:S(2)}) collective-permute-start(f32[2,3,22,256]{3,2,1,0:T(8,128)S(1)} %pad_maximum_fusion.5), channel_id=1, source_target_pairs={{0,4},{4,8},{8,12},{12,16},{16,20},{20,24},{24,28},{28,32},{32,36}... | collective-permute-start | bytes 405512 | tf_op jit(solution)/shard_map/ppermute | solution.py:70
  13.6 9.7 %collective-permute-start.2 = (f32[2,3,22,256]{3,2,1,0:T(8,128)S(1)}, f32[2,3,22,256]{3,2,1,0:T(8,128)S(1)}, u32[]{:S(2)}, u32[]{:S(2)}) collective-permute-start(f32[2,3,22,256]{3,2,1,0:T(8,128)S(1)} %pad_maximum_fusion.6), channel_id=1, source_target_pairs={{4,0},{8,4},{12,8},{16,12},{20,16},{24,20},{28,24},{32,28},{36,32}... | collective-permute-start | bytes 405512 | tf_op jit(solution)/shard_map/ppermute | solution.py:71
  18.2 9.3 %collective-permute-start.3 = (bf16[512,192]{0,1:T(8,128)(2,1)S(1)}, bf16[512,192]{0,1:T(8,128)(2,1)S(1)}, u32[]{:S(2)}, u32[]{:S(2)}) collective-permute-start(bf16[512,192]{0,1:T(8,128)(2,1)S(1)} %copy-done.6), channel_id=1, source_target_pairs={{0,2},{2,0},{1,3},{3,1},{4,6},{6,4},{5,7},{7,5},{8,10},{10,8},{9,1... | collective-permute-start | bytes 589832 | tf_op jit(solution)/shard_map/ppermute | solution.py:40
  27.5 21.7 %collective-permute-start.4 = (bf16[2,512,192]{1,2,0:T(8,128)(2,1)S(1)}, bf16[2,512,192]{1,2,0:T(8,128)(2,1)S(1)}, u32[]{:S(2)}, u32[]{:S(2)}) collective-permute-start(bf16[2,512,192]{1,2,0:T(8,128)(2,1)S(1)} %pad_maximum_fusion.2), channel_id=1, source_target_pairs={{0,256},{256,0},{1,257},{257,1},{2,258},{258,2},{3,259},{259,3},{4... | collective-permute-start | bytes 1179656 | tf_op jit(solution)/shard_map/ppermute | solution.py:40
  31.4 39.9 %all-to-all-start = ((bf16[64,4,640]{2,1,0:T(4,128)(2,1)}), bf16[64,4,640]{2,1,0:T(4,128)(2,1)S(1)}, u32[]{:S(2)}, u32[]{:S(2)}) async-start(bf16[64,4,640]{2,1,0:T(4,128)(2,1)} %all_to_all.30), calls=%async_computation | async-start | bytes 655360 | tf_op jit(solution)/shard_map/all_to_all | solution.py:31
  49.4 4.2 %collective-permute-start.5 = (bf16[2,2,512,192]{2,3,1,0:T(8,128)(2,1)S(1)}, bf16[2,2,512,192]{2,3,1,0:T(8,128)(2,1)S(1)}, u32[]{:S(2)}, u32[]{:S(2)}) collective-permute-start(bf16[2,2,512,192]{2,3,1,0:T(8,128)(2,1)S(1)} %get-tuple-element.49), channel_id=1, source_target_pairs={{0,1},{1,0},{2,3},{3,2},{4,5},{5,4},{6,7},{7,6},{8,9},{9,8},{10,11... | collective-permute-start | bytes 2359304 | tf_op jit(solution)/shard_map/ppermute | solution.py:40
  71.4 14.9 %copy-start.7 = (f32[1536]{0:T(1024)S(1)}, f32[1536]{0:T(1024)}, u32[]{:S(2)}) copy-start(f32[1536]{0:T(1024)} %param.16) | copy-start | bytes 18436
  84.4 4.3 %collective-permute-start.6 = (bf16[512,640]{1,0:T(8,128)(2,1)}, bf16[512,640]{1,0:T(8,128)(2,1)}, u32[]{:S(2)}, u32[]{:S(2)}) collective-permute-start(bf16[512,640]{1,0:T(8,128)(2,1)} %bitcast.25.sample_ref), channel_id=1, source_target_pairs={{0,1},{1,0},{2,3},{3,2},{4,5},{5,4},{6,7},{7,6},{8,9},{9,8},{10,11... | collective-permute-start | bytes 1966088 | tf_op jit(solution)/shard_map/ppermute | solution.py:40
  86.4 2.4 %copy-start = (bf16[128,1536]{1,0:T(8,128)(2,1)S(1)}, bf16[128,1536]{1,0:T(8,128)(2,1)}, u32[]{:S(2)}) copy-start(bf16[128,1536]{1,0:T(8,128)(2,1)} %out_ref.7) | copy-start | bytes 1179652
  86.4 2.4 %copy-start.1 = (bf16[1536,128]{1,0:T(8,128)(2,1)S(1)}, bf16[1536,128]{1,0:T(8,128)(2,1)}, u32[]{:S(2)}) copy-start(bf16[1536,128]{1,0:T(8,128)(2,1)} %read_ref.7) | copy-start | bytes 1179652
  86.4 2.4 %copy-start.2 = (bf16[3,1536,128]{2,1,0:T(8,128)(2,1)S(1)}, bf16[3,1536,128]{2,1,0:T(8,128)(2,1)}, u32[]{:S(2)}) copy-start(bf16[3,1536,128]{2,1,0:T(8,128)(2,1)} %proj_w_ref.3) | copy-start | bytes 3538948
  93.8 7.8 %collective-permute-start.7 = (bf16[512,128]{1,0:T(8,128)(2,1)S(1)}, bf16[512,128]{1,0:T(8,128)(2,1)S(1)}, u32[]{:S(2)}, u32[]{:S(2)}) collective-permute-start(bf16[512,128]{1,0:T(8,128)(2,1)S(1)} %get-tuple-element.29), channel_id=1, source_target_pairs={{0,1},{1,0},{2,3},{3,2},{4,5},{5,4},{6,7},{7,6},{8,9},{9,8},{10,11... | collective-permute-start | bytes 393224 | tf_op jit(solution)/shard_map/ppermute | solution.py:40
  114.2 4.4 %collective-permute-start.8 = (bf16[512,128]{1,0:T(8,128)(2,1)S(1)}, bf16[512,128]{1,0:T(8,128)(2,1)S(1)}, u32[]{:S(2)}, u32[]{:S(2)}) collective-permute-start(bf16[512,128]{1,0:T(8,128)(2,1)S(1)} %delta.1.delta_ref), channel_id=1, source_target_pairs={{0,1},{1,0},{2,3},{3,2},{4,5},{5,4},{6,7},{7,6},{8,9},{9,8},{10,11... | collective-permute-start | bytes 393224 | tf_op jit(solution)/shard_map/ppermute | solution.py:40
  122.0 21.2 %all-to-all-start.3 = ((bf16[4,1152,128]{2,1,0:T(8,128)(2,1)}), bf16[4,1152,128]{2,1,0:T(8,128)(2,1)S(1)}, u32[]{:S(2)}, u32[]{:S(2)}) async-start(bf16[4,1152,128]{2,1,0:T(8,128)(2,1)} %bitcast.26), calls=%async_computation.3 | async-start | bytes 2359296 | tf_op jit(solution)/shard_map/all_to_all | solution.py:31
  127.2 3.2 %collective-permute-start.9 = (f32[1536]{0:T(1024)S(1)}, f32[1536]{0:T(1024)S(1)}, u32[]{:S(2)}, u32[]{:S(2)}) collective-permute-start(f32[1536]{0:T(1024)S(1)} %div.3), channel_id=1, source_target_pairs={{0,1},{1,0},{2,3},{3,2},{4,5},{5,4},{6,7},{7,6},{8,9},{9,8},{10,11... | collective-permute-start | bytes 18440 | tf_op jit(solution)/shard_map/ppermute | solution.py:40
  130.4 5.5 %collective-permute-start.10 = (f32[1536]{0:T(1024)S(1)}, f32[1536]{0:T(1024)S(1)}, u32[]{:S(2)}, u32[]{:S(2)}) collective-permute-start(f32[1536]{0:T(1024)S(1)} %add.125), channel_id=1, source_target_pairs={{0,256},{256,0},{1,257},{257,1},{2,258},{258,2},{3,259},{259,3},{4... | collective-permute-start | bytes 18440 | tf_op jit(solution)/shard_map/ppermute | solution.py:40
  136.0 7.0 %collective-permute-start.11 = (f32[1536]{0:T(1024)S(1)}, f32[1536]{0:T(1024)S(1)}, u32[]{:S(2)}, u32[]{:S(2)}) collective-permute-start(f32[1536]{0:T(1024)S(1)} %add.126), channel_id=1, source_target_pairs={{0,2},{2,0},{1,3},{3,1},{4,6},{6,4},{5,7},{7,5},{8,10},{10,8},{9,1... | collective-permute-start | bytes 18440 | tf_op jit(solution)/shard_map/ppermute | solution.py:40

commit v5 on v4

--- a/solution.py
+++ b/solution.py
@@ -285,122 +285,171 @@
     return pick, place
 
 
-def mixing_parts(out_ref, read_ref):
-    mixing = jnp.dot(out_ref[...], read_ref[...], preferred_element_type=jnp.float32)
+def layout(token_width, model):
+    heads = 6 * HD
+    mix = model + model // token_width * heads
+    return heads, mix, mix + HD, mix + 2 * HD
+
+
+def prepare_kernel(
+    order_ref, parts_ref, w_own_ref, w_other_ref, out_own_ref, out_other_ref, read_ref, all_ref
+):
+    count, width, rows = parts_ref.shape
+    model = count * width
+    heads, mix, read, _ = layout(rows, model)
+    for i in range(count // 2):
+        pair = jnp.concatenate(
+            [parts_ref[order_ref[2 * i]], parts_ref[order_ref[2 * i + 1]]], axis=0
+        )
+        all_ref[:, 2 * i * width : 2 * (i + 1) * width] = pair.T
+    for block in range(model // rows):
+        for head, ref in enumerate((w_own_ref, w_other_ref)):
+            for i in range(3):
+                start = model + block * heads + (3 * head + i) * HD
+                all_ref[:, start : start + HD] = ref[i, block * rows : (block + 1) * rows, :]
+    out_w = jnp.concatenate([out_own_ref[...], out_other_ref[...]], axis=0)
+    mixing = jnp.dot(out_w, read_ref[...], preferred_element_type=jnp.float32)
     high = mixing.astype(jnp.bfloat16)
-    return high, (mixing - high.astype(jnp.float32)).astype(jnp.bfloat16)
+    all_ref[: 2 * HD, mix:read] = high
+    all_ref[2 * HD :, mix:read] = (mixing - high.astype(jnp.float32)).astype(jnp.bfloat16)
+    share = 2 * width
+    start = pl.multiple_of(order_ref[count] * share, share)
+    all_ref[:share, read:] = read_ref[pl.ds(start, share), :]
+    all_ref[share:, read:] = jnp.zeros((rows - share, HD), jnp.bfloat16)
+
+
+def run_prepare(order, parts, w_own, w_other, out_own, out_other, w_read):
+    rows, model = parts.shape[2], w_own.shape[1]
+    return pl.pallas_call(
+        prepare_kernel,
+        out_shape=jax.ShapeDtypeStruct((rows, layout(rows, model)[-1]), jnp.bfloat16),
+        in_specs=[SMEM] + [VMEM] * 6,
+        out_specs=VMEM,
+        compiler_params=pltpu.CompilerParams(vmem_limit_bytes=LIMIT),
+        cost_estimate=pl.CostEstimate(flops=1 << 28, bytes_accessed=1 << 23, transcendentals=0),
+        name="prepare",
+    )(order, parts, w_own, w_other, out_own, out_other, w_read)
 
 
 def forward_kernel(
-    sample_ref, embed_ref, gain_ref, proj_w_ref, out_ref, read_ref,
-    normed_ref, proj_ref, prob_ref, pred_ref, *base_ref,
+    chip_ref, sample_ref, all_ref, gain_ref, normed_ref, proj_ref, prob_ref, pred_ref, embed_ref
 ):
+    token_width = all_ref.shape[0]
+    model = normed_ref.shape[1]
+    heads, mix, read, _ = layout(token_width, model)
+    across = (((1,), (1,)), ((), ()))
     embedded = jnp.dot(
-        sample_ref[:, : embed_ref.shape[0]], embed_ref[...], preferred_element_type=jnp.float32
+        sample_ref[:, :token_width], all_ref[:, :model], preferred_element_type=jnp.float32
     ).astype(jnp.bfloat16)
+    embed_ref[...] = embedded
     wide = embedded.astype(jnp.float32)
     mean = jnp.mean(wide, axis=1, keepdims=True)
     removed = wide - mean
     variance = jnp.mean(removed * removed, axis=1, keepdims=True)
     normed = (removed * lax.rsqrt(variance + NORM_EPSILON) * gain_ref[...]).astype(jnp.bfloat16)
     normed_ref[...] = normed
-    proj_w = jnp.concatenate([proj_w_ref[i] for i in range(3)], axis=1)
+    proj_w = jnp.concatenate(
+        [all_ref[:, start : start + heads] for start in range(model, mix, heads)], axis=0
+    )
     proj = jnp.dot(normed, proj_w, preferred_element_type=jnp.float32).astype(jnp.bfloat16)
     proj_ref[...] = proj
     attended = []
     for seq in range(sample_ref.shape[0] // SPD):
         rows = slice(seq * SPD, (seq + 1) * SPD)
-        query, key, value = (proj[rows, i * HD : (i + 1) * HD] for i in range(3))
-        scores = lax.dot_general(
-            query, key, (((1,), (1,)), ((), ())), preferred_element_type=jnp.float32
-        ) * (1.0 / math.sqrt(HD))
-        raised = jnp.exp(scores - jnp.max(scores, axis=-1, keepdims=True))
-        probs = raised / jnp.sum(raised, axis=-1, keepdims=True)
-        prob_ref[rows, :] = probs
-        attended.append(
-            jnp.dot(
-                probs.astype(jnp.bfloat16), value, preferred_element_type=jnp.float32
-            ).astype(jnp.bfloat16)
-        )
+        parts = []
+        for head in range(2):
+            query, key, value = (
+                proj[rows, i * HD : (i + 1) * HD] for i in range(3 * head, 3 * head + 3)
+            )
+            scores = lax.dot_general(
+                query, key, across, preferred_element_type=jnp.float32
+            ) * (1.0 / math.sqrt(HD))
+            raised = jnp.exp(scores - jnp.max(scores, axis=-1, keepdims=True))
+            probs = raised / jnp.sum(raised, axis=-1, keepdims=True)
+            prob_ref[rows, head * SPD : (head + 1) * SPD] = probs
+            parts.append(
+                jnp.dot(
+                    probs.astype(jnp.bfloat16), value, preferred_element_type=jnp.float32
+                ).astype(jnp.bfloat16)
+            )
+        attended.append(jnp.concatenate(parts, axis=1))
     attended = jnp.concatenate(attended, axis=0)
-    high, low = mixing_parts(out_ref, read_ref)
+    share = model // 4
+    start = pl.multiple_of(chip_ref[0] * share, share)
     pred_ref[...] = jnp.dot(
-        jnp.concatenate([attended, attended], axis=1),
-        jnp.concatenate([high, low], axis=0),
+        jnp.concatenate([attended, attended, embed_ref[:, pl.ds(start, share)]], axis=1),
+        jnp.concatenate([all_ref[:, mix:read], all_ref[:share, read:]], axis=0),
         preferred_element_type=jnp.float32,
     ).astype(pred_ref.dtype)
-    if base_ref:
-        targets = sample_ref[:, embed_ref.shape[0] :].astype(jnp.float32)
-        base_ref[0][...] = (
-            jnp.dot(embedded, read_ref[...], preferred_element_type=jnp.float32) - targets
-        )
-
-
-def run_forward(samples, embed, gain, w_qkv, w_out, w_read, own):
+
+
+def run_forward(chip, samples, weights, gain):
     rows = samples.shape[0]
-    kinds, model, head = w_qkv.shape
-    out_width = w_read.shape[1]
-    shapes = [
+    model = gain.shape[1]
+    heads = layout(weights.shape[0], model)[0]
+    shapes = (
         jax.ShapeDtypeStruct((rows, model), jnp.bfloat16),
-        jax.ShapeDtypeStruct((rows, kinds * head), jnp.bfloat16),
-        jax.ShapeDtypeStruct((rows, SPD), jnp.float32),
-        jax.ShapeDtypeStruct((rows, out_width), jnp.float32 if own else jnp.bfloat16),
-    ]
-    if own:
-        shapes.append(jax.ShapeDtypeStruct((rows, out_width), jnp.float32))
-    weights = (embed, gain, w_qkv, w_out, w_read)
+        jax.ShapeDtypeStruct((rows, heads), jnp.bfloat16),
+        jax.ShapeDtypeStruct((rows, 2 * SPD), jnp.float32),
+        jax.ShapeDtypeStruct((rows, HD), jnp.bfloat16),
+    )
     return pl.pallas_call(
         forward_kernel,
-        out_shape=tuple(shapes),
-        in_specs=[VMEM] * (1 + len(weights)),
+        out_shape=shapes,
+        in_specs=[SMEM] + [VMEM] * 3,
         out_specs=(VMEM,) * len(shapes),
+        scratch_shapes=[pltpu.VMEM((rows, model), jnp.bfloat16)],
         compiler_params=pltpu.CompilerParams(vmem_limit_bytes=LIMIT),
         cost_estimate=pl.CostEstimate(
-            flops=2 * rows * model * (embed.shape[0] + kinds * head),
+            flops=2 * rows * model * (weights.shape[0] + heads),
             bytes_accessed=rows * model * 8,
-            transcendentals=rows * SPD,
+            transcendentals=2 * rows * SPD,
         ),
-        name="forward_own" if own else "forward_other",
-    )(samples, *weights)
-
-
-def delta_kernel(share_ref, base_ref, delta_ref, *, scale):
-    total = base_ref[...]
-    for i in range(share_ref.shape[0]):
+        name="forward",
+    )(chip, samples, weights, gain)
+
+
+def delta_kernel(share_ref, sample_ref, delta_ref, *, scale):
+    targets = sample_ref[:, sample_ref.shape[1] - delta_ref.shape[1] :]
+    total = share_ref[0].astype(jnp.float32)
+    for i in range(1, share_ref.shape[0]):
         total = total + share_ref[i].astype(jnp.float32)
-    delta_ref[...] = (total * scale).astype(delta_ref.dtype)
-
-
-def run_delta(shares, base, scale):
+    delta_ref[...] = ((total - targets.astype(jnp.float32)) * scale).astype(delta_ref.dtype)
+
+
+def run_delta(shares, samples, scale):
     return pl.pallas_call(
         functools.partial(delta_kernel, scale=scale),
-        out_shape=jax.ShapeDtypeStruct(base.shape, jnp.bfloat16),
+        out_shape=jax.ShapeDtypeStruct(shares.shape[1:], jnp.bfloat16),
         in_specs=[VMEM, VMEM],
         out_specs=VMEM,
         compiler_params=pltpu.CompilerParams(vmem_limit_bytes=LIMIT),
         name="delta",
-    )(shares, base)
-
-
-def backward_kernel(delta_ref, out_ref, read_ref, proj_ref, prob_ref, normed_ref, *rest):
-    start_ref = rest[0] if len(rest) == 2 else None
-    grad_ref = rest[-1]
+    )(shares, samples)
+
+
+def backward_kernel(
+    delta_ref, all_ref, proj_ref, prob_ref, normed_ref, grad_ref, *, head
+):
+    _, mix, read, _ = layout(all_ref.shape[0], normed_ref.shape[1])
     across = (((1,), (1,)), ((), ()))
     down = (((0,), (0,)), ((), ()))
     delta = delta_ref[...]
-    high, low = mixing_parts(out_ref, read_ref)
+    mixing = [all_ref[(2 * i + head) * HD : (2 * i + head + 1) * HD, mix:read] for i in range(2)]
     grad_attended = lax.dot_general(
         jnp.concatenate([delta, delta], axis=1),
-        jnp.concatenate([high, low], axis=1),
+        jnp.concatenate(mixing, axis=1),
         across,
         preferred_element_type=jnp.float32,
     ).astype(jnp.bfloat16)
     grads = []
     for seq in range(delta_ref.shape[0] // SPD):
         rows = slice(seq * SPD, (seq + 1) * SPD)
-        query, key, value = (proj_ref[rows, i * HD : (i + 1) * HD] for i in range(3))
+        query, key, value = (
+            proj_ref[rows, i * HD : (i + 1) * HD] for i in range(3 * head, 3 * head + 3)
+        )
         upper = grad_attended[rows]
-        probs = prob_ref[rows, :]
+        probs = prob_ref[rows, head * SPD : (head + 1) * SPD]
         grad_probs = lax.dot_general(upper, value, across, preferred_element_type=jnp.float32)
         grad_value = lax.dot_general(
             probs.astype(jnp.bfloat16), upper, down, preferred_element_type=jnp.float32
@@ -413,80 +462,54 @@
             jnp.concatenate([grad_query, grad_key, grad_value], axis=1).astype(jnp.bfloat16)
         )
     grads = jnp.concatenate(grads, axis=0)
-
     total = lax.dot_general(normed_ref[...], grads, down, preferred_element_type=jnp.float32)
-    if start_ref is None:
-        grad_ref[...] = total
-    else:
-        total = total + start_ref[...]
-        for i in range(grad_ref.shape[0]):
-            grad_ref[i] = total[:, i * HD : (i + 1) * HD].astype(grad_ref.dtype)
-
-
-def run_backward(delta, w_out, w_read, proj, prob, normed, start):
+    for i in range(grad_ref.shape[0]):
+        grad_ref[i] = total[:, i * HD : (i + 1) * HD].astype(grad_ref.dtype)
+
+
+def run_backward(delta, weights, proj, prob, normed, head):
     rows, model = normed.shape
-    heads = proj.shape[1]
-    if start is None:
-        out = jax.ShapeDtypeStruct((model, heads), jnp.float32)
-    else:
-        out = jax.ShapeDtypeStruct((heads // HD, model, HD), jnp.bfloat16)
-    operands = [delta, w_out, w_read, proj, prob, normed]
-    if start is not None:
-        operands.append(start)
+    heads = proj.shape[1] // 2
+    operands = (delta, weights, proj, prob, normed)
     return pl.pallas_call(
-        backward_kernel,
-        out_shape=out,
+        functools.partial(backward_kernel, head=head),
+        out_shape=jax.ShapeDtypeStruct((heads // HD, model, HD), jnp.bfloat16),
         in_specs=[VMEM] * len(operands),
         out_specs=VMEM,
         compiler_params=pltpu.CompilerParams(vmem_limit_bytes=LIMIT),
         cost_estimate=pl.CostEstimate(
             flops=2 * rows * model * heads, bytes_accessed=rows * model * 4, transcendentals=0
         ),
-        name="backward_own" if start is None else "backward_other",
+        name="backward_other" if head else "backward_own",
     )(*operands)
-
-
-def split(values, rows):
-    columns = 128
-    high = values.astype(jnp.bfloat16)
-    low = (values - high.astype(jnp.float32)).astype(jnp.bfloat16)
-    both = jnp.stack([high, low], axis=-2)
-    both = both.reshape(both.shape[:-2] + (-1, min(columns, both.shape[-1])))
-    pad = [(0, 0)] * (both.ndim - 2)
-    return jnp.pad(both, pad + [(0, rows - both.shape[-2]), (0, columns - both.shape[-1])])
 
 
 def sum_over_devices(parts, gain):
     count_x, count_z = lax.axis_size("x"), lax.axis_size("z")
     shape, columns, width = parts.shape, parts.shape[-1], gain.shape[0]
-    chunk = width // count_z
-    spare = 8
-
-    part = jnp.sum(swap(parts.reshape(count_x, -1, columns), "x").astype(jnp.float32), axis=0)
+
+    sent = jnp.concatenate(
+        [
+            parts.reshape(count_x, -1, columns),
+            gain.astype(jnp.bfloat16).reshape(count_x, -1, columns),
+        ],
+        axis=1,
+    )
+    extra = width // (count_x * columns)
+    part = jnp.sum(swap(sent, "x").astype(jnp.float32), axis=0)
+    gain = part[-extra:]
+    part = part[:-extra].astype(jnp.bfloat16).reshape(count_z, -1, columns)
+    total = jnp.sum(swap(part, "z").astype(jnp.float32), axis=0).astype(jnp.bfloat16)
     for axis in ("core", "grp", "yhi"):
         gain = gain + swap_with(gain, axis)
 
-    sent = jnp.concatenate(
-        [
-            part.astype(jnp.bfloat16).reshape(count_z, -1, columns),
-            split(gain.reshape(count_z, chunk), spare),
-        ],
-        axis=1,
-    )
-    total = jnp.sum(swap(sent, "z").astype(jnp.float32), axis=0)
-    rows = total.shape[0] - spare
-    own_gain = total[rows, :chunk] + total[rows + 1, :chunk]
-    sent = jnp.concatenate([total[:rows].astype(jnp.bfloat16), split(own_gain, spare)], axis=0)
+    sent = jnp.concatenate([total, gain.astype(jnp.bfloat16)], axis=0)
     got = spread(sent, "z").reshape(count_z, -1, columns)
-    gain = (
-        got[:, rows, :chunk].astype(jnp.float32) + got[:, rows + 1, :chunk].astype(jnp.float32)
-    ).reshape(width)
-    gain_rows = 2 * width // columns
-    sent = jnp.concatenate([got[:, :rows].reshape(-1, columns), split(gain, gain_rows)], axis=0)
+    gain = jnp.sum(got[:, -extra:].astype(jnp.float32), axis=0)
+    sent = jnp.concatenate([got[:, :-extra].reshape(-1, columns), gain.astype(jnp.bfloat16)], axis=0)
     got = spread(sent, "x").reshape(count_x, -1, columns)
-    gain = jnp.sum(got[:, -gain_rows:].astype(jnp.float32), axis=0)
-    gain = (gain[: gain_rows // 2] + gain[gain_rows // 2 :]).reshape(width)
-    return got[:, :-gain_rows].reshape(shape), gain
+    gain = got[:, -extra:].astype(jnp.float32)
+    return got[:, :-extra].reshape(shape), gain.reshape(width)
 
 
 def shards(
@@ -508,42 +531,42 @@
         conductivity[0],
         owners[0, 0, :, :, 0],
         tile_ids[0, 0],
-        embed_weight,
+        embed_weight.T,
     )
     send, embed = lax.optimization_barrier((send, embed))
-    got = swap(send, SPACE)
+    got = swap(send.reshape(lax.axis_size(SPACE), -1, send.shape[1]), SPACE)
     embed = jnp.stack([embed, swap_with(embed, "grp")])
-    embed = jnp.stack([embed, swap_cores(embed)]).reshape((-1,) + embed_weight.shape)
+    embed, w_own, out_own = lax.optimization_barrier((embed, w_qkv, w_out))
+    w_other, out_other = swap_cores(w_own), swap_cores(out_own)
+    embed = jnp.stack([embed, swap_cores(embed)]).reshape((-1,) + embed_weight.T.shape)
     away = lax.axis_index(GROUP) ^ jnp.arange(embed.shape[0], dtype=jnp.int32)
-    embed = embed[((away & 1) << 2) + ((away >> 2 & 1) << 1) + (away >> 1 & 1)]
-    embed = embed.transpose(1, 0, 2).reshape(embed_weight.shape[0], -1)
+    order = ((away & 1) << 2) + ((away >> 2 & 1) << 1) + (away >> 1 & 1)
+
+    chip = lax.axis_index(CHIPS).astype(jnp.int32)[None]
+    order = jnp.concatenate([order, chip])
+    weights = run_prepare(order, embed, w_own, w_other, out_own, out_other, w_read)
+    got, weights, gain_row = lax.optimization_barrier((got, weights, gain_row))
+    got = got.reshape(-1, got.shape[2])
 
     chips = lax.axis_size(CHIPS)
     copies = jnp.dot(
         jnp.tile(place, (chips, 1)), got, preferred_element_type=jnp.float32
     ).astype(jnp.bfloat16)
-    copies, embed = lax.optimization_barrier((copies, embed))
     samples = swap(copies, CHIPS)
 
-    samples_other = swap_cores(samples)
-    weights = (embed, gain_row, w_qkv, w_out, w_read)
-    normed, proj, prob, pred, base = run_forward(samples, *weights, own=True)
-    normed_other, proj_other, prob_other, pred_other = run_forward(
-        samples_other, *weights, own=False
-    )
-    chip_pred = (pred + swap_cores(pred_other).astype(jnp.float32)).astype(jnp.bfloat16)
-    shares = spread(chip_pred, CHIPS).reshape((chips,) + base.shape)
+    normed, proj, prob, pred = run_forward(chip, samples, weights, gain_row)
+    shares = spread(pred, CHIPS).reshape((chips,) + pred.shape)
     row_count = lax.axis_size(GROUP) * SPD
     loss_scale = math.sqrt(
         w_read.shape[0] / (lax.axis_size(SPACE) * row_count * w_read.shape[1])
     )
-    delta = run_delta(shares, base, loss_scale)
-
-    delta_other = swap_cores(delta)
-    half = run_backward(delta, w_out, w_read, proj, prob, normed, None)
-    grads = run_backward(
-        delta_other, w_out, w_read, proj_other, prob_other, normed_other, half
-    )
+    delta = run_delta(shares, samples, loss_scale)
+
+    saved = (weights, proj, prob, normed)
+    grads_other = swap_cores(run_backward(delta, *saved, head=1))
+    grads = (
+        run_backward(delta, *saved, head=0).astype(jnp.float32) + grads_other.astype(jnp.float32)
+    ).astype(jnp.bfloat16)
 
     gain_share = (
         jnp.sum(w_qkv.astype(jnp.float32) * grads.astype(jnp.float32), axis=(0, 2))

time: 216 us -> 207 us (0.958)
  blocking collectives: 93.8 us -> 86.6 us
  starting transfers between devices: 57 us -> 62.2 us
  Pallas kernels: 20.6 us -> 16.4 us
  other arithmetic: 8.52 us -> 4.95 us
  local copies, waits for them, and re-layouts: 8.33 us -> 11 us
    all_to_all x5, blocking collectives: 93.8 us -> 86.6 us  [swap(): return lax.all_to_all(parts, axis, split_axis=0, concat_axis=0, tiled=True)]
    all_to_all x2, starting transfers between devices: 21.3 us -> 26.7 us  [swap(): return lax.all_to_all(parts, axis, split_axis=0, concat_axis=0, tiled=True)]
    unnamed x17 -> x29, local copies, waits for them, and re-layouts: 0.05 us -> 4.29 us
    pallas_call x4, Pallas kernels: 16.4 us -> 12.2 us  [the longest x1 6.01 us: run_forward(): pl.pallas_call(forward_kernel, out_shape=shapes, in_specs=[SMEM] + [VMEM]...]
    all_to_all x2, waiting for transfers between devices: 15.8 us -> 11.7 us  [swap(): return lax.all_to_all(parts, axis, split_axis=0, concat_axis=0, tiled=True)]
    ppermute x10, waiting for transfers between devices: 8.83 us -> 11.3 us  [swap_with(): return lax.ppermute(own, axis, [(0, 1), (1, 0)])]
    reshape x2 -> x4, local copies, waits for them, and re-layouts: 0.1 us -> 2.48 us  [the longest x1 1.05 us: shards(): got = got.reshape(-1, got.shape[2])]
  transfers between devices with their start and end apart: 14 -> 14, of which waited for: 6 -> 8; matrix products, arithmetic and copies ran while one was open for 5% -> 2% of each run, Pallas kernels for 6% -> 4%
where the time goes in v5:
time: 207 us; the launch traced here: 206 us
  blocking collectives  86.6 us (42%)
  starting transfers between devices  62.2 us (30%)
  waiting for transfers between devices  23.1 us (11%)
  Pallas kernels  16.4 us (8%)
  local copies, waits for them, and re-layouts  11 us (5%)
  other arithmetic  4.95 us (2%)
    all_to_all x5, blocking collectives, swap(): return lax.all_to_all(parts, axis, split_axis=0, concat_axis=0, tiled=True)  86.6 us
    ppermute x10, starting transfers between devices, swap_with(): return lax.ppermute(own, axis, [(0, 1), (1, 0)])  27.5 us
    all_to_all x2, starting transfers between devices, swap(): return lax.all_to_all(parts, axis, split_axis=0, concat_axis=0, tiled=True)  26.7 us
    all_to_all x2, waiting for transfers between devices, swap(): return lax.all_to_all(parts, axis, split_axis=0, concat_axis=0, tiled=True)  11.7 us
    ppermute x10, waiting for transfers between devices, swap_with(): return lax.ppermute(own, axis, [(0, 1), (1, 0)])  11.3 us
    pallas_call x1, Pallas kernels, run_forward(): pl.pallas_call(forward_kernel, out_shape=shapes, in_specs=[SMEM] + [VMEM]...  6.01 us
    ppermute x1, starting transfers between devices, halos(): high = lax.ppermute(bottom, SPACE, backward)  4.55 us
    pallas_call x2, Pallas kernels, run_backward(): pl.pallas_call(functools.partial(backward_kernel, head=head), out_shape=j...  4.39 us
  transfers between devices with their start and end apart: 14, of which 8 were waited for; matrix products, arithmetic and copies ran while one was open for 2% of the time, Pallas kernels for 4%

profile of v5, /device:TPU:32, one launch (start us, length us, event | category | flops | bytes accessed | tf_op | source)
XLA Modules:
  0.0 205.8 jit_solution(513386672141746119)
XLA Ops:
  0.7 1.0 slice_bitcast_fusion
  1.8 1.0 convert_bitcast_fusion
  2.8 3.5 %collective-permute-start = (f32[2,16,3,256]{3,2,1,0:T(4,128)S(1)}, f32[2,16,3,256]{3,2,1,0:T(4,128)S(1)}, u32[]{:S(2)}, u32[]{:S(2)}) collective-permute-start(f32[2,16,3,256]{3,2,1,0:T(4,128)S(1)} %maximum_select_fusion), channel_id=1, source_target_pairs={{0,256},{256,0},{1,257},{257,1},{2,258},{258,2},{3,259},{259,3},{4... | collective-permute-start | bytes 294920 | tf_op jit(solution)/shard_map/ppermute | solution.py:40
  6.3 0.8 fusion.5
  7.8 2.2 %collective-permute-done.side_ref = f32[2,16,3,256]{3,2,1,0:T(4,128)S(1)} collective-permute-done((f32[2,16,3,256]{3,2,1,0:T(4,128)S(1)}, f32[2,16,3,256]{3,2,1,0:T(4,128)S(1)}, u32[]{:S(2)}, u32[]{:S(2)}) %collective-permute-start) | collective-permute-done | bytes 98336 | tf_op jit(solution)/shard_map/ppermute | solution.py:40
  10.0 3.4 %collective-permute-start.1 = (f32[2,3,22,256]{3,2,1,0:T(8,128)S(1)}, f32[2,3,22,256]{3,2,1,0:T(8,128)S(1)}, u32[]{:S(2)}, u32[]{:S(2)}) collective-permute-start(f32[2,3,22,256]{3,2,1,0:T(8,128)S(1)} %pad_maximum_fusion.5), channel_id=1, source_target_pairs={{0,4},{4,8},{8,12},{12,16},{16,20},{20,24},{24,28},{28,32},{32,36}... | collective-permute-start | bytes 405512 | tf_op jit(solution)/shard_map/ppermute | solution.py:70
  13.4 4.6 %collective-permute-start.2 = (f32[2,3,22,256]{3,2,1,0:T(8,128)S(1)}, f32[2,3,22,256]{3,2,1,0:T(8,128)S(1)}, u32[]{:S(2)}, u32[]{:S(2)}) collective-permute-start(f32[2,3,22,256]{3,2,1,0:T(8,128)S(1)} %pad_maximum_fusion.6), channel_id=1, source_target_pairs={{4,0},{8,4},{12,8},{16,12},{20,16},{24,20},{28,24},{32,28},{36,32}... | collective-permute-start | bytes 405512 | tf_op jit(solution)/shard_map/ppermute | solution.py:71
  18.0 5.1 %collective-permute-start.3 = (bf16[192,512]{1,0:T(8,128)(2,1)S(1)}, bf16[192,512]{1,0:T(8,128)(2,1)S(1)}, u32[]{:S(2)}, u32[]{:S(2)}) collective-permute-start(bf16[192,512]{1,0:T(8,128)(2,1)S(1)} %bitcast.61), channel_id=1, source_target_pairs={{0,2},{2,0},{1,3},{3,1},{4,6},{6,4},{5,7},{7,5},{8,10},{10,8},{9,1... | collective-permute-start | bytes 589832 | tf_op jit(solution)/shard_map/ppermute | solution.py:40
  23.3 4.1 %slab.1 = (f32[16,16,256]{2,1,0:T(8,128)}, bf16[256,640]{1,0:T(8,128)(2,1)S(1)}) custom-call(s32[2]{0:T(128)S(1)} %pad_add_fusion.place_ref, f32[8]{0:T(128)S(1)} %bitcast.51, f32[16,16,256]{2,1,0:T(8,128)S(1)} %bitcast.50, s32[16,16,256]{2,1,0:T(8,128)S(1)} %copy-done.5, f32[2,16,3,256]{3,2,1,0:T(4,128)S(1)} %collective-permute-done.side_ref, ...), custom_call_target="tpu_custom_call" | custom-call | tf_op jit(solution)/shard_map/slab/pallas_call | solution.py:240
  27.5 3.1 %collective-permute-start.4 = (bf16[2,192,512]{2,1,0:T(8,128)(2,1)S(1)}, bf16[2,192,512]{2,1,0:T(8,128)(2,1)S(1)}, u32[]{:S(2)}, u32[]{:S(2)}) collective-permute-start(bf16[2,192,512]{2,1,0:T(8,128)(2,1)S(1)} %pad_maximum_fusion.3), channel_id=1, source_target_pairs={{0,256},{256,0},{1,257},{257,1},{2,258},{258,2},{3,259},{259,3},{4... | collective-permute-start | bytes 1179656 | tf_op jit(solution)/shard_map/ppermute | solution.py:40
  30.6 0.8 reshape.103
  31.4 18.1 %all-to-all-start = ((bf16[64,4,640]{2,1,0:T(4,128)(2,1)}), bf16[64,4,640]{2,1,0:T(4,128)(2,1)}, u32[]{:S(2)}, u32[]{:S(2)}) async-start(bf16[64,4,640]{2,1,0:T(4,128)(2,1)} %reshape.103), calls=%async_computation | async-start | bytes 655360 | tf_op jit(solution)/shard_map/all_to_all | solution.py:31
  49.6 1.9 collective-permute-start.6
  51.6 2.4 %collective-permute-start.5 = (bf16[2,2,192,512]{3,2,1,0:T(8,128)(2,1)S(1)}, bf16[2,2,192,512]{3,2,1,0:T(8,128)(2,1)S(1)}, u32[]{:S(2)}, u32[]{:S(2)}) collective-permute-start(bf16[2,2,192,512]{3,2,1,0:T(8,128)(2,1)S(1)} %pad_maximum_fusion.2), channel_id=1, source_target_pairs={{0,1},{1,0},{2,3},{3,2},{4,5},{5,4},{6,7},{7,6},{8,9},{9,8},{10,11... | collective-permute-start | bytes 2359304 | tf_op jit(solution)/shard_map/ppermute | solution.py:40
  54.0 0.7 fusion.4
  54.8 0.7 multiply_add_fusion
  55.4 1.9 collective-permute-start.7
  57.4 0.7 fusion.2
  58.3 0.7 collective-permute-done.7.out_other_ref
  59.1 1.8 prepare.1.all_ref
  60.9 1.9 copy-done
  62.9 8.7 %all-to-all-done = bf16[64,4,640]{2,1,0:T(4,128)(2,1)} async-done(((bf16[64,4,640]{2,1,0:T(4,128)(2,1)}), bf16[64,4,640]{2,1,0:T(4,128)(2,1)}, u32[]{:S(2)}, u32[]{:S(2)}) %all-to-all-start) | async-done | bytes 327712 | tf_op jit(solution)/shard_map/all_to_all | solution.py:31
  71.6 1.1 reshape.105
  72.7 0.4 convolution_convert_fusion
  73.0 12.5 %all_to_all.41 = bf16[4,128,640]{2,1,0:T(8,128)(2,1)S(1)} all-to-all(bf16[4,128,640]{2,1,0:T(8,128)(2,1)S(1)} %bitcast.54), channel_id=1, replica_groups=mesh['grp'=2,'z'=16,'x'=4,'yhi'=2,'core'=2] {'grp','yhi'}, dimensions={0} | all-to-all | bytes 1310720 | tf_op jit(solution)/shard_map/all_to_all | solution.py:31
  85.5 2.2 %copy-done.1 = bf16[512,4096]{1,0:T(8,128)(2,1)S(1)} copy-done((bf16[512,4096]{1,0:T(8,128)(2,1)S(1)}, bf16[512,4096]{1,0:T(8,128)(2,1)}, u32[]{:S(2)}) %copy-start.1) | copy-done | bytes 4194328
  87.7 6.0 %forward.1 = (bf16[512,1536]{1,0:T(8,128)(2,1)S(1)}, bf16[512,768]{1,0:T(8,128)(2,1)S(1)}, f32[512,256]{1,0:T(8,128)S(1)}, bf16[512,128]{1,0:T(8,128)(2,1)S(1)}) custom-call(s32[1]{0:T(128)} %bitcast.13.chip_ref, bf16[512,640]{1,0:T(8,128)(2,1)S(1)} %bitcast.47, bf16[512,4096]{1,0:T(8,128)(2,1)S(1)} %copy-done.1, f32[1,1536]{1,0:T(1,128)S(1)} %broadcast_in_dim.68.gain_ref), custom_call_target="tpu_custom_call" | custom-call | flops 2013265920 | bytes 6291456 | tf_op jit(solution)/shard_map/forward/pallas_call | solution.py:396
  93.8 10.3 %all_to_all.42.share_ref = bf16[4,512,128]{2,1,0:T(8,128)(2,1)S(1)} all-to-all(bf16[4,512,128]{2,1,0:T(8,128)(2,1)S(1)} %broadcast_in_dim.69), channel_id=1, replica_groups=mesh['grp'=2,'z'=16,'x'=4,'yhi'=2,'core'=2] {'grp','yhi'}, dimensions={0} | all-to-all | bytes 1048576 | tf_op jit(solution)/shard_map/all_to_all | solution.py:31
  104.2 2.2 %backward_other.1 = bf16[3,1536,128]{2,1,0:T(8,128)(2,1)S(1)} custom-call(bf16[512,128]{1,0:T(8,128)(2,1)S(1)} %delta.1.delta_ref, bf16[512,4096]{1,0:T(8,128)(2,1)S(1)} %copy-done.2, bf16[512,768]{1,0:T(8,128)(2,1)S(1)} %get-tuple-element.32.proj_ref, f32[512,256]{1,0:T(8,128)S(1)} %get-tuple-element.33.prob_ref, ...), custom_call_target="tpu_custom_call" | custom-call | flops 603979776 | bytes 3145728 | tf_op jit(solution)/shard_map/backward_other/pallas_call | solution.py:474
  106.4 1.9 collective-permute-start.8
  108.3 2.2 %backward_own.1 = bf16[3,1536,128]{2,1,0:T(8,128)(2,1)S(1)} custom-call(bf16[512,128]{1,0:T(8,128)(2,1)S(1)} %delta.1.delta_ref, bf16[512,4096]{1,0:T(8,128)(2,1)S(1)} %copy-done.2, bf16[512,768]{1,0:T(8,128)(2,1)S(1)} %get-tuple-element.32.proj_ref, f32[512,256]{1,0:T(8,128)S(1)} %get-tuple-element.33.prob_ref, ...), custom_call_target="tpu_custom_call" | custom-call | flops 603979776 | bytes 3145728 | tf_op jit(solution)/shard_map/backward_own/pallas_call | solution.py:474
  110.5 0.6 collective-permute-done.8
  111.2 0.6 multiply_reduce_fusion
  111.9 19.6 %all_to_all.43 = bf16[4,1155,128]{2,1,0:T(8,128)(2,1)S(1)} all-to-all(bf16[4,1155,128]{2,1,0:T(8,128)(2,1)S(1)} %pad_maximum_fusion.1), channel_id=1, replica_groups=mesh['grp'=2,'z'=16,'x'=4,'yhi'=2,'core'=2] {'x'}, dimensions={0} | all-to-all | bytes 2365440 | tf_op jit(solution)/shard_map/all_to_all | solution.py:31
  131.5 0.2 convert_reduce_fusion
  131.7 0.7 slice.92
  132.5 8.6 %all-to-all-start.4 = ((bf16[16,72,128]{2,1,0:T(8,128)(2,1)}), bf16[16,72,128]{2,1,0:T(8,128)(2,1)S(1)}, u32[]{:S(2)}, u32[]{:S(2)}) async-start(bf16[16,72,128]{2,1,0:T(8,128)(2,1)} %bitcast.26), calls=%async_computation.4 | async-start | bytes 589824 | tf_op jit(solution)/shard_map/all_to_all | solution.py:31
  141.0 1.9 collective-permute-start.9
  143.0 1.1 collective-permute-done.9
  144.1 2.4 %collective-permute-start.10 = (f32[3,128]{1,0:T(4,128)S(1)}, f32[3,128]{1,0:T(4,128)S(1)}, u32[]{:S(2)}, u32[]{:S(2)}) collective-permute-start(f32[3,128]{1,0:T(4,128)S(1)} %slice_add_fusion), channel_id=1, source_target_pairs={{0,256},{256,0},{1,257},{257,1},{2,258},{258,2},{3,259},{259,3},{4... | collective-permute-start | bytes 4616 | tf_op jit(solution)/shard_map/ppermute | solution.py:40
  146.5 3.1 %collective-permute-done.10 = f32[3,128]{1,0:T(4,128)S(1)} collective-permute-done((f32[3,128]{1,0:T(4,128)S(1)}, f32[3,128]{1,0:T(4,128)S(1)}, u32[]{:S(2)}, u32[]{:S(2)}) %collective-permute-start.10) | collective-permute-done | bytes 1568 | tf_op jit(solution)/shard_map/ppermute | solution.py:40
  149.6 3.4 %collective-permute-start.11 = (f32[3,128]{1,0:T(4,128)S(1)}, f32[3,128]{1,0:T(4,128)S(1)}, u32[]{:S(2)}, u32[]{:S(2)}) collective-permute-start(f32[3,128]{1,0:T(4,128)S(1)} %add.75), channel_id=1, source_target_pairs={{0,2},{2,0},{1,3},{3,1},{4,6},{6,4},{5,7},{7,5},{8,10},{10,8},{9,1... | collective-permute-start | bytes 4616 | tf_op jit(solution)/shard_map/ppermute | solution.py:40
  152.9 3.6 %collective-permute-done.11 = f32[3,128]{1,0:T(4,128)S(1)} collective-permute-done((f32[3,128]{1,0:T(4,128)S(1)}, f32[3,128]{1,0:T(4,128)S(1)}, u32[]{:S(2)}, u32[]{:S(2)}) %collective-permute-start.11) | collective-permute-done | bytes 1568 | tf_op jit(solution)/shard_map/ppermute | solution.py:40
  156.5 3.0 %all-to-all-done.4 = bf16[16,72,128]{2,1,0:T(8,128)(2,1)S(1)} async-done(((bf16[16,72,128]{2,1,0:T(8,128)(2,1)}), bf16[16,72,128]{2,1,0:T(8,128)(2,1)S(1)}, u32[]{:S(2)}, u32[]{:S(2)}) %all-to-all-start.4) | async-done | bytes 294944 | tf_op jit(solution)/shard_map/all_to_all | solution.py:31
  159.7 27.3 %all_to_all.44 = bf16[16,75,128]{2,1,0:T(8,128)(2,1)S(1)} all-to-all(bf16[16,75,128]{2,1,0:T(8,128)(2,1)S(1)} %broadcast_in_dim.70), channel_id=1, replica_groups=mesh['grp'=2,'z'=16,'x'=4,'yhi'=2,'core'=2] {'z'}, dimensions={0} | all-to-all | bytes 614400 | tf_op jit(solution)/shard_map/all_to_all | solution.py:31
  187.2 16.9 %all_to_all.45 = bf16[4,1155,128]{2,1,0:T(8,128)(2,1)S(1)} all-to-all(bf16[4,1155,128]{2,1,0:T(8,128)(2,1)S(1)} %broadcast_in_dim.71), channel_id=1, replica_groups=mesh['grp'=2,'z'=16,'x'=4,'yhi'=2,'core'=2] {'x'}, dimensions={0} | all-to-all | bytes 2365440 | tf_op jit(solution)/shard_map/all_to_all | solution.py:31
  204.1 0.6 reshape.141
  204.8 1.1 slice.80
  (72 shorter events, 2.1 us)
Async XLA Ops:
  0.6 6.5 %copy-start.5 = (s32[16,16,256]{2,1,0:T(8,128)S(1)}, s32[16,16,256]{2,1,0:T(8,128)}, u32[]{:S(2)}) copy-start(s32[16,16,256]{2,1,0:T(8,128)} %material_ref.1) | copy-start | bytes 786436
  0.6 6.5 %copy-start.11 = (s32[1,1,64,128,1]{3,4,2,1,0:T(1,128)S(1)}, s32[1,1,64,128,1]{3,4,2,1,0:T(1,128)}, u32[]{:S(2)}) copy-start(s32[1,1,64,128,1]{3,4,2,1,0:T(1,128)} %param.13) | copy-start | bytes 98308
  0.7 6.7 %copy-start.13 = (s32[1,1,64,128]{3,2,1,0:T(8,128)S(1)}, s32[1,1,64,128]{3,2,1,0:T(8,128)}, u32[]{:S(2)}) copy-start(s32[1,1,64,128]{3,2,1,0:T(8,128)} %param.14) | copy-start | bytes 98308
  0.7 17.3 %copy-start.10 = (bf16[512,192]{0,1:T(8,128)(2,1)S(1)}, bf16[512,192]{0,1:T(8,128)(2,1)}, u32[]{:S(2)}) copy-start(bf16[512,192]{0,1:T(8,128)(2,1)} %param.15) | copy-start | bytes 589828
  0.7 22.6 %copy-start.4 = (f32[1,16,16,256]{3,2,1,0:T(8,128)S(1)}, f32[1,16,16,256]{3,2,1,0:T(8,128)}, u32[]{:S(2)}) copy-start(f32[1,16,16,256]{3,2,1,0:T(8,128)} %param.10) | copy-start | bytes 786436
  0.7 22.6 %copy-start.8 = (f32[1,8]{1,0:T(1,128)S(1)}, f32[1,8]{1,0:T(1,128)}, u32[]{:S(2)}) copy-start(f32[1,8]{1,0:T(1,128)} %param.12) | copy-start | bytes 100
  2.8 7.1 %collective-permute-start = (f32[2,16,3,256]{3,2,1,0:T(4,128)S(1)}, f32[2,16,3,256]{3,2,1,0:T(4,128)S(1)}, u32[]{:S(2)}, u32[]{:S(2)}) collective-permute-start(f32[2,16,3,256]{3,2,1,0:T(4,128)S(1)} %maximum_select_fusion), channel_id=1, source_target_pairs={{0,256},{256,0},{1,257},{257,1},{2,258},{258,2},{3,259},{259,3},{4... | collective-permute-start | bytes 294920 | tf_op jit(solution)/shard_map/ppermute | solution.py:40
  10.0 13.3 %collective-permute-start.1 = (f32[2,3,22,256]{3,2,1,0:T(8,128)S(1)}, f32[2,3,22,256]{3,2,1,0:T(8,128)S(1)}, u32[]{:S(2)}, u32[]{:S(2)}) collective-permute-start(f32[2,3,22,256]{3,2,1,0:T(8,128)S(1)} %pad_maximum_fusion.5), channel_id=1, source_target_pairs={{0,4},{4,8},{8,12},{12,16},{16,20},{20,24},{24,28},{28,32},{32,36}... | collective-permute-start | bytes 405512 | tf_op jit(solution)/shard_map/ppermute | solution.py:70
  13.4 9.9 %collective-permute-start.2 = (f32[2,3,22,256]{3,2,1,0:T(8,128)S(1)}, f32[2,3,22,256]{3,2,1,0:T(8,128)S(1)}, u32[]{:S(2)}, u32[]{:S(2)}) collective-permute-start(f32[2,3,22,256]{3,2,1,0:T(8,128)S(1)} %pad_maximum_fusion.6), channel_id=1, source_target_pairs={{4,0},{8,4},{12,8},{16,12},{20,16},{24,20},{28,24},{32,28},{36,32}... | collective-permute-start | bytes 405512 | tf_op jit(solution)/shard_map/ppermute | solution.py:71
  18.0 9.4 %collective-permute-start.3 = (bf16[192,512]{1,0:T(8,128)(2,1)S(1)}, bf16[192,512]{1,0:T(8,128)(2,1)S(1)}, u32[]{:S(2)}, u32[]{:S(2)}) collective-permute-start(bf16[192,512]{1,0:T(8,128)(2,1)S(1)} %bitcast.61), channel_id=1, source_target_pairs={{0,2},{2,0},{1,3},{3,1},{4,6},{6,4},{5,7},{7,5},{8,10},{10,8},{9,1... | collective-permute-start | bytes 589832 | tf_op jit(solution)/shard_map/ppermute | solution.py:40
  27.5 22.0 %collective-permute-start.4 = (bf16[2,192,512]{2,1,0:T(8,128)(2,1)S(1)}, bf16[2,192,512]{2,1,0:T(8,128)(2,1)S(1)}, u32[]{:S(2)}, u32[]{:S(2)}) collective-permute-start(bf16[2,192,512]{2,1,0:T(8,128)(2,1)S(1)} %pad_maximum_fusion.3), channel_id=1, source_target_pairs={{0,256},{256,0},{1,257},{257,1},{2,258},{258,2},{3,259},{259,3},{4... | collective-permute-start | bytes 1179656 | tf_op jit(solution)/shard_map/ppermute | solution.py:40
  31.4 18.2 %copy-start.3 = (bf16[3,1536,128]{2,1,0:T(8,128)(2,1)S(1)}, bf16[3,1536,128]{2,1,0:T(8,128)(2,1)}, u32[]{:S(2)}) copy-start(bf16[3,1536,128]{2,1,0:T(8,128)(2,1)} %w_own_ref) | copy-start | bytes 3538948
  31.4 24.0 %copy-start.6 = (bf16[128,1536]{1,0:T(8,128)(2,1)S(1)}, bf16[128,1536]{1,0:T(8,128)(2,1)}, u32[]{:S(2)}) copy-start(bf16[128,1536]{1,0:T(8,128)(2,1)} %out_own_ref) | copy-start | bytes 1179652
  31.4 26.0 %copy-start.12 = (f32[1536]{0:T(1024)S(1)}, f32[1536]{0:T(1024)}, u32[]{:S(2)}) copy-start(f32[1536]{0:T(1024)} %param.16) | copy-start | bytes 18436
  31.4 40.2 %all-to-all-start = ((bf16[64,4,640]{2,1,0:T(4,128)(2,1)}), bf16[64,4,640]{2,1,0:T(4,128)(2,1)}, u32[]{:S(2)}, u32[]{:S(2)}) async-start(bf16[64,4,640]{2,1,0:T(4,128)(2,1)} %reshape.103), calls=%async_computation | async-start | bytes 655360 | tf_op jit(solution)/shard_map/all_to_all | solution.py:31
  49.6 9.4 %collective-permute-start.6 = (bf16[3,1536,128]{2,1,0:T(8,128)(2,1)S(1)}, bf16[3,1536,128]{2,1,0:T(8,128)(2,1)S(1)}, u32[]{:S(2)}, u32[]{:S(2)}) collective-permute-start(bf16[3,1536,128]{2,1,0:T(8,128)(2,1)S(1)} %copy-done.3), channel_id=1, source_target_pairs={{0,1},{1,0},{2,3},{3,2},{4,5},{5,4},{6,7},{7,6},{8,9},{9,8},{10,11... | collective-permute-start | bytes 3538952 | tf_op jit(solution)/shard_map/ppermute | solution.py:40
  51.6 6.6 %collective-permute-start.5 = (bf16[2,2,192,512]{3,2,1,0:T(8,128)(2,1)S(1)}, bf16[2,2,192,512]{3,2,1,0:T(8,128)(2,1)S(1)}, u32[]{:S(2)}, u32[]{:S(2)}) collective-permute-start(bf16[2,2,192,512]{3,2,1,0:T(8,128)(2,1)S(1)} %pad_maximum_fusion.2), channel_id=1, source_target_pairs={{0,1},{1,0},{2,3},{3,2},{4,5},{5,4},{6,7},{7,6},{8,9},{9,8},{10,11... | collective-permute-start | bytes 2359304 | tf_op jit(solution)/shard_map/ppermute | solution.py:40
  55.4 3.6 %collective-permute-start.7 = (bf16[128,1536]{1,0:T(8,128)(2,1)S(1)}, bf16[128,1536]{1,0:T(8,128)(2,1)S(1)}, u32[]{:S(2)}, u32[]{:S(2)}) collective-permute-start(bf16[128,1536]{1,0:T(8,128)(2,1)S(1)} %copy-done.6), channel_id=1, source_target_pairs={{0,1},{1,0},{2,3},{3,2},{4,5},{5,4},{6,7},{7,6},{8,9},{9,8},{10,11... | collective-permute-start | bytes 1179656 | tf_op jit(solution)/shard_map/ppermute | solution.py:40
  58.1 1.0 copy-start.7
  59.1 13.5 %copy-start.9 = (bf16[128,256]{1,0:T(8,128)(2,1)S(1)}, bf16[128,256]{1,0:T(8,128)(2,1)}, u32[]{:S(2)}) copy-start(bf16[128,256]{1,0:T(8,128)(2,1)} %fusion.2) | copy-start | bytes 196612
  60.9 1.9 copy-start
  85.5 2.2 %copy-start.1 = (bf16[512,4096]{1,0:T(8,128)(2,1)S(1)}, bf16[512,4096]{1,0:T(8,128)(2,1)}, u32[]{:S(2)}) copy-start(bf16[512,4096]{1,0:T(8,128)(2,1)} %copy-done) | copy-start | bytes 12582916
  87.7 16.5 %copy-start.2 = (bf16[512,4096]{1,0:T(8,128)(2,1)S(1)}, bf16[512,4096]{1,0:T(8,128)(2,1)}, u32[]{:S(2)}) copy-start(bf16[512,4096]{1,0:T(8,128)(2,1)} %copy-done) | copy-start | bytes 12582916
  106.4 4.7 %collective-permute-start.8 = (bf16[3,1536,128]{2,1,0:T(8,128)(2,1)S(1)}, bf16[3,1536,128]{2,1,0:T(8,128)(2,1)S(1)}, u32[]{:S(2)}, u32[]{:S(2)}) collective-permute-start(bf16[3,1536,128]{2,1,0:T(8,128)(2,1)S(1)} %backward_other.1), channel_id=1, source_target_pairs={{0,1},{1,0},{2,3},{3,2},{4,5},{5,4},{6,7},{7,6},{8,9},{9,8},{10,11... | collective-permute-start | bytes 3538952 | tf_op jit(solution)/shard_map/ppermute | solution.py:40
  132.5 27.1 %all-to-all-start.4 = ((bf16[16,72,128]{2,1,0:T(8,128)(2,1)}), bf16[16,72,128]{2,1,0:T(8,128)(2,1)S(1)}, u32[]{:S(2)}, u32[]{:S(2)}) async-start(bf16[16,72,128]{2,1,0:T(8,128)(2,1)} %bitcast.26), calls=%async_computation.4 | async-start | bytes 589824 | tf_op jit(solution)/shard_map/all_to_all | solution.py:31
  141.0 3.1 %collective-permute-start.9 = (f32[3,128]{1,0:T(4,128)S(1)}, f32[3,128]{1,0:T(4,128)S(1)}, u32[]{:S(2)}, u32[]{:S(2)}) collective-permute-start(f32[3,128]{1,0:T(4,128)S(1)} %slice.77), channel_id=1, source_target_pairs={{0,1},{1,0},{2,3},{3,2},{4,5},{5,4},{6,7},{7,6},{8,9},{9,8},{10,11... | collective-permute-start | bytes 4616 | tf_op jit(solution)/shard_map/ppermute | solution.py:40
  144.1 5.5 %collective-permute-start.10 = (f32[3,128]{1,0:T(4,128)S(1)}, f32[3,128]{1,0:T(4,128)S(1)}, u32[]{:S(2)}, u32[]{:S(2)}) collective-permute-start(f32[3,128]{1,0:T(4,128)S(1)} %slice_add_fusion), channel_id=1, source_target_pairs={{0,256},{256,0},{1,257},{257,1},{2,258},{258,2},{3,259},{259,3},{4... | collective-permute-start | bytes 4616 | tf_op jit(solution)/shard_map/ppermute | solution.py:40
  149.6 7.0 %collective-permute-start.11 = (f32[3,128]{1,0:T(4,128)S(1)}, f32[3,128]{1,0:T(4,128)S(1)}, u32[]{:S(2)}, u32[]{:S(2)}) collective-permute-start(f32[3,128]{1,0:T(4,128)S(1)} %add.75), channel_id=1, source_target_pairs={{0,2},{2,0},{1,3},{3,1},{4,6},{6,4},{5,7},{7,5},{8,10},{10,8},{9,1... | collective-permute-start | bytes 4616 | tf_op jit(solution)/shard_map/ppermute | solution.py:40

commit v6 on v5

--- a/solution.py
+++ b/solution.py
@@ -24,6 +24,7 @@
 VMEM = pl.BlockSpec(memory_space=pltpu.VMEM)
 SMEM = pl.BlockSpec(memory_space=pltpu.SMEM)
 LIMIT = 20 * 1024 * 1024
+FORWARD_LIMIT = 48 * 1024 * 1024
 EXACT = lax.Precision.HIGHEST
 
 
@@ -332,11 +333,22 @@
 
 
 def forward_kernel(
-    chip_ref, sample_ref, all_ref, gain_ref, normed_ref, proj_ref, prob_ref, pred_ref, embed_ref
+    chip_ref, sample_ref, all_hbm, gain_ref,
+    normed_ref, proj_ref, prob_ref, pred_ref, mix_ref,
+    embed_ref, all_ref, sems,
 ):
     token_width = all_ref.shape[0]
     model = normed_ref.shape[1]
-    heads, mix, read, _ = layout(token_width, model)
+    heads, mix, read, end = layout(token_width, model)
+    fetches = [
+        pltpu.make_async_copy(
+            all_hbm.at[:, pl.ds(start, size)], all_ref.at[:, pl.ds(start, size)], sems.at[i]
+        )
+        for i, (start, size) in enumerate(((0, model), (model, mix - model), (mix, end - mix)))
+    ]
+    for fetch in fetches:
+        fetch.start()
+    fetches[0].wait()
     across = (((1,), (1,)), ((), ()))
     embedded = jnp.dot(
         sample_ref[:, :token_width], all_ref[:, :model], preferred_element_type=jnp.float32
@@ -348,6 +360,9 @@
     variance = jnp.mean(removed * removed, axis=1, keepdims=True)
     normed = (removed * lax.rsqrt(variance + NORM_EPSILON) * gain_ref[...]).astype(jnp.bfloat16)
     normed_ref[...] = normed
+    fetches[1].wait()
+    fetches[2].wait()
+    mix_ref[...] = all_ref[:, mix:read]
     proj_w = jnp.concatenate(
         [all_ref[:, start : start + heads] for start in range(model, mix, heads)], axis=0
     )
@@ -392,14 +407,19 @@
         jax.ShapeDtypeStruct((rows, heads), jnp.bfloat16),
         jax.ShapeDtypeStruct((rows, 2 * SPD), jnp.float32),
         jax.ShapeDtypeStruct((rows, HD), jnp.bfloat16),
+        jax.ShapeDtypeStruct((weights.shape[0], HD), jnp.bfloat16),
     )
     return pl.pallas_call(
         forward_kernel,
         out_shape=shapes,
-        in_specs=[SMEM] + [VMEM] * 3,
+        in_specs=[SMEM, VMEM, pl.BlockSpec(memory_space=pl.ANY), VMEM],
         out_specs=(VMEM,) * len(shapes),
-        scratch_shapes=[pltpu.VMEM((rows, model), jnp.bfloat16)],
-        compiler_params=pltpu.CompilerParams(vmem_limit_bytes=LIMIT),
+        scratch_shapes=[
+            pltpu.VMEM((rows, model), jnp.bfloat16),
+            pltpu.VMEM(weights.shape, weights.dtype),
+            pltpu.SemaphoreType.DMA((3,)),
+        ],
+        compiler_params=pltpu.CompilerParams(vmem_limit_bytes=FORWARD_LIMIT),
         cost_estimate=pl.CostEstimate(
             flops=2 * rows * model * (weights.shape[0] + heads),
             bytes_accessed=rows * model * 8,
@@ -429,13 +449,12 @@
 
 
 def backward_kernel(
-    delta_ref, all_ref, proj_ref, prob_ref, normed_ref, grad_ref, *, head
+    delta_ref, mix_ref, proj_ref, prob_ref, normed_ref, grad_ref, *, head
 ):
-    _, mix, read, _ = layout(all_ref.shape[0], normed_ref.shape[1])
     across = (((1,), (1,)), ((), ()))
     down = (((0,), (0,)), ((), ()))
     delta = delta_ref[...]
-    mixing = [all_ref[(2 * i + head) * HD : (2 * i + head + 1) * HD, mix:read] for i in range(2)]
+    mixing = [mix_ref[(2 * i + head) * HD : (2 * i + head + 1) * HD, :] for i in range(2)]
     grad_attended = lax.dot_general(
         jnp.concatenate([delta, delta], axis=1),
         jnp.concatenate(mixing, axis=1),
@@ -467,10 +486,10 @@
         grad_ref[i] = total[:, i * HD : (i + 1) * HD].astype(grad_ref.dtype)
 
 
-def run_backward(delta, weights, proj, prob, normed, head):
+def run_backward(delta, mix, proj, prob, normed, head):
     rows, model = normed.shape
     heads = proj.shape[1] // 2
-    operands = (delta, weights, proj, prob, normed)
+    operands = (delta, mix, proj, prob, normed)
     return pl.pallas_call(
         functools.partial(backward_kernel, head=head),
         out_shape=jax.ShapeDtypeStruct((heads // HD, model, HD), jnp.bfloat16),
@@ -487,26 +506,27 @@
 def sum_over_devices(parts, gain):
     count_x, count_z = lax.axis_size("x"), lax.axis_size("z")
     shape, columns, width = parts.shape, parts.shape[-1], gain.shape[0]
-
-    sent = jnp.concatenate(
-        [
-            parts.reshape(count_x, -1, columns),
-            gain.astype(jnp.bfloat16).reshape(count_x, -1, columns),
-        ],
-        axis=1,
-    )
     extra = width // (count_x * columns)
-    part = jnp.sum(swap(sent, "x").astype(jnp.float32), axis=0)
-    gain = part[-extra:]
-    part = part[:-extra].astype(jnp.bfloat16).reshape(count_z, -1, columns)
-    total = jnp.sum(swap(part, "z").astype(jnp.float32), axis=0).astype(jnp.bfloat16)
+
+    def exchange(block, values, axis):
+        got = swap(jnp.concatenate([block, values.astype(jnp.bfloat16)], axis=1), axis)
+        return (
+            jnp.sum(got[:, :-extra].astype(jnp.float32), axis=0).astype(jnp.bfloat16),
+            jnp.sum(got[:, -extra:].astype(jnp.float32), axis=0),
+        )
+
+    part, gain = exchange(
+        parts.reshape(count_x, -1, columns), gain.reshape(count_x, extra, columns), "x"
+    )
+    total, gain = exchange(
+        part.reshape(count_z, -1, columns),
+        jnp.broadcast_to(gain, (count_z, extra, columns)),
+        "z",
+    )
+    got = spread(total, "z").reshape(-1, columns)
     for axis in ("core", "grp", "yhi"):
         gain = gain + swap_with(gain, axis)
-
-    sent = jnp.concatenate([total, gain.astype(jnp.bfloat16)], axis=0)
-    got = spread(sent, "z").reshape(count_z, -1, columns)
-    gain = jnp.sum(got[:, -extra:].astype(jnp.float32), axis=0)
-    sent = jnp.concatenate([got[:, :-extra].reshape(-1, columns), gain.astype(jnp.bfloat16)], axis=0)
+    sent = jnp.concatenate([got, gain.astype(jnp.bfloat16)], axis=0)
     got = spread(sent, "x").reshape(count_x, -1, columns)
     gain = got[:, -extra:].astype(jnp.float32)
     return got[:, :-extra].reshape(shape), gain.reshape(width)
@@ -554,7 +574,7 @@
     ).astype(jnp.bfloat16)
     samples = swap(copies, CHIPS)
 
-    normed, proj, prob, pred = run_forward(chip, samples, weights, gain_row)
+    normed, proj, prob, pred, mix = run_forward(chip, samples, weights, gain_row)
     shares = spread(pred, CHIPS).reshape((chips,) + pred.shape)
     row_count = lax.axis_size(GROUP) * SPD
     loss_scale = math.sqrt(
@@ -562,7 +582,7 @@
     )
     delta = run_delta(shares, samples, loss_scale)
 
-    saved = (weights, proj, prob, normed)
+    saved = (mix, proj, prob, normed)
     grads_other = swap_cores(run_backward(delta, *saved, head=1))
     grads = (
         run_backward(delta, *saved, head=0).astype(jnp.float32) + grads_other.astype(jnp.float32)

time: 207 us -> 206 us (level)
  blocking collectives: 86.6 us -> 89 us
  starting transfers between devices: 62.2 us -> 59.8 us
  local copies, waits for them, and re-layouts: 11 us -> 8.79 us
    all_to_all x2, starting transfers between devices: 26.7 us -> 24.3 us  [swap(): return lax.all_to_all(parts, axis, split_axis=0, concat_axis=0, tiled=True)]
    all_to_all x5, blocking collectives: 86.6 us -> 89 us  [swap(): return lax.all_to_all(parts, axis, split_axis=0, concat_axis=0, tiled=True)]
    unnamed x29 -> x25, local copies, waits for them, and re-layouts: 4.29 us -> 2.1 us
where the time goes in v6:
time: 206 us; the launch traced here: 205 us
  blocking collectives  89 us (43%)
  starting transfers between devices  59.8 us (29%)
  waiting for transfers between devices  22.7 us (11%)
  Pallas kernels  18.2 us (9%)
  local copies, waits for them, and re-layouts  8.79 us (4%)
  other arithmetic  4.96 us (2%)
    all_to_all x5, blocking collectives, swap(): return lax.all_to_all(parts, axis, split_axis=0, concat_axis=0, tiled=True)  89 us
    ppermute x10, starting transfers between devices, swap_with(): return lax.ppermute(own, axis, [(0, 1), (1, 0)])  27.5 us
    all_to_all x2, starting transfers between devices, swap(): return lax.all_to_all(parts, axis, split_axis=0, concat_axis=0, tiled=True)  24.3 us
    ppermute x10, waiting for transfers between devices, swap_with(): return lax.ppermute(own, axis, [(0, 1), (1, 0)])  11.3 us
    all_to_all x2, waiting for transfers between devices, swap(): return lax.all_to_all(parts, axis, split_axis=0, concat_axis=0, tiled=True)  11.3 us
    pallas_call x1, Pallas kernels, run_forward(): pl.pallas_call(forward_kernel, out_shape=shapes, in_specs=[SMEM, VMEM, pl...  7.79 us
    ppermute x1, starting transfers between devices, halos(): high = lax.ppermute(bottom, SPACE, backward)  4.55 us
    pallas_call x2, Pallas kernels, run_backward(): pl.pallas_call(functools.partial(backward_kernel, head=head), out_shape=j...  4.39 us
  transfers between devices with their start and end apart: 14, of which 8 were waited for; matrix products, arithmetic and copies ran while one was open for 2% of the time, Pallas kernels for 4%

profile of v6, /device:TPU:32, one launch (start us, length us, event | category | flops | bytes accessed | tf_op | source)
XLA Modules:
  0.0 205.0 jit_solution(11811825949315890568)
XLA Ops:
  0.7 1.0 slice_bitcast_fusion
  1.8 1.0 convert_bitcast_fusion
  2.8 3.5 %collective-permute-start = (f32[2,16,3,256]{3,2,1,0:T(4,128)S(1)}, f32[2,16,3,256]{3,2,1,0:T(4,128)S(1)}, u32[]{:S(2)}, u32[]{:S(2)}) collective-permute-start(f32[2,16,3,256]{3,2,1,0:T(4,128)S(1)} %maximum_select_fusion), channel_id=1, source_target_pairs={{0,256},{256,0},{1,257},{257,1},{2,258},{258,2},{3,259},{259,3},{4... | collective-permute-start | bytes 294920 | tf_op jit(solution)/shard_map/ppermute | solution.py:41
  6.3 0.8 fusion.5
  7.8 2.2 %collective-permute-done.side_ref = f32[2,16,3,256]{3,2,1,0:T(4,128)S(1)} collective-permute-done((f32[2,16,3,256]{3,2,1,0:T(4,128)S(1)}, f32[2,16,3,256]{3,2,1,0:T(4,128)S(1)}, u32[]{:S(2)}, u32[]{:S(2)}) %collective-permute-start) | collective-permute-done | bytes 98336 | tf_op jit(solution)/shard_map/ppermute | solution.py:41
  10.0 3.4 %collective-permute-start.1 = (f32[2,3,22,256]{3,2,1,0:T(8,128)S(1)}, f32[2,3,22,256]{3,2,1,0:T(8,128)S(1)}, u32[]{:S(2)}, u32[]{:S(2)}) collective-permute-start(f32[2,3,22,256]{3,2,1,0:T(8,128)S(1)} %pad_maximum_fusion.6), channel_id=1, source_target_pairs={{0,4},{4,8},{8,12},{12,16},{16,20},{20,24},{24,28},{28,32},{32,36}... | collective-permute-start | bytes 405512 | tf_op jit(solution)/shard_map/ppermute | solution.py:71
  13.4 4.6 %collective-permute-start.2 = (f32[2,3,22,256]{3,2,1,0:T(8,128)S(1)}, f32[2,3,22,256]{3,2,1,0:T(8,128)S(1)}, u32[]{:S(2)}, u32[]{:S(2)}) collective-permute-start(f32[2,3,22,256]{3,2,1,0:T(8,128)S(1)} %pad_maximum_fusion.7), channel_id=1, source_target_pairs={{4,0},{8,4},{12,8},{16,12},{20,16},{24,20},{28,24},{32,28},{36,32}... | collective-permute-start | bytes 405512 | tf_op jit(solution)/shard_map/ppermute | solution.py:72
  18.0 5.1 %collective-permute-start.3 = (bf16[192,512]{1,0:T(8,128)(2,1)S(1)}, bf16[192,512]{1,0:T(8,128)(2,1)S(1)}, u32[]{:S(2)}, u32[]{:S(2)}) collective-permute-start(bf16[192,512]{1,0:T(8,128)(2,1)S(1)} %bitcast.62), channel_id=1, source_target_pairs={{0,2},{2,0},{1,3},{3,1},{4,6},{6,4},{5,7},{7,5},{8,10},{10,8},{9,1... | collective-permute-start | bytes 589832 | tf_op jit(solution)/shard_map/ppermute | solution.py:41
  23.3 4.1 %slab.1 = (f32[16,16,256]{2,1,0:T(8,128)}, bf16[256,640]{1,0:T(8,128)(2,1)S(1)}) custom-call(s32[2]{0:T(128)S(1)} %pad_add_fusion.place_ref, f32[8]{0:T(128)S(1)} %bitcast.51, f32[16,16,256]{2,1,0:T(8,128)S(1)} %bitcast.50, s32[16,16,256]{2,1,0:T(8,128)S(1)} %copy-done.3, f32[2,16,3,256]{3,2,1,0:T(4,128)S(1)} %collective-permute-done.side_ref, ...), custom_call_target="tpu_custom_call" | custom-call | tf_op jit(solution)/shard_map/slab/pallas_call | solution.py:241
  27.5 3.1 %collective-permute-start.4 = (bf16[2,192,512]{2,1,0:T(8,128)(2,1)S(1)}, bf16[2,192,512]{2,1,0:T(8,128)(2,1)S(1)}, u32[]{:S(2)}, u32[]{:S(2)}) collective-permute-start(bf16[2,192,512]{2,1,0:T(8,128)(2,1)S(1)} %pad_maximum_fusion.3), channel_id=1, source_target_pairs={{0,256},{256,0},{1,257},{257,1},{2,258},{258,2},{3,259},{259,3},{4... | collective-permute-start | bytes 1179656 | tf_op jit(solution)/shard_map/ppermute | solution.py:41
  30.6 0.8 reshape.102
  31.4 18.1 %all-to-all-start = ((bf16[64,4,640]{2,1,0:T(4,128)(2,1)}), bf16[64,4,640]{2,1,0:T(4,128)(2,1)}, u32[]{:S(2)}, u32[]{:S(2)}) async-start(bf16[64,4,640]{2,1,0:T(4,128)(2,1)} %reshape.102), calls=%async_computation | async-start | bytes 655360 | tf_op jit(solution)/shard_map/all_to_all | solution.py:32
  49.6 1.9 collective-permute-start.6
  51.6 2.4 %collective-permute-start.5 = (bf16[2,2,192,512]{3,2,1,0:T(8,128)(2,1)S(1)}, bf16[2,2,192,512]{3,2,1,0:T(8,128)(2,1)S(1)}, u32[]{:S(2)}, u32[]{:S(2)}) collective-permute-start(bf16[2,2,192,512]{3,2,1,0:T(8,128)(2,1)S(1)} %pad_maximum_fusion.2), channel_id=1, source_target_pairs={{0,1},{1,0},{2,3},{3,2},{4,5},{5,4},{6,7},{7,6},{8,9},{9,8},{10,11... | collective-permute-start | bytes 2359304 | tf_op jit(solution)/shard_map/ppermute | solution.py:41
  54.0 0.7 fusion.4
  54.8 0.7 multiply_add_fusion
  55.4 1.9 collective-permute-start.7
  57.4 0.7 fusion.2
  58.3 0.7 collective-permute-done.7.out_other_ref
  59.1 1.8 prepare.1.all_hbm
  60.9 1.9 copy-done.1
  62.9 8.7 %all-to-all-done = bf16[64,4,640]{2,1,0:T(4,128)(2,1)} async-done(((bf16[64,4,640]{2,1,0:T(4,128)(2,1)}), bf16[64,4,640]{2,1,0:T(4,128)(2,1)}, u32[]{:S(2)}, u32[]{:S(2)}) %all-to-all-start) | async-done | bytes 327712 | tf_op jit(solution)/shard_map/all_to_all | solution.py:32
  71.6 1.1 reshape.104
  72.7 0.4 convolution_convert_fusion
  73.0 12.5 %all_to_all.41 = bf16[4,128,640]{2,1,0:T(8,128)(2,1)S(1)} all-to-all(bf16[4,128,640]{2,1,0:T(8,128)(2,1)S(1)} %bitcast.54), channel_id=1, replica_groups=mesh['grp'=2,'z'=16,'x'=4,'yhi'=2,'core'=2] {'grp','yhi'}, dimensions={0} | all-to-all | bytes 1310720 | tf_op jit(solution)/shard_map/all_to_all | solution.py:32
  85.5 7.8 %forward.1 = (bf16[512,1536]{1,0:T(8,128)(2,1)S(1)}, bf16[512,768]{1,0:T(8,128)(2,1)S(1)}, f32[512,256]{1,0:T(8,128)S(1)}, bf16[512,128]{1,0:T(8,128)(2,1)S(1)}, bf16[512,128]{1,0:T(8,128)(2,1)S(1)}) custom-call(s32[1]{0:T(128)} %bitcast.13.chip_ref, bf16[512,640]{1,0:T(8,128)(2,1)S(1)} %bitcast.47, bf16[512,4096]{1,0:T(8,128)(2,1)} %copy-done.1, ...), custom_call_target="tpu_custom_call" | custom-call | flops 2013265920 | bytes 6291456 | tf_op jit(solution)/shard_map/forward/pallas_call | solution.py:412
  93.4 10.3 %all_to_all.42.share_ref = bf16[4,512,128]{2,1,0:T(8,128)(2,1)S(1)} all-to-all(bf16[4,512,128]{2,1,0:T(8,128)(2,1)S(1)} %broadcast_in_dim.72), channel_id=1, replica_groups=mesh['grp'=2,'z'=16,'x'=4,'yhi'=2,'core'=2] {'grp','yhi'}, dimensions={0} | all-to-all | bytes 1048576 | tf_op jit(solution)/shard_map/all_to_all | solution.py:32
  103.8 2.2 %backward_other.1 = bf16[3,1536,128]{2,1,0:T(8,128)(2,1)S(1)} custom-call(bf16[512,128]{1,0:T(8,128)(2,1)S(1)} %delta.1.delta_ref, bf16[512,128]{1,0:T(8,128)(2,1)S(1)} %get-tuple-element.33.mix_ref, bf16[512,768]{1,0:T(8,128)(2,1)S(1)} %get-tuple-element.34.proj_ref, f32[512,256]{1,0:T(8,128)S(1)} %get-tuple-element.35.prob_ref, ...), custom_call_target="tpu_custom_call" | custom-call | flops 603979776 | bytes 3145728 | tf_op jit(solution)/shard_map/backward_other/pallas_call | solution.py:493
  106.0 1.9 collective-permute-start.8
  107.9 2.2 %backward_own.1 = bf16[3,1536,128]{2,1,0:T(8,128)(2,1)S(1)} custom-call(bf16[512,128]{1,0:T(8,128)(2,1)S(1)} %delta.1.delta_ref, bf16[512,128]{1,0:T(8,128)(2,1)S(1)} %get-tuple-element.33.mix_ref, bf16[512,768]{1,0:T(8,128)(2,1)S(1)} %get-tuple-element.34.proj_ref, f32[512,256]{1,0:T(8,128)S(1)} %get-tuple-element.35.prob_ref, ...), custom_call_target="tpu_custom_call" | custom-call | flops 603979776 | bytes 3145728 | tf_op jit(solution)/shard_map/backward_own/pallas_call | solution.py:493
  110.1 0.6 collective-permute-done.8
  110.7 0.6 multiply_reduce_fusion
  111.5 19.7 %all_to_all.43 = bf16[4,1155,128]{2,1,0:T(8,128)(2,1)S(1)} all-to-all(bf16[4,1155,128]{2,1,0:T(8,128)(2,1)S(1)} %pad_maximum_fusion.1), channel_id=1, replica_groups=mesh['grp'=2,'z'=16,'x'=4,'yhi'=2,'core'=2] {'x'}, dimensions={0} | all-to-all | bytes 2365440 | tf_op jit(solution)/shard_map/all_to_all | solution.py:32
  131.1 0.2 slice_reduce_fusion
  131.3 28.0 %all_to_all.44 = bf16[16,75,128]{2,1,0:T(8,128)(2,1)S(1)} all-to-all(bf16[16,75,128]{2,1,0:T(8,128)(2,1)S(1)} %pad_maximum_fusion.4), channel_id=1, replica_groups=mesh['grp'=2,'z'=16,'x'=4,'yhi'=2,'core'=2] {'z'}, dimensions={0} | all-to-all | bytes 614400 | tf_op jit(solution)/shard_map/all_to_all | solution.py:32
  159.4 0.8 broadcast_in_dim.74
  160.1 6.2 %all-to-all-start.5 = ((bf16[16,72,128]{2,1,0:T(8,128)(2,1)}), bf16[16,72,128]{2,1,0:T(8,128)(2,1)S(1)}, u32[]{:S(2)}, u32[]{:S(2)}) async-start(bf16[16,72,128]{2,1,0:T(8,128)(2,1)} %broadcast_in_dim.74), calls=%async_computation.5 | async-start | bytes 589824 | tf_op jit(solution)/shard_map/all_to_all | solution.py:32
  166.4 1.9 collective-permute-start.9
  168.3 1.1 collective-permute-done.9
  169.4 2.4 %collective-permute-start.10 = (f32[3,128]{1,0:T(4,128)S(1)}, f32[3,128]{1,0:T(4,128)S(1)}, u32[]{:S(2)}, u32[]{:S(2)}) collective-permute-start(f32[3,128]{1,0:T(4,128)S(1)} %add.74), channel_id=1, source_target_pairs={{0,256},{256,0},{1,257},{257,1},{2,258},{258,2},{3,259},{259,3},{4... | collective-permute-start | bytes 4616 | tf_op jit(solution)/shard_map/ppermute | solution.py:41
  171.8 3.1 %collective-permute-done.10 = f32[3,128]{1,0:T(4,128)S(1)} collective-permute-done((f32[3,128]{1,0:T(4,128)S(1)}, f32[3,128]{1,0:T(4,128)S(1)}, u32[]{:S(2)}, u32[]{:S(2)}) %collective-permute-start.10) | collective-permute-done | bytes 1568 | tf_op jit(solution)/shard_map/ppermute | solution.py:41
  174.9 3.4 %collective-permute-start.11 = (f32[3,128]{1,0:T(4,128)S(1)}, f32[3,128]{1,0:T(4,128)S(1)}, u32[]{:S(2)}, u32[]{:S(2)}) collective-permute-start(f32[3,128]{1,0:T(4,128)S(1)} %add.75), channel_id=1, source_target_pairs={{0,2},{2,0},{1,3},{3,1},{4,6},{6,4},{5,7},{7,5},{8,10},{10,8},{9,1... | collective-permute-start | bytes 4616 | tf_op jit(solution)/shard_map/ppermute | solution.py:41
  178.3 3.6 %collective-permute-done.11 = f32[3,128]{1,0:T(4,128)S(1)} collective-permute-done((f32[3,128]{1,0:T(4,128)S(1)}, f32[3,128]{1,0:T(4,128)S(1)}, u32[]{:S(2)}, u32[]{:S(2)}) %collective-permute-start.11) | collective-permute-done | bytes 1568 | tf_op jit(solution)/shard_map/ppermute | solution.py:41
  181.9 2.6 %all-to-all-done.5 = bf16[16,72,128]{2,1,0:T(8,128)(2,1)S(1)} async-done(((bf16[16,72,128]{2,1,0:T(8,128)(2,1)}), bf16[16,72,128]{2,1,0:T(8,128)(2,1)S(1)}, u32[]{:S(2)}, u32[]{:S(2)}) %all-to-all-start.5) | async-done | bytes 294944 | tf_op jit(solution)/shard_map/all_to_all | solution.py:32
  184.5 0.2 broadcast_in_dim.75
  184.7 18.6 %all_to_all.45 = bf16[4,1155,128]{2,1,0:T(8,128)(2,1)S(1)} all-to-all(bf16[4,1155,128]{2,1,0:T(8,128)(2,1)S(1)} %broadcast_in_dim.75), channel_id=1, replica_groups=mesh['grp'=2,'z'=16,'x'=4,'yhi'=2,'core'=2] {'x'}, dimensions={0} | all-to-all | bytes 2365440 | tf_op jit(solution)/shard_map/all_to_all | solution.py:32
  203.3 0.6 reshape.139
  203.9 1.1 slice.79
  (68 shorter events, 1.9 us)
Async XLA Ops:
  0.6 6.5 %copy-start.3 = (s32[16,16,256]{2,1,0:T(8,128)S(1)}, s32[16,16,256]{2,1,0:T(8,128)}, u32[]{:S(2)}) copy-start(s32[16,16,256]{2,1,0:T(8,128)} %material_ref.1) | copy-start | bytes 786436
  0.6 6.5 %copy-start.9 = (s32[1,1,64,128,1]{3,4,2,1,0:T(1,128)S(1)}, s32[1,1,64,128,1]{3,4,2,1,0:T(1,128)}, u32[]{:S(2)}) copy-start(s32[1,1,64,128,1]{3,4,2,1,0:T(1,128)} %param.13) | copy-start | bytes 98308
  0.7 6.7 %copy-start.11 = (s32[1,1,64,128]{3,2,1,0:T(8,128)S(1)}, s32[1,1,64,128]{3,2,1,0:T(8,128)}, u32[]{:S(2)}) copy-start(s32[1,1,64,128]{3,2,1,0:T(8,128)} %param.14) | copy-start | bytes 98308
  0.7 17.3 %copy-start.8 = (bf16[512,192]{0,1:T(8,128)(2,1)S(1)}, bf16[512,192]{0,1:T(8,128)(2,1)}, u32[]{:S(2)}) copy-start(bf16[512,192]{0,1:T(8,128)(2,1)} %param.15) | copy-start | bytes 589828
  0.7 22.6 %copy-start.2 = (f32[1,16,16,256]{3,2,1,0:T(8,128)S(1)}, f32[1,16,16,256]{3,2,1,0:T(8,128)}, u32[]{:S(2)}) copy-start(f32[1,16,16,256]{3,2,1,0:T(8,128)} %param.10) | copy-start | bytes 786436
  0.7 22.6 %copy-start.6 = (f32[1,8]{1,0:T(1,128)S(1)}, f32[1,8]{1,0:T(1,128)}, u32[]{:S(2)}) copy-start(f32[1,8]{1,0:T(1,128)} %param.12) | copy-start | bytes 100
  2.8 7.1 %collective-permute-start = (f32[2,16,3,256]{3,2,1,0:T(4,128)S(1)}, f32[2,16,3,256]{3,2,1,0:T(4,128)S(1)}, u32[]{:S(2)}, u32[]{:S(2)}) collective-permute-start(f32[2,16,3,256]{3,2,1,0:T(4,128)S(1)} %maximum_select_fusion), channel_id=1, source_target_pairs={{0,256},{256,0},{1,257},{257,1},{2,258},{258,2},{3,259},{259,3},{4... | collective-permute-start | bytes 294920 | tf_op jit(solution)/shard_map/ppermute | solution.py:41
  10.0 13.3 %collective-permute-start.1 = (f32[2,3,22,256]{3,2,1,0:T(8,128)S(1)}, f32[2,3,22,256]{3,2,1,0:T(8,128)S(1)}, u32[]{:S(2)}, u32[]{:S(2)}) collective-permute-start(f32[2,3,22,256]{3,2,1,0:T(8,128)S(1)} %pad_maximum_fusion.6), channel_id=1, source_target_pairs={{0,4},{4,8},{8,12},{12,16},{16,20},{20,24},{24,28},{28,32},{32,36}... | collective-permute-start | bytes 405512 | tf_op jit(solution)/shard_map/ppermute | solution.py:71
  13.4 9.9 %collective-permute-start.2 = (f32[2,3,22,256]{3,2,1,0:T(8,128)S(1)}, f32[2,3,22,256]{3,2,1,0:T(8,128)S(1)}, u32[]{:S(2)}, u32[]{:S(2)}) collective-permute-start(f32[2,3,22,256]{3,2,1,0:T(8,128)S(1)} %pad_maximum_fusion.7), channel_id=1, source_target_pairs={{4,0},{8,4},{12,8},{16,12},{20,16},{24,20},{28,24},{32,28},{36,32}... | collective-permute-start | bytes 405512 | tf_op jit(solution)/shard_map/ppermute | solution.py:72
  18.0 9.4 %collective-permute-start.3 = (bf16[192,512]{1,0:T(8,128)(2,1)S(1)}, bf16[192,512]{1,0:T(8,128)(2,1)S(1)}, u32[]{:S(2)}, u32[]{:S(2)}) collective-permute-start(bf16[192,512]{1,0:T(8,128)(2,1)S(1)} %bitcast.62), channel_id=1, source_target_pairs={{0,2},{2,0},{1,3},{3,1},{4,6},{6,4},{5,7},{7,5},{8,10},{10,8},{9,1... | collective-permute-start | bytes 589832 | tf_op jit(solution)/shard_map/ppermute | solution.py:41
  27.5 22.0 %collective-permute-start.4 = (bf16[2,192,512]{2,1,0:T(8,128)(2,1)S(1)}, bf16[2,192,512]{2,1,0:T(8,128)(2,1)S(1)}, u32[]{:S(2)}, u32[]{:S(2)}) collective-permute-start(bf16[2,192,512]{2,1,0:T(8,128)(2,1)S(1)} %pad_maximum_fusion.3), channel_id=1, source_target_pairs={{0,256},{256,0},{1,257},{257,1},{2,258},{258,2},{3,259},{259,3},{4... | collective-permute-start | bytes 1179656 | tf_op jit(solution)/shard_map/ppermute | solution.py:41
  31.4 18.2 %copy-start = (bf16[3,1536,128]{2,1,0:T(8,128)(2,1)S(1)}, bf16[3,1536,128]{2,1,0:T(8,128)(2,1)}, u32[]{:S(2)}) copy-start(bf16[3,1536,128]{2,1,0:T(8,128)(2,1)} %w_own_ref) | copy-start | bytes 3538948
  31.4 24.0 %copy-start.4 = (bf16[128,1536]{1,0:T(8,128)(2,1)S(1)}, bf16[128,1536]{1,0:T(8,128)(2,1)}, u32[]{:S(2)}) copy-start(bf16[128,1536]{1,0:T(8,128)(2,1)} %out_own_ref) | copy-start | bytes 1179652
  31.4 26.0 %copy-start.10 = (f32[1536]{0:T(1024)S(1)}, f32[1536]{0:T(1024)}, u32[]{:S(2)}) copy-start(f32[1536]{0:T(1024)} %param.16) | copy-start | bytes 18436
  31.4 40.2 %all-to-all-start = ((bf16[64,4,640]{2,1,0:T(4,128)(2,1)}), bf16[64,4,640]{2,1,0:T(4,128)(2,1)}, u32[]{:S(2)}, u32[]{:S(2)}) async-start(bf16[64,4,640]{2,1,0:T(4,128)(2,1)} %reshape.102), calls=%async_computation | async-start | bytes 655360 | tf_op jit(solution)/shard_map/all_to_all | solution.py:32
  49.6 9.4 %collective-permute-start.6 = (bf16[3,1536,128]{2,1,0:T(8,128)(2,1)S(1)}, bf16[3,1536,128]{2,1,0:T(8,128)(2,1)S(1)}, u32[]{:S(2)}, u32[]{:S(2)}) collective-permute-start(bf16[3,1536,128]{2,1,0:T(8,128)(2,1)S(1)} %copy-done), channel_id=1, source_target_pairs={{0,1},{1,0},{2,3},{3,2},{4,5},{5,4},{6,7},{7,6},{8,9},{9,8},{10,11... | collective-permute-start | bytes 3538952 | tf_op jit(solution)/shard_map/ppermute | solution.py:41
  51.6 6.6 %collective-permute-start.5 = (bf16[2,2,192,512]{3,2,1,0:T(8,128)(2,1)S(1)}, bf16[2,2,192,512]{3,2,1,0:T(8,128)(2,1)S(1)}, u32[]{:S(2)}, u32[]{:S(2)}) collective-permute-start(bf16[2,2,192,512]{3,2,1,0:T(8,128)(2,1)S(1)} %pad_maximum_fusion.2), channel_id=1, source_target_pairs={{0,1},{1,0},{2,3},{3,2},{4,5},{5,4},{6,7},{7,6},{8,9},{9,8},{10,11... | collective-permute-start | bytes 2359304 | tf_op jit(solution)/shard_map/ppermute | solution.py:41
  55.4 3.6 %collective-permute-start.7 = (bf16[128,1536]{1,0:T(8,128)(2,1)S(1)}, bf16[128,1536]{1,0:T(8,128)(2,1)S(1)}, u32[]{:S(2)}, u32[]{:S(2)}) collective-permute-start(bf16[128,1536]{1,0:T(8,128)(2,1)S(1)} %copy-done.4), channel_id=1, source_target_pairs={{0,1},{1,0},{2,3},{3,2},{4,5},{5,4},{6,7},{7,6},{8,9},{9,8},{10,11... | collective-permute-start | bytes 1179656 | tf_op jit(solution)/shard_map/ppermute | solution.py:41
  58.1 1.0 copy-start.5
  59.1 13.5 %copy-start.7 = (bf16[128,256]{1,0:T(8,128)(2,1)S(1)}, bf16[128,256]{1,0:T(8,128)(2,1)}, u32[]{:S(2)}) copy-start(bf16[128,256]{1,0:T(8,128)(2,1)} %fusion.2) | copy-start | bytes 196612
  60.9 2.0 copy-start.1
  106.0 4.7 %collective-permute-start.8 = (bf16[3,1536,128]{2,1,0:T(8,128)(2,1)S(1)}, bf16[3,1536,128]{2,1,0:T(8,128)(2,1)S(1)}, u32[]{:S(2)}, u32[]{:S(2)}) collective-permute-start(bf16[3,1536,128]{2,1,0:T(8,128)(2,1)S(1)} %backward_other.1), channel_id=1, source_target_pairs={{0,1},{1,0},{2,3},{3,2},{4,5},{5,4},{6,7},{7,6},{8,9},{9,8},{10,11... | collective-permute-start | bytes 3538952 | tf_op jit(solution)/shard_map/ppermute | solution.py:41
  160.1 24.4 %all-to-all-start.5 = ((bf16[16,72,128]{2,1,0:T(8,128)(2,1)}), bf16[16,72,128]{2,1,0:T(8,128)(2,1)S(1)}, u32[]{:S(2)}, u32[]{:S(2)}) async-start(bf16[16,72,128]{2,1,0:T(8,128)(2,1)} %broadcast_in_dim.74), calls=%async_computation.5 | async-start | bytes 589824 | tf_op jit(solution)/shard_map/all_to_all | solution.py:32
  166.4 3.0 %collective-permute-start.9 = (f32[3,128]{1,0:T(4,128)S(1)}, f32[3,128]{1,0:T(4,128)S(1)}, u32[]{:S(2)}, u32[]{:S(2)}) collective-permute-start(f32[3,128]{1,0:T(4,128)S(1)} %convert_reduce_fusion.1), channel_id=1, source_target_pairs={{0,1},{1,0},{2,3},{3,2},{4,5},{5,4},{6,7},{7,6},{8,9},{9,8},{10,11... | collective-permute-start | bytes 4616 | tf_op jit(solution)/shard_map/ppermute | solution.py:41
  169.4 5.5 %collective-permute-start.10 = (f32[3,128]{1,0:T(4,128)S(1)}, f32[3,128]{1,0:T(4,128)S(1)}, u32[]{:S(2)}, u32[]{:S(2)}) collective-permute-start(f32[3,128]{1,0:T(4,128)S(1)} %add.74), channel_id=1, source_target_pairs={{0,256},{256,0},{1,257},{257,1},{2,258},{258,2},{3,259},{259,3},{4... | collective-permute-start | bytes 4616 | tf_op jit(solution)/shard_map/ppermute | solution.py:41
  174.9 7.0 %collective-permute-start.11 = (f32[3,128]{1,0:T(4,128)S(1)}, f32[3,128]{1,0:T(4,128)S(1)}, u32[]{:S(2)}, u32[]{:S(2)}) collective-permute-start(f32[3,128]{1,0:T(4,128)S(1)} %add.75), channel_id=1, source_target_pairs={{0,2},{2,0},{1,3},{3,1},{4,6},{6,4},{5,7},{7,5},{8,10},{10,8},{9,1... | collective-permute-start | bytes 4616 | tf_op jit(solution)/shard_map/ppermute | solution.py:41

commit v7 on v6

--- a/solution.py
+++ b/solution.py
@@ -344,15 +344,28 @@
         pltpu.make_async_copy(
             all_hbm.at[:, pl.ds(start, size)], all_ref.at[:, pl.ds(start, size)], sems.at[i]
         )
-        for i, (start, size) in enumerate(((0, model), (model, mix - model), (mix, end - mix)))
+        for i, (start, size) in enumerate(
+            [(part * model // 3, model // 3) for part in range(3)]
+            + [(model, mix - model), (mix, end - mix)]
+        )
     ]
-    for fetch in fetches:
+    for fetch in fetches[:3]:
         fetch.start()
-    fetches[0].wait()
     across = (((1,), (1,)), ((), ()))
-    embedded = jnp.dot(
-        sample_ref[:, :token_width], all_ref[:, :model], preferred_element_type=jnp.float32
-    ).astype(jnp.bfloat16)
+    tokens = sample_ref[:, :token_width]
+    parts = []
+    for part in range(3):
+        columns = slice(part * model // 3, (part + 1) * model // 3)
+        fetches[part].wait()
+        if part == 2:
+            for fetch in fetches[3:]:
+                fetch.start()
+        parts.append(
+            jnp.dot(tokens, all_ref[:, columns], preferred_element_type=jnp.float32).astype(
+                jnp.bfloat16
+            )
+        )
+    embedded = jnp.concatenate(parts, axis=1)
     embed_ref[...] = embedded
     wide = embedded.astype(jnp.float32)
     mean = jnp.mean(wide, axis=1, keepdims=True)
@@ -360,8 +373,8 @@
     variance = jnp.mean(removed * removed, axis=1, keepdims=True)
     normed = (removed * lax.rsqrt(variance + NORM_EPSILON) * gain_ref[...]).astype(jnp.bfloat16)
     normed_ref[...] = normed
-    fetches[1].wait()
-    fetches[2].wait()
+    for fetch in fetches[3:]:
+        fetch.wait()
     mix_ref[...] = all_ref[:, mix:read]
     proj_w = jnp.concatenate(
         [all_ref[:, start : start + heads] for start in range(model, mix, heads)], axis=0
@@ -417,7 +430,7 @@
         scratch_shapes=[
             pltpu.VMEM((rows, model), jnp.bfloat16),
             pltpu.VMEM(weights.shape, weights.dtype),
-            pltpu.SemaphoreType.DMA((3,)),
+            pltpu.SemaphoreType.DMA((5,)),
         ],
         compiler_params=pltpu.CompilerParams(vmem_limit_bytes=FORWARD_LIMIT),
         cost_estimate=pl.CostEstimate(

time: 206 us -> 206 us (level)
  no operation moved by 1% of the time
where the time goes in v7:
time: 206 us; the launch traced here: 205 us
  blocking collectives  89 us (43%)
  starting transfers between devices  59.8 us (29%)
  waiting for transfers between devices  22.7 us (11%)
  Pallas kernels  18.5 us (9%)
  local copies, waits for them, and re-layouts  8.79 us (4%)
  other arithmetic  4.96 us (2%)
    all_to_all x5, blocking collectives, swap(): return lax.all_to_all(parts, axis, split_axis=0, concat_axis=0, tiled=True)  89 us
    ppermute x10, starting transfers between devices, swap_with(): return lax.ppermute(own, axis, [(0, 1), (1, 0)])  27.5 us
    all_to_all x2, starting transfers between devices, swap(): return lax.all_to_all(parts, axis, split_axis=0, concat_axis=0, tiled=True)  24.3 us
    ppermute x10, waiting for transfers between devices, swap_with(): return lax.ppermute(own, axis, [(0, 1), (1, 0)])  11.3 us
    all_to_all x2, waiting for transfers between devices, swap(): return lax.all_to_all(parts, axis, split_axis=0, concat_axis=0, tiled=True)  11.3 us
    pallas_call x1, Pallas kernels, run_forward(): pl.pallas_call(forward_kernel, out_shape=shapes, in_specs=[SMEM, VMEM, pl...  8.16 us
    ppermute x1, starting transfers between devices, halos(): high = lax.ppermute(bottom, SPACE, backward)  4.55 us
    pallas_call x2, Pallas kernels, run_backward(): pl.pallas_call(functools.partial(backward_kernel, head=head), out_shape=j...  4.39 us
  transfers between devices with their start and end apart: 14, of which 8 were waited for; matrix products, arithmetic and copies ran while one was open for 2% of the time, Pallas kernels for 4%

profile of v7, /device:TPU:32, one launch (start us, length us, event | category | flops | bytes accessed | tf_op | source)
XLA Modules:
  0.0 205.3 jit_solution(4276453565214116985)
XLA Ops:
  0.7 1.0 slice_bitcast_fusion
  1.8 1.0 convert_bitcast_fusion
  2.8 3.5 %collective-permute-start = (f32[2,16,3,256]{3,2,1,0:T(4,128)S(1)}, f32[2,16,3,256]{3,2,1,0:T(4,128)S(1)}, u32[]{:S(2)}, u32[]{:S(2)}) collective-permute-start(f32[2,16,3,256]{3,2,1,0:T(4,128)S(1)} %maximum_select_fusion), channel_id=1, source_target_pairs={{0,256},{256,0},{1,257},{257,1},{2,258},{258,2},{3,259},{259,3},{4... | collective-permute-start | bytes 294920 | tf_op jit(solution)/shard_map/ppermute | solution.py:41
  6.3 0.8 fusion.5
  7.8 2.2 %collective-permute-done.side_ref = f32[2,16,3,256]{3,2,1,0:T(4,128)S(1)} collective-permute-done((f32[2,16,3,256]{3,2,1,0:T(4,128)S(1)}, f32[2,16,3,256]{3,2,1,0:T(4,128)S(1)}, u32[]{:S(2)}, u32[]{:S(2)}) %collective-permute-start) | collective-permute-done | bytes 98336 | tf_op jit(solution)/shard_map/ppermute | solution.py:41
  10.0 3.4 %collective-permute-start.1 = (f32[2,3,22,256]{3,2,1,0:T(8,128)S(1)}, f32[2,3,22,256]{3,2,1,0:T(8,128)S(1)}, u32[]{:S(2)}, u32[]{:S(2)}) collective-permute-start(f32[2,3,22,256]{3,2,1,0:T(8,128)S(1)} %pad_maximum_fusion.6), channel_id=1, source_target_pairs={{0,4},{4,8},{8,12},{12,16},{16,20},{20,24},{24,28},{28,32},{32,36}... | collective-permute-start | bytes 405512 | tf_op jit(solution)/shard_map/ppermute | solution.py:71
  13.4 4.6 %collective-permute-start.2 = (f32[2,3,22,256]{3,2,1,0:T(8,128)S(1)}, f32[2,3,22,256]{3,2,1,0:T(8,128)S(1)}, u32[]{:S(2)}, u32[]{:S(2)}) collective-permute-start(f32[2,3,22,256]{3,2,1,0:T(8,128)S(1)} %pad_maximum_fusion.7), channel_id=1, source_target_pairs={{4,0},{8,4},{12,8},{16,12},{20,16},{24,20},{28,24},{32,28},{36,32}... | collective-permute-start | bytes 405512 | tf_op jit(solution)/shard_map/ppermute | solution.py:72
  18.0 5.1 %collective-permute-start.3 = (bf16[192,512]{1,0:T(8,128)(2,1)S(1)}, bf16[192,512]{1,0:T(8,128)(2,1)S(1)}, u32[]{:S(2)}, u32[]{:S(2)}) collective-permute-start(bf16[192,512]{1,0:T(8,128)(2,1)S(1)} %bitcast.62), channel_id=1, source_target_pairs={{0,2},{2,0},{1,3},{3,1},{4,6},{6,4},{5,7},{7,5},{8,10},{10,8},{9,1... | collective-permute-start | bytes 589832 | tf_op jit(solution)/shard_map/ppermute | solution.py:41
  23.3 4.1 %slab.1 = (f32[16,16,256]{2,1,0:T(8,128)}, bf16[256,640]{1,0:T(8,128)(2,1)S(1)}) custom-call(s32[2]{0:T(128)S(1)} %pad_add_fusion.place_ref, f32[8]{0:T(128)S(1)} %bitcast.51, f32[16,16,256]{2,1,0:T(8,128)S(1)} %bitcast.50, s32[16,16,256]{2,1,0:T(8,128)S(1)} %copy-done.3, f32[2,16,3,256]{3,2,1,0:T(4,128)S(1)} %collective-permute-done.side_ref, ...), custom_call_target="tpu_custom_call" | custom-call | tf_op jit(solution)/shard_map/slab/pallas_call | solution.py:241
  27.5 3.1 %collective-permute-start.4 = (bf16[2,192,512]{2,1,0:T(8,128)(2,1)S(1)}, bf16[2,192,512]{2,1,0:T(8,128)(2,1)S(1)}, u32[]{:S(2)}, u32[]{:S(2)}) collective-permute-start(bf16[2,192,512]{2,1,0:T(8,128)(2,1)S(1)} %pad_maximum_fusion.3), channel_id=1, source_target_pairs={{0,256},{256,0},{1,257},{257,1},{2,258},{258,2},{3,259},{259,3},{4... | collective-permute-start | bytes 1179656 | tf_op jit(solution)/shard_map/ppermute | solution.py:41
  30.6 0.8 reshape.102
  31.4 18.1 %all-to-all-start = ((bf16[64,4,640]{2,1,0:T(4,128)(2,1)}), bf16[64,4,640]{2,1,0:T(4,128)(2,1)}, u32[]{:S(2)}, u32[]{:S(2)}) async-start(bf16[64,4,640]{2,1,0:T(4,128)(2,1)} %reshape.102), calls=%async_computation | async-start | bytes 655360 | tf_op jit(solution)/shard_map/all_to_all | solution.py:32
  49.6 1.9 collective-permute-start.6
  51.6 2.4 %collective-permute-start.5 = (bf16[2,2,192,512]{3,2,1,0:T(8,128)(2,1)S(1)}, bf16[2,2,192,512]{3,2,1,0:T(8,128)(2,1)S(1)}, u32[]{:S(2)}, u32[]{:S(2)}) collective-permute-start(bf16[2,2,192,512]{3,2,1,0:T(8,128)(2,1)S(1)} %pad_maximum_fusion.2), channel_id=1, source_target_pairs={{0,1},{1,0},{2,3},{3,2},{4,5},{5,4},{6,7},{7,6},{8,9},{9,8},{10,11... | collective-permute-start | bytes 2359304 | tf_op jit(solution)/shard_map/ppermute | solution.py:41
  54.0 0.7 fusion.4
  54.8 0.7 multiply_add_fusion
  55.4 1.9 collective-permute-start.7
  57.4 0.7 fusion.2
  58.3 0.7 collective-permute-done.7.out_other_ref
  59.1 1.8 prepare.1.all_hbm
  60.9 1.9 copy-done.1
  62.9 8.7 %all-to-all-done = bf16[64,4,640]{2,1,0:T(4,128)(2,1)} async-done(((bf16[64,4,640]{2,1,0:T(4,128)(2,1)}), bf16[64,4,640]{2,1,0:T(4,128)(2,1)}, u32[]{:S(2)}, u32[]{:S(2)}) %all-to-all-start) | async-done | bytes 327712 | tf_op jit(solution)/shard_map/all_to_all | solution.py:32
  71.6 1.1 reshape.104
  72.7 0.4 convolution_convert_fusion
  73.0 12.5 %all_to_all.41 = bf16[4,128,640]{2,1,0:T(8,128)(2,1)S(1)} all-to-all(bf16[4,128,640]{2,1,0:T(8,128)(2,1)S(1)} %bitcast.54), channel_id=1, replica_groups=mesh['grp'=2,'z'=16,'x'=4,'yhi'=2,'core'=2] {'grp','yhi'}, dimensions={0} | all-to-all | bytes 1310720 | tf_op jit(solution)/shard_map/all_to_all | solution.py:32
  85.5 8.2 %forward.1 = (bf16[512,1536]{1,0:T(8,128)(2,1)S(1)}, bf16[512,768]{1,0:T(8,128)(2,1)S(1)}, f32[512,256]{1,0:T(8,128)S(1)}, bf16[512,128]{1,0:T(8,128)(2,1)S(1)}, bf16[512,128]{1,0:T(8,128)(2,1)S(1)}) custom-call(s32[1]{0:T(128)} %bitcast.13.chip_ref, bf16[512,640]{1,0:T(8,128)(2,1)S(1)} %bitcast.47, bf16[512,4096]{1,0:T(8,128)(2,1)} %copy-done.1, ...), custom_call_target="tpu_custom_call" | custom-call | flops 2013265920 | bytes 6291456 | tf_op jit(solution)/shard_map/forward/pallas_call | solution.py:425
  93.7 10.3 %all_to_all.42.share_ref = bf16[4,512,128]{2,1,0:T(8,128)(2,1)S(1)} all-to-all(bf16[4,512,128]{2,1,0:T(8,128)(2,1)S(1)} %broadcast_in_dim.72), channel_id=1, replica_groups=mesh['grp'=2,'z'=16,'x'=4,'yhi'=2,'core'=2] {'grp','yhi'}, dimensions={0} | all-to-all | bytes 1048576 | tf_op jit(solution)/shard_map/all_to_all | solution.py:32
  104.2 2.2 %backward_other.1 = bf16[3,1536,128]{2,1,0:T(8,128)(2,1)S(1)} custom-call(bf16[512,128]{1,0:T(8,128)(2,1)S(1)} %delta.1.delta_ref, bf16[512,128]{1,0:T(8,128)(2,1)S(1)} %get-tuple-element.33.mix_ref, bf16[512,768]{1,0:T(8,128)(2,1)S(1)} %get-tuple-element.34.proj_ref, f32[512,256]{1,0:T(8,128)S(1)} %get-tuple-element.35.prob_ref, ...), custom_call_target="tpu_custom_call" | custom-call | flops 603979776 | bytes 3145728 | tf_op jit(solution)/shard_map/backward_other/pallas_call | solution.py:506
  106.4 1.9 collective-permute-start.8
  108.3 2.2 %backward_own.1 = bf16[3,1536,128]{2,1,0:T(8,128)(2,1)S(1)} custom-call(bf16[512,128]{1,0:T(8,128)(2,1)S(1)} %delta.1.delta_ref, bf16[512,128]{1,0:T(8,128)(2,1)S(1)} %get-tuple-element.33.mix_ref, bf16[512,768]{1,0:T(8,128)(2,1)S(1)} %get-tuple-element.34.proj_ref, f32[512,256]{1,0:T(8,128)S(1)} %get-tuple-element.35.prob_ref, ...), custom_call_target="tpu_custom_call" | custom-call | flops 603979776 | bytes 3145728 | tf_op jit(solution)/shard_map/backward_own/pallas_call | solution.py:506
  110.5 0.6 collective-permute-done.8
  111.1 0.6 multiply_reduce_fusion
  111.8 19.7 %all_to_all.43 = bf16[4,1155,128]{2,1,0:T(8,128)(2,1)S(1)} all-to-all(bf16[4,1155,128]{2,1,0:T(8,128)(2,1)S(1)} %pad_maximum_fusion.1), channel_id=1, replica_groups=mesh['grp'=2,'z'=16,'x'=4,'yhi'=2,'core'=2] {'x'}, dimensions={0} | all-to-all | bytes 2365440 | tf_op jit(solution)/shard_map/all_to_all | solution.py:32
  131.5 0.2 slice_reduce_fusion
  131.7 28.0 %all_to_all.44 = bf16[16,75,128]{2,1,0:T(8,128)(2,1)S(1)} all-to-all(bf16[16,75,128]{2,1,0:T(8,128)(2,1)S(1)} %pad_maximum_fusion.4), channel_id=1, replica_groups=mesh['grp'=2,'z'=16,'x'=4,'yhi'=2,'core'=2] {'z'}, dimensions={0} | all-to-all | bytes 614400 | tf_op jit(solution)/shard_map/all_to_all | solution.py:32
  159.8 0.8 broadcast_in_dim.74
  160.5 6.2 %all-to-all-start.5 = ((bf16[16,72,128]{2,1,0:T(8,128)(2,1)}), bf16[16,72,128]{2,1,0:T(8,128)(2,1)S(1)}, u32[]{:S(2)}, u32[]{:S(2)}) async-start(bf16[16,72,128]{2,1,0:T(8,128)(2,1)} %broadcast_in_dim.74), calls=%async_computation.5 | async-start | bytes 589824 | tf_op jit(solution)/shard_map/all_to_all | solution.py:32
  166.8 1.9 collective-permute-start.9
  168.7 1.1 collective-permute-done.9
  169.8 2.4 %collective-permute-start.10 = (f32[3,128]{1,0:T(4,128)S(1)}, f32[3,128]{1,0:T(4,128)S(1)}, u32[]{:S(2)}, u32[]{:S(2)}) collective-permute-start(f32[3,128]{1,0:T(4,128)S(1)} %add.74), channel_id=1, source_target_pairs={{0,256},{256,0},{1,257},{257,1},{2,258},{258,2},{3,259},{259,3},{4... | collective-permute-start | bytes 4616 | tf_op jit(solution)/shard_map/ppermute | solution.py:41
  172.2 3.1 %collective-permute-done.10 = f32[3,128]{1,0:T(4,128)S(1)} collective-permute-done((f32[3,128]{1,0:T(4,128)S(1)}, f32[3,128]{1,0:T(4,128)S(1)}, u32[]{:S(2)}, u32[]{:S(2)}) %collective-permute-start.10) | collective-permute-done | bytes 1568 | tf_op jit(solution)/shard_map/ppermute | solution.py:41
  175.3 3.4 %collective-permute-start.11 = (f32[3,128]{1,0:T(4,128)S(1)}, f32[3,128]{1,0:T(4,128)S(1)}, u32[]{:S(2)}, u32[]{:S(2)}) collective-permute-start(f32[3,128]{1,0:T(4,128)S(1)} %add.75), channel_id=1, source_target_pairs={{0,2},{2,0},{1,3},{3,1},{4,6},{6,4},{5,7},{7,5},{8,10},{10,8},{9,1... | collective-permute-start | bytes 4616 | tf_op jit(solution)/shard_map/ppermute | solution.py:41
  178.6 3.6 %collective-permute-done.11 = f32[3,128]{1,0:T(4,128)S(1)} collective-permute-done((f32[3,128]{1,0:T(4,128)S(1)}, f32[3,128]{1,0:T(4,128)S(1)}, u32[]{:S(2)}, u32[]{:S(2)}) %collective-permute-start.11) | collective-permute-done | bytes 1568 | tf_op jit(solution)/shard_map/ppermute | solution.py:41
  182.3 2.6 %all-to-all-done.5 = bf16[16,72,128]{2,1,0:T(8,128)(2,1)S(1)} async-done(((bf16[16,72,128]{2,1,0:T(8,128)(2,1)}), bf16[16,72,128]{2,1,0:T(8,128)(2,1)S(1)}, u32[]{:S(2)}, u32[]{:S(2)}) %all-to-all-start.5) | async-done | bytes 294944 | tf_op jit(solution)/shard_map/all_to_all | solution.py:32
  184.9 0.2 broadcast_in_dim.75
  185.1 18.6 %all_to_all.45 = bf16[4,1155,128]{2,1,0:T(8,128)(2,1)S(1)} all-to-all(bf16[4,1155,128]{2,1,0:T(8,128)(2,1)S(1)} %broadcast_in_dim.75), channel_id=1, replica_groups=mesh['grp'=2,'z'=16,'x'=4,'yhi'=2,'core'=2] {'x'}, dimensions={0} | all-to-all | bytes 2365440 | tf_op jit(solution)/shard_map/all_to_all | solution.py:32
  203.6 0.6 reshape.139
  204.3 1.1 slice.79
  (68 shorter events, 1.9 us)
Async XLA Ops:
  0.6 6.5 %copy-start.3 = (s32[16,16,256]{2,1,0:T(8,128)S(1)}, s32[16,16,256]{2,1,0:T(8,128)}, u32[]{:S(2)}) copy-start(s32[16,16,256]{2,1,0:T(8,128)} %material_ref.1) | copy-start | bytes 786436
  0.6 6.5 %copy-start.9 = (s32[1,1,64,128,1]{3,4,2,1,0:T(1,128)S(1)}, s32[1,1,64,128,1]{3,4,2,1,0:T(1,128)}, u32[]{:S(2)}) copy-start(s32[1,1,64,128,1]{3,4,2,1,0:T(1,128)} %param.13) | copy-start | bytes 98308
  0.7 6.7 %copy-start.11 = (s32[1,1,64,128]{3,2,1,0:T(8,128)S(1)}, s32[1,1,64,128]{3,2,1,0:T(8,128)}, u32[]{:S(2)}) copy-start(s32[1,1,64,128]{3,2,1,0:T(8,128)} %param.14) | copy-start | bytes 98308
  0.7 17.3 %copy-start.8 = (bf16[512,192]{0,1:T(8,128)(2,1)S(1)}, bf16[512,192]{0,1:T(8,128)(2,1)}, u32[]{:S(2)}) copy-start(bf16[512,192]{0,1:T(8,128)(2,1)} %param.15) | copy-start | bytes 589828
  0.7 22.6 %copy-start.2 = (f32[1,16,16,256]{3,2,1,0:T(8,128)S(1)}, f32[1,16,16,256]{3,2,1,0:T(8,128)}, u32[]{:S(2)}) copy-start(f32[1,16,16,256]{3,2,1,0:T(8,128)} %param.10) | copy-start | bytes 786436
  0.7 22.6 %copy-start.6 = (f32[1,8]{1,0:T(1,128)S(1)}, f32[1,8]{1,0:T(1,128)}, u32[]{:S(2)}) copy-start(f32[1,8]{1,0:T(1,128)} %param.12) | copy-start | bytes 100
  2.8 7.1 %collective-permute-start = (f32[2,16,3,256]{3,2,1,0:T(4,128)S(1)}, f32[2,16,3,256]{3,2,1,0:T(4,128)S(1)}, u32[]{:S(2)}, u32[]{:S(2)}) collective-permute-start(f32[2,16,3,256]{3,2,1,0:T(4,128)S(1)} %maximum_select_fusion), channel_id=1, source_target_pairs={{0,256},{256,0},{1,257},{257,1},{2,258},{258,2},{3,259},{259,3},{4... | collective-permute-start | bytes 294920 | tf_op jit(solution)/shard_map/ppermute | solution.py:41
  10.0 13.3 %collective-permute-start.1 = (f32[2,3,22,256]{3,2,1,0:T(8,128)S(1)}, f32[2,3,22,256]{3,2,1,0:T(8,128)S(1)}, u32[]{:S(2)}, u32[]{:S(2)}) collective-permute-start(f32[2,3,22,256]{3,2,1,0:T(8,128)S(1)} %pad_maximum_fusion.6), channel_id=1, source_target_pairs={{0,4},{4,8},{8,12},{12,16},{16,20},{20,24},{24,28},{28,32},{32,36}... | collective-permute-start | bytes 405512 | tf_op jit(solution)/shard_map/ppermute | solution.py:71
  13.4 9.9 %collective-permute-start.2 = (f32[2,3,22,256]{3,2,1,0:T(8,128)S(1)}, f32[2,3,22,256]{3,2,1,0:T(8,128)S(1)}, u32[]{:S(2)}, u32[]{:S(2)}) collective-permute-start(f32[2,3,22,256]{3,2,1,0:T(8,128)S(1)} %pad_maximum_fusion.7), channel_id=1, source_target_pairs={{4,0},{8,4},{12,8},{16,12},{20,16},{24,20},{28,24},{32,28},{36,32}... | collective-permute-start | bytes 405512 | tf_op jit(solution)/shard_map/ppermute | solution.py:72
  18.0 9.4 %collective-permute-start.3 = (bf16[192,512]{1,0:T(8,128)(2,1)S(1)}, bf16[192,512]{1,0:T(8,128)(2,1)S(1)}, u32[]{:S(2)}, u32[]{:S(2)}) collective-permute-start(bf16[192,512]{1,0:T(8,128)(2,1)S(1)} %bitcast.62), channel_id=1, source_target_pairs={{0,2},{2,0},{1,3},{3,1},{4,6},{6,4},{5,7},{7,5},{8,10},{10,8},{9,1... | collective-permute-start | bytes 589832 | tf_op jit(solution)/shard_map/ppermute | solution.py:41
  27.5 22.0 %collective-permute-start.4 = (bf16[2,192,512]{2,1,0:T(8,128)(2,1)S(1)}, bf16[2,192,512]{2,1,0:T(8,128)(2,1)S(1)}, u32[]{:S(2)}, u32[]{:S(2)}) collective-permute-start(bf16[2,192,512]{2,1,0:T(8,128)(2,1)S(1)} %pad_maximum_fusion.3), channel_id=1, source_target_pairs={{0,256},{256,0},{1,257},{257,1},{2,258},{258,2},{3,259},{259,3},{4... | collective-permute-start | bytes 1179656 | tf_op jit(solution)/shard_map/ppermute | solution.py:41
  31.4 18.2 %copy-start = (bf16[3,1536,128]{2,1,0:T(8,128)(2,1)S(1)}, bf16[3,1536,128]{2,1,0:T(8,128)(2,1)}, u32[]{:S(2)}) copy-start(bf16[3,1536,128]{2,1,0:T(8,128)(2,1)} %w_own_ref) | copy-start | bytes 3538948
  31.4 24.0 %copy-start.4 = (bf16[128,1536]{1,0:T(8,128)(2,1)S(1)}, bf16[128,1536]{1,0:T(8,128)(2,1)}, u32[]{:S(2)}) copy-start(bf16[128,1536]{1,0:T(8,128)(2,1)} %out_own_ref) | copy-start | bytes 1179652
  31.4 26.0 %copy-start.10 = (f32[1536]{0:T(1024)S(1)}, f32[1536]{0:T(1024)}, u32[]{:S(2)}) copy-start(f32[1536]{0:T(1024)} %param.16) | copy-start | bytes 18436
  31.4 40.2 %all-to-all-start = ((bf16[64,4,640]{2,1,0:T(4,128)(2,1)}), bf16[64,4,640]{2,1,0:T(4,128)(2,1)}, u32[]{:S(2)}, u32[]{:S(2)}) async-start(bf16[64,4,640]{2,1,0:T(4,128)(2,1)} %reshape.102), calls=%async_computation | async-start | bytes 655360 | tf_op jit(solution)/shard_map/all_to_all | solution.py:32
  49.6 9.4 %collective-permute-start.6 = (bf16[3,1536,128]{2,1,0:T(8,128)(2,1)S(1)}, bf16[3,1536,128]{2,1,0:T(8,128)(2,1)S(1)}, u32[]{:S(2)}, u32[]{:S(2)}) collective-permute-start(bf16[3,1536,128]{2,1,0:T(8,128)(2,1)S(1)} %copy-done), channel_id=1, source_target_pairs={{0,1},{1,0},{2,3},{3,2},{4,5},{5,4},{6,7},{7,6},{8,9},{9,8},{10,11... | collective-permute-start | bytes 3538952 | tf_op jit(solution)/shard_map/ppermute | solution.py:41
  51.6 6.6 %collective-permute-start.5 = (bf16[2,2,192,512]{3,2,1,0:T(8,128)(2,1)S(1)}, bf16[2,2,192,512]{3,2,1,0:T(8,128)(2,1)S(1)}, u32[]{:S(2)}, u32[]{:S(2)}) collective-permute-start(bf16[2,2,192,512]{3,2,1,0:T(8,128)(2,1)S(1)} %pad_maximum_fusion.2), channel_id=1, source_target_pairs={{0,1},{1,0},{2,3},{3,2},{4,5},{5,4},{6,7},{7,6},{8,9},{9,8},{10,11... | collective-permute-start | bytes 2359304 | tf_op jit(solution)/shard_map/ppermute | solution.py:41
  55.4 3.6 %collective-permute-start.7 = (bf16[128,1536]{1,0:T(8,128)(2,1)S(1)}, bf16[128,1536]{1,0:T(8,128)(2,1)S(1)}, u32[]{:S(2)}, u32[]{:S(2)}) collective-permute-start(bf16[128,1536]{1,0:T(8,128)(2,1)S(1)} %copy-done.4), channel_id=1, source_target_pairs={{0,1},{1,0},{2,3},{3,2},{4,5},{5,4},{6,7},{7,6},{8,9},{9,8},{10,11... | collective-permute-start | bytes 1179656 | tf_op jit(solution)/shard_map/ppermute | solution.py:41
  58.1 1.0 copy-start.5
  59.1 13.5 %copy-start.7 = (bf16[128,256]{1,0:T(8,128)(2,1)S(1)}, bf16[128,256]{1,0:T(8,128)(2,1)}, u32[]{:S(2)}) copy-start(bf16[128,256]{1,0:T(8,128)(2,1)} %fusion.2) | copy-start | bytes 196612
  60.9 2.0 copy-start.1
  106.4 4.7 %collective-permute-start.8 = (bf16[3,1536,128]{2,1,0:T(8,128)(2,1)S(1)}, bf16[3,1536,128]{2,1,0:T(8,128)(2,1)S(1)}, u32[]{:S(2)}, u32[]{:S(2)}) collective-permute-start(bf16[3,1536,128]{2,1,0:T(8,128)(2,1)S(1)} %backward_other.1), channel_id=1, source_target_pairs={{0,1},{1,0},{2,3},{3,2},{4,5},{5,4},{6,7},{7,6},{8,9},{9,8},{10,11... | collective-permute-start | bytes 3538952 | tf_op jit(solution)/shard_map/ppermute | solution.py:41
  160.5 24.4 %all-to-all-start.5 = ((bf16[16,72,128]{2,1,0:T(8,128)(2,1)}), bf16[16,72,128]{2,1,0:T(8,128)(2,1)S(1)}, u32[]{:S(2)}, u32[]{:S(2)}) async-start(bf16[16,72,128]{2,1,0:T(8,128)(2,1)} %broadcast_in_dim.74), calls=%async_computation.5 | async-start | bytes 589824 | tf_op jit(solution)/shard_map/all_to_all | solution.py:32
  166.8 3.0 %collective-permute-start.9 = (f32[3,128]{1,0:T(4,128)S(1)}, f32[3,128]{1,0:T(4,128)S(1)}, u32[]{:S(2)}, u32[]{:S(2)}) collective-permute-start(f32[3,128]{1,0:T(4,128)S(1)} %convert_reduce_fusion.1), channel_id=1, source_target_pairs={{0,1},{1,0},{2,3},{3,2},{4,5},{5,4},{6,7},{7,6},{8,9},{9,8},{10,11... | collective-permute-start | bytes 4616 | tf_op jit(solution)/shard_map/ppermute | solution.py:41
  169.8 5.5 %collective-permute-start.10 = (f32[3,128]{1,0:T(4,128)S(1)}, f32[3,128]{1,0:T(4,128)S(1)}, u32[]{:S(2)}, u32[]{:S(2)}) collective-permute-start(f32[3,128]{1,0:T(4,128)S(1)} %add.74), channel_id=1, source_target_pairs={{0,256},{256,0},{1,257},{257,1},{2,258},{258,2},{3,259},{259,3},{4... | collective-permute-start | bytes 4616 | tf_op jit(solution)/shard_map/ppermute | solution.py:41
  175.3 7.0 %collective-permute-start.11 = (f32[3,128]{1,0:T(4,128)S(1)}, f32[3,128]{1,0:T(4,128)S(1)}, u32[]{:S(2)}, u32[]{:S(2)}) collective-permute-start(f32[3,128]{1,0:T(4,128)S(1)} %add.75), channel_id=1, source_target_pairs={{0,2},{2,0},{1,3},{3,1},{4,6},{6,4},{5,7},{7,5},{8,10},{10,8},{9,1... | collective-permute-start | bytes 4616 | tf_op jit(solution)/shard_map/ppermute | solution.py:41
